TPU v7x, 128 devices: a whole 4x4x4 slice. The times are simulated.
128 devices in a mesh: frame: 16 (over z, y_hi, core), res: 8 (over x, y_lo).
Axes of the slice: x: 4, y: 4 (y_hi: 2, y_lo: 2; y = y_hi * 2 + y_lo), z: 4, core: 2. Of those that a mesh axis runs over, the one named last changes fastest.
Arguments:
- tokens: bfloat16 [128, 128, 384], P('frame', 'res'), may hold values from -6 to 6
- rigid_frames: bfloat16 [12, 128, 128], P(None, 'frame', 'res'), may hold values from -4 to 4, as said below
- neighbors: int32 [128, 32], P('res'), may hold values from 0 to 127, as said below
- w_time_qkv: bfloat16 [384, 1152], replicated, may hold values from -3.6742346 to 3.6742346
- w_time_out: bfloat16 [384, 384], replicated, may hold values from -0.3125 to 0.3125
- w_ipa_qkv: bfloat16 [384, 1152], replicated, may hold values from -3.6742346 to 3.6742346
- w_ipa_points: bfloat16 [384, 288], replicated, may hold values from -0.3125 to 0.3125
- point_weight: float32 [12], replicated, may hold values from -2 to 1.5
- w_ipa_out: bfloat16 [384, 384], replicated, may hold values from -0.3125 to 0.3125
- w_up: bfloat16 [384, 1536], replicated, may hold values from -0.3125 to 0.3125
- w_down: bfloat16 [1536, 384], replicated, may hold values from -0.15625 to 0.15625
- cotangent: bfloat16 [128, 128, 384], P('frame', 'res'), may hold values from -6 to 6
Outputs:
- updated: bfloat16 [128, 128, 384], P('frame', 'res')
- grad_tokens: bfloat16 [128, 128, 384], P('frame', 'res')
- grad_time_qkv: float32 [384, 1152], replicated
- grad_time_out: float32 [384, 384], replicated
- grad_ipa_qkv: float32 [384, 1152], replicated
- grad_ipa_points: float32 [384, 288], replicated
- grad_point_weight: float32 [12], replicated
- grad_ipa_out: float32 [384, 384], replicated
- grad_up: float32 [384, 1536], replicated
- grad_down: float32 [1536, 384], replicated
Inputs may be any that keep to these rules, and one draw needn't show every extreme that they name: `rigid_frames`: the first nine rows of each column form a rotation matrix row by row, the last three a translation. `neighbors`: each residue's list contains the residue itself.
All inputs are finite; a program needn't handle non-finite values.
Results may differ from a plain program's by a relative error of at most 0.025.
Values may be sent and summed in bfloat16 or wider, within the bound.
No kernel may reach another device: no remote copies, remote signals or barrier semaphores. Data moves between devices by JAX's collectives and lax.ppermute only.
A program may use at most 192 MiB of HBM per device.

v0:
```python
import math

import jax
import jax.numpy as jnp
from jax import lax
from jax.sharding import PartitionSpec as P

H = 12
P_SIZE = 4
NB = 32


EPSILON = 1e-05
PRECISE = lax.Precision.HIGHEST


def stored(values):
    return lax.optimization_barrier(values.astype(jnp.bfloat16))


def normalize(values):
    widened = values.astype(jnp.float32)
    centered = widened - jnp.mean(widened, axis=-1, keepdims=True)
    variance = jnp.mean(centered * centered, axis=-1, keepdims=True)
    return stored(centered * lax.rsqrt(variance + EPSILON))


def project(activations, weight):
    return jnp.dot(activations, weight, preferred_element_type=jnp.float32)


def split_three(activations, weight):
    product = project(activations, weight)
    portion = weight.shape[1] // 3
    return (
        stored(product[..., :portion]),
        stored(product[..., portion : 2 * portion]),
        stored(product[..., 2 * portion :]),
    )


def softmax_rounded(logits):
    highest = jnp.max(logits, axis=-1, keepdims=True)
    raised = jnp.exp(logits - highest)
    shares = raised / jnp.sum(raised, axis=-1, keepdims=True)
    return stored(shares).astype(jnp.float32)


def time_mix(query_rows, key_rows, value_rows):
    frames, residues, channels = query_rows.shape

    def shaped(tensor):
        return tensor.astype(jnp.float32).reshape(frames, residues, H, channels // H)

    scores = jnp.einsum(
        "fshd,gshd->shfg", shaped(query_rows), shaped(key_rows), precision=PRECISE
    ) * (1.0 / math.sqrt(channels // H))
    shares = softmax_rounded(scores)
    mixture = jnp.einsum("shfg,gshd->fshd", shares, shaped(value_rows), precision=PRECISE)
    return stored(mixture.reshape(frames, residues, channels))


def ipa_inputs(hidden, rigid_frames, weight_qkv, weight_points):
    normed = normalize(hidden)
    query_rows, key_rows, value_rows = split_three(normed, weight_qkv)
    frames, residues = (hidden.shape[0], hidden.shape[1])
    points = project(normed, weight_points).reshape(frames, residues, 2, 3, H * P_SIZE)
    frame_data = rigid_frames.astype(jnp.float32)
    rotation = frame_data[:9].reshape(3, 3, frames, residues)
    offset = jnp.transpose(frame_data[9:], (1, 2, 0))
    placed = (
        jnp.einsum("abfr,frcbp->frcap", rotation, points, precision=PRECISE)
        + offset[:, :, None, :, None]
    )
    query_points = placed[:, :, 0].reshape(frames, residues, 3 * H * P_SIZE)
    key_points = stored(placed[:, :, 1].reshape(frames, residues, 3 * H * P_SIZE))
    return (query_rows, key_rows, value_rows, query_points, key_points)


def ipa_mix(
    query_rows, query_points, key_table, value_table, point_table, neighbor_rows, point_weight
):
    frames, members, channels = query_rows.shape
    near_keys = key_table[:, neighbor_rows].reshape(frames, members, NB, H, channels // H)
    near_values = value_table[:, neighbor_rows].reshape(frames, members, NB, H, channels // H)
    near_points = point_table[:, neighbor_rows].reshape(frames, members, NB, 3, H, P_SIZE)
    queries = query_rows.astype(jnp.float32).reshape(frames, members, H, channels // H)
    direct = jnp.einsum("frhd,frnhd->frhn", queries, near_keys, precision=PRECISE) * (
        1.0 / math.sqrt(channels // H)
    )
    spread = query_points.reshape(frames, members, 1, 3, H, P_SIZE) - near_points
    distance = jnp.transpose(jnp.sum(spread * spread, axis=(3, 5)), (0, 1, 3, 2))
    strength = jax.nn.softplus(point_weight) * math.sqrt(2.0 / (9.0 * P_SIZE))
    logits = math.sqrt(0.5) * (direct - 0.5 * strength[:, None] * distance)
    shares = softmax_rounded(logits)
    mixture = jnp.einsum("frhn,frnhd->frhd", shares, near_values, precision=PRECISE)
    return stored(mixture.reshape(frames, members, channels))


def frame_mix(
    query_rows, query_points, key_table, value_table, point_table, neighbor_rows, point_weight
):

    def per_frame(tensors):
        return ipa_mix(
            tensors[0][None],
            tensors[1][None],
            tensors[2][None],
            tensors[3][None],
            tensors[4][None],
            neighbor_rows,
            point_weight,
        )[0]

    return lax.map(
        jax.checkpoint(per_frame), (query_rows, query_points, key_table, value_table, point_table)
    )


def closing(hidden, mixture, weight_out, weight_up, weight_down):
    second = stored(hidden.astype(jnp.float32) + project(mixture, weight_out))
    hidden_units = stored(jax.nn.gelu(project(normalize(second), weight_up), approximate=True))
    return stored(second.astype(jnp.float32) + project(hidden_units, weight_down))


def residual_add(source, mixture, weight):
    return stored(source.astype(jnp.float32) + project(mixture, weight))


def body(
    tokens,
    rigid_frames,
    neighbors,
    w_time_qkv,
    w_time_out,
    w_ipa_qkv,
    w_ipa_points,
    point_weight,
    w_ipa_out,
    w_up,
    w_down,
    cotangent,
):
    time_qkv = w_time_qkv.astype(jnp.float32)
    time_out = w_time_out.astype(jnp.float32)
    ipa_qkv = w_ipa_qkv.astype(jnp.float32)
    ipa_points = w_ipa_points.astype(jnp.float32)
    ipa_out = w_ipa_out.astype(jnp.float32)
    up_weight = w_up.astype(jnp.float32)
    down_weight = w_down.astype(jnp.float32)

    def lift_inputs(source, weight):
        return split_three(normalize(source), weight)

    time_rows, lift_rows = jax.vjp(lift_inputs, tokens, time_qkv)
    moved_rows = (
        lax.all_to_all(time_rows[0], "frame", split_axis=1, concat_axis=0, tiled=True),
        lax.all_to_all(time_rows[1], "frame", split_axis=1, concat_axis=0, tiled=True),
        lax.all_to_all(time_rows[2], "frame", split_axis=1, concat_axis=0, tiled=True),
    )
    mixture_there, pull_mixture = jax.vjp(time_mix, moved_rows[0], moved_rows[1], moved_rows[2])
    mixture_here = lax.all_to_all(mixture_there, "frame", split_axis=0, concat_axis=1, tiled=True)
    after_time, pull_residual = jax.vjp(residual_add, tokens, mixture_here, time_out)

    def lift_ipa(source, weight_qkv, weight_points):
        return ipa_inputs(source, rigid_frames, weight_qkv, weight_points)

    ipa_parts, pull_inputs = jax.vjp(lift_ipa, after_time, ipa_qkv, ipa_points)
    key_all, value_all, point_all = (
        lax.all_gather(ipa_parts[1], "res", axis=1, tiled=True),
        lax.all_gather(ipa_parts[2], "res", axis=1, tiled=True),
        lax.all_gather(ipa_parts[4], "res", axis=1, tiled=True),
    )

    def tail_part(
        source,
        query_rows,
        query_points,
        key_table,
        value_table,
        point_table,
        weight_point,
        weight_out,
        weight_up,
        weight_down,
    ):
        attended = frame_mix(
            query_rows, query_points, key_table, value_table, point_table, neighbors, weight_point
        )
        return closing(source, attended, weight_out, weight_up, weight_down)

    output, pull_tail = jax.vjp(
        tail_part,
        after_time,
        ipa_parts[0],
        ipa_parts[3],
        key_all.astype(jnp.float32),
        value_all.astype(jnp.float32),
        point_all.astype(jnp.float32),
        point_weight,
        ipa_out,
        up_weight,
        down_weight,
    )
    tail_grads = pull_tail(cotangent)
    table_grads = (
        lax.psum_scatter(
            tail_grads[3].astype(jnp.bfloat16), "res", scatter_dimension=1, tiled=True
        ).astype(jnp.float32),
        lax.psum_scatter(
            tail_grads[4].astype(jnp.bfloat16), "res", scatter_dimension=1, tiled=True
        ).astype(jnp.float32),
        lax.psum_scatter(
            tail_grads[5].astype(jnp.bfloat16), "res", scatter_dimension=1, tiled=True
        ).astype(jnp.float32),
    )
    input_grads = pull_inputs(
        (
            tail_grads[1],
            table_grads[0].astype(jnp.bfloat16),
            table_grads[1].astype(jnp.bfloat16),
            tail_grads[2],
            table_grads[2].astype(jnp.bfloat16),
        )
    )
    after_grad = tail_grads[0] + input_grads[0]
    ipa_grads = (
        input_grads[1],
        input_grads[2],
        tail_grads[6],
        tail_grads[7],
        tail_grads[8],
        tail_grads[9],
    )
    token_grad_res, mixture_grad, time_out_grad = pull_residual(after_grad)
    mixture_grad_there = lax.all_to_all(
        mixture_grad, "frame", split_axis=1, concat_axis=0, tiled=True
    )
    row_grads = pull_mixture(mixture_grad_there)
    row_back = (
        lax.all_to_all(row_grads[0], "frame", split_axis=0, concat_axis=1, tiled=True),
        lax.all_to_all(row_grads[1], "frame", split_axis=0, concat_axis=1, tiled=True),
        lax.all_to_all(row_grads[2], "frame", split_axis=0, concat_axis=1, tiled=True),
    )
    token_grad_norm, time_qkv_grad = lift_rows((row_back[0], row_back[1], row_back[2]))
    token_grad = token_grad_res + token_grad_norm
    summed = lax.psum(
        (
            time_qkv_grad,
            time_out_grad,
            ipa_grads[0],
            ipa_grads[1],
            ipa_grads[2],
            ipa_grads[3],
            ipa_grads[4],
            ipa_grads[5],
        ),
        ("frame", "res"),
    )
    return (
        output,
        token_grad,
        summed[0],
        summed[1],
        summed[2],
        summed[3],
        summed[4],
        summed[5],
        summed[6],
        summed[7],
    )


def solution(mesh):
    placed = (
        P("frame", "res", None),
        P(None, "frame", "res"),
        P("res", None),
        P(),
        P(),
        P(),
        P(),
        P(),
        P(),
        P(),
        P(),
        P("frame", "res", None),
    )
    return jax.shard_map(
        body,
        mesh=mesh,
        in_specs=placed,
        out_specs=(
            P("frame", "res", None),
            P("frame", "res", None),
            P(),
            P(),
            P(),
            P(),
            P(),
            P(),
            P(),
            P(),
        ),
        check_vma=False,
    )
```

profile of v0, /device:TPU:1, one launch (start us, length us, event | category | flops | bytes accessed | tf_op | source)
XLA Modules:
  0.0 1230.5 jit_solution(6576271929330338306)
XLA Ops:
  13.9 9.5 all-to-all-start
  25.3 5.4 all-to-all-done
  30.7 3.9 all-to-all-start.1
  35.3 6.7 all-to-all-done.1
  42.0 3.9 all-to-all-start.2
  48.0 5.3 all-to-all-done.2
  59.9 3.9 all-to-all-start.3
  64.3 6.9 all-to-all-done.3
  76.9 24.6 %all_gather.9 = bf16[8,128,384]{2,1,0:T(8,128)(2,1)S(1)} all-gather(bf16[8,16,384]{2,1,0:T(8,128)(2,1)S(1)} %get-tuple-element.672), channel_id=1, replica_groups=mesh['frame'=16,'res'=8] {'res'}, dimensions={1}, use_global_device_ids=true | all-gather | bytes 884736 | tf_op jit(solution)/shard_map/all_gather | solution.py:170
  103.1 22.9 %all_gather.10 = bf16[8,128,144]{2,1,0:T(8,128)(2,1)S(1)} all-gather(bf16[8,16,144]{2,1,0:T(8,128)(2,1)S(1)} %convert_element_type.337), channel_id=1, replica_groups=mesh['frame'=16,'res'=8] {'res'}, dimensions={1}, use_global_device_ids=true | all-gather | bytes 331776 | tf_op jit(solution)/shard_map/all_gather | solution.py:172
  127.1 23.2 %all_gather.11 = bf16[8,128,384]{2,1,0:T(8,128)(2,1)S(1)} all-gather(bf16[8,16,384]{2,1,0:T(8,128)(2,1)S(1)} %get-tuple-element.671), channel_id=1, replica_groups=mesh['frame'=16,'res'=8] {'res'}, dimensions={1}, use_global_device_ids=true | all-gather | bytes 884736 | tf_op jit(solution)/shard_map/all_gather | solution.py:171
  152.2 211.3 %while.37 = (s32[]{:T(128)}, bf16[8,16,384]{2,1,0:T(8,128)(2,1)}, bf16[8,16,384]{2,1,0:T(8,128)(2,1)}, f32[8,128,384]{2,1,0:T(8,128)}, s32[16,32,1]{1,2,0:T(1,12...) while((s32[]{:T(128)}, bf16[8,16,384]{2,1,0:T(8,128)(2,1)}, ...), condition=%wide.region_10.11_spmd, body=%wide.region_6.10_spmd.sunk | while | flops 4995714 | bytes 11267049 | solution.py:115
  167.8 5.4 fusion.216
  173.7 4.5 fusion.219
  194.2 5.4 fusion.216
  200.1 4.5 fusion.219
  220.5 5.4 fusion.216
  226.4 4.5 fusion.219
  246.9 5.4 fusion.216
  252.8 4.5 fusion.219
  273.3 5.4 fusion.216
  279.2 4.5 fusion.219
  299.6 5.4 fusion.216
  305.5 4.5 fusion.219
  326.0 5.4 fusion.216
  331.9 4.5 fusion.219
  352.4 5.4 fusion.216
  358.3 4.5 fusion.219
  372.5 486.1 %while.38 = (s32[]{:T(128)}, f32[12]{0:T(128)S(1)}, bf16[8,16,384]{2,1,0:T(8,128)(2,1)}, f32[8,16,144]{1,2,0:T(8,128)}, bf16[8,128,384]{2,1,0:T(8,128)(2,1)}, /*...) while((s32[]{:T(128)}, f32[12]{0:T(128)S(1)}, ...), condition=%wide.region_27.28_spmd.clone, body=%wide.region_15.27_spmd.clone.sunk | while | flops 8940032 | bytes 29410036 | solution.py:115
  402.7 5.4 fusion.229
  412.9 5.5 fusion.232
  460.0 5.4 fusion.229
  470.3 5.5 fusion.232
  488.5 3.6 scatter_custom_fusion.18
  497.4 3.6 scatter_custom_fusion.19
  517.4 5.4 fusion.229
  527.6 5.5 fusion.232
  574.7 5.4 fusion.229
  584.9 5.5 fusion.232
  603.1 3.6 scatter_custom_fusion.18
  612.1 3.6 scatter_custom_fusion.19
  632.1 5.4 fusion.229
  642.3 5.5 fusion.232
  689.4 5.4 fusion.229
  699.6 5.5 fusion.232
  717.8 3.6 scatter_custom_fusion.18
  726.8 3.6 scatter_custom_fusion.19
  746.7 5.4 fusion.229
  756.9 5.5 fusion.232
  804.0 5.4 fusion.229
  814.3 5.5 fusion.232
  865.9 40.2 %reduce-scatter.4.cloned.1.call-done = bf16[8,16,144]{2,1,0:T(8,128)(2,1)} async-done(((bf16[8,128,144]{2,1,0:T(8,128)(2,1)}), bf16[8,16,144]{2,1,0:T(8,128)(2,1)}) %reduce-scatter.4.cloned.1.call-update) | async-done | bytes 36880 | tf_op jit(solution)/shard_map/reduce_scatter | solution.py:213
  909.2 36.6 %reduce-scatter.8.cloned.1.call-done = bf16[8,16,384]{2,1,0:T(8,128)(2,1)} async-done(((bf16[8,128,384]{2,1,0:T(8,128)(2,1)}), bf16[8,16,384]{2,1,0:T(8,128)(2,1)}) %reduce-scatter.8.cloned.1.call-update) | async-done | bytes 98320 | tf_op jit(solution)/shard_map/reduce_scatter | solution.py:207
  945.9 39.5 %reduce-scatter.6.cloned.1.call-done = bf16[8,16,384]{2,1,0:T(8,128)(2,1)} async-done(((bf16[8,128,384]{2,1,0:T(8,128)(2,1)}), bf16[8,16,384]{2,1,0:T(8,128)(2,1)}) %reduce-scatter.6.cloned.1.call-update) | async-done | bytes 98320 | tf_op jit(solution)/shard_map/reduce_scatter | solution.py:210
  988.3 12.2 all-to-all-start.4
  1003.1 4.7 all-to-all-done.4
  1011.4 4.0 all-to-all-start.7
  1017.7 5.1 all-to-all-done.7
  1022.8 3.9 all-to-all-start.6
  1028.5 5.6 all-to-all-done.6
  1034.1 3.9 all-to-all-start.5
  1039.3 6.0 all-to-all-done.5
  1047.8 63.0 %psum.60 = f32[12]{0:T(128)} all-reduce(f32[12]{0:T(128)S(1)} %copy-done.88), channel_id=1, replica_groups=mesh['frame'=16,'res'=8] {'frame','res'}, use_global_device_ids=true, to_apply=%region_42.43 | all-reduce | flops 12 | bytes 96 | tf_op jit(solution)/shard_map/psum | solution.py:247
  1113.5 99.7 %all-reduce.11.cloned.1.call-done = (f32[384,1152]{1,0:T(8,128)}, f32[384,384]{1,0:T(8,128)}, f32[384,1152]{1,0:T(8,128)}, f32[384,288]{0,1:T(8,128)}, f32[384,3...) async-done(((f32[384,1152]{1,0:T(8,128)}, f32[384,384]{1,0:T(8,128)}, f32[384,1152]{1,0:T(8,128)}, f32[384,288]{0,1:T(8,128)}, f32[384,384]{1,0:T(8,128)}, ...) | async-done | bytes 9879568 | tf_op jit(solution)/shard_map/psum | solution.py:247
  (1102 shorter events, 553.9 us)
Async XLA Ops:
  7.2 358.1 %copy-start = (bf16[384,1536]{1,0:T(8,128)(2,1)S(1)}, bf16[384,1536]{1,0:T(8,128)(2,1)}, u32[]{:S(2)}) copy-start(bf16[384,1536]{1,0:T(8,128)(2,1)} %param.25) | copy-start | bytes 3538948
  7.2 16.2 %copy-start.46 = (bf16[8,16,384]{2,1,0:T(8,128)(2,1)S(1)}, bf16[8,16,384]{2,1,0:T(8,128)(2,1)}, u32[]{:S(2)}) copy-start(bf16[8,16,384]{2,1,0:T(8,128)(2,1)} %param.27) | copy-start | bytes 294916
  7.2 16.2 %copy-start.12 = (bf16[1536,384]{1,0:T(8,128)(2,1)S(1)}, bf16[1536,384]{1,0:T(8,128)(2,1)}, u32[]{:S(2)}) copy-start(bf16[1536,384]{1,0:T(8,128)(2,1)} %param.26) | copy-start | bytes 3538948
  13.2 21.4 %copy-start.71 = (bf16[12,8,16]{2,1,0:T(8,128)(2,1)S(1)}, bf16[12,8,16]{2,1,0:T(8,128)(2,1)}, u32[]{:S(2)}) copy-start(bf16[12,8,16]{2,1,0:T(8,128)(2,1)} %param.17) | copy-start | bytes 9220
  13.2 32.7 %copy-start.56 = (s32[16,32]{1,0:T(8,128)S(1)}, s32[16,32]{1,0:T(8,128)}, u32[]{:S(2)}) copy-start(s32[16,32]{1,0:T(8,128)} %param.18) | copy-start | bytes 6148
  13.9 16.8 %all-to-all-start = ((bf16[8,16,384]{2,0,1:T(8,128)(2,1)}), bf16[8,16,384]{2,0,1:T(8,128)(2,1)S(1)}, u32[]{:S(2)}, u32[]{:S(2)}) async-start(bf16[8,16,384]{2,0,1:T(8,128)(2,1)} %copy.176), calls=%async_computation | async-start | bytes 196608 | tf_op jit(solution)/shard_map/all_to_all | solution.py:159
  30.7 11.3 all-to-all-start.1
  42.0 11.3 all-to-all-start.2
  47.2 9.7 copy-start.28
  47.9 6.6 copy-start.34
  54.4 9.4 copy-start.81
  54.4 9.5 slice-start
  55.3 16.0 %copy-start.10 = (bf16[8,16,384]{2,1,0:T(8,128)(2,1)S(1)}, bf16[8,16,384]{2,1,0:T(8,128)(2,1)}, u32[]{:S(2)}) copy-start(bf16[8,16,384]{2,1,0:T(8,128)(2,1)} %param.16) | copy-start | bytes 294916
  55.3 16.0 %copy-start.26 = (bf16[384,384]{1,0:T(8,128)(2,1)S(1)}, bf16[384,384]{1,0:T(8,128)(2,1)}, u32[]{:S(2)}) copy-start(bf16[384,384]{1,0:T(8,128)(2,1)} %param.20) | copy-start | bytes 884740
  56.9 16.2 %copy-start.32 = (bf16[384,288]{0,1:T(8,128)(2,1)S(1)}, bf16[384,288]{0,1:T(8,128)(2,1)}, u32[]{:S(2)}) copy-start(bf16[384,288]{0,1:T(8,128)(2,1)} %param.22) | copy-start | bytes 663556
  59.9 11.3 all-to-all-start.3
  63.8 842.3 %reduce-scatter.4.cloned.1.call-start = ((), (), s32[]{:S(2)}) async-start(), calls=%async_computation.11 | async-start | bytes 589824 | tf_op jit(solution)/shard_map/reduce_scatter | solution.py:213
  64.1 10.4 copy-start.42
  71.5 292.0 %copy-start.8 = (bf16[8,16,384]{2,1,0:T(8,128)(2,1)}, bf16[8,16,384]{2,1,0:T(8,128)(2,1)S(1)}, u32[]{:S(2)}) copy-start(bf16[8,16,384]{2,1,0:T(8,128)(2,1)S(1)} %fusion.43) | copy-start | bytes 294916
  127.1 25.1 %copy-start.57 = (s32[16,32]{1,0:T(8,128)S(1)}, s32[16,32]{1,0:T(8,128)}, u32[]{:S(2)}) copy-start(s32[16,32]{1,0:T(8,128)} %compare_select_fusion.4) | copy-start | bytes 6148
  412.9 6.9 copy-start.2
  449.4 5.3 copy-start.16
  470.3 6.9 copy-start.2
  506.8 5.3 copy-start.16
  527.6 6.9 copy-start.2
  564.1 5.3 copy-start.16
  584.9 6.9 copy-start.2
  621.4 5.3 copy-start.16
  642.3 6.9 copy-start.2
  678.8 5.3 copy-start.16
  699.6 6.9 copy-start.2
  736.1 5.3 copy-start.16
  756.9 6.9 copy-start.2
  814.3 6.9 copy-start.2
  858.8 87.1 %reduce-scatter.8.cloned.1.call-start = ((), (), s32[]{:S(2)}) async-start(), calls=%async_computation.13 | async-start | bytes 884736 | tf_op jit(solution)/shard_map/reduce_scatter | solution.py:207
  859.5 125.9 %reduce-scatter.6.cloned.1.call-start = ((), (), s32[]{:S(2)}) async-start(), calls=%async_computation.12 | async-start | bytes 884736 | tf_op jit(solution)/shard_map/reduce_scatter | solution.py:210
  863.6 43.5 %copy-start.43 = (bf16[3,3,8,16,1]{0,1,4,3,2:T(4,128)(2,1)S(1)}, bf16[3,3,8,16,1]{0,1,4,3,2:T(4,128)(2,1)}, u32[]{:S(2)}) copy-start(bf16[3,3,8,16,1]{0,1,4,3,2:T(4,128)(2,1)} %copy-done.42) | copy-start | bytes 6916
  865.8 42.1 %copy-start.24 = (bf16[8,16,384]{2,1,0:T(8,128)(2,1)S(1)}, bf16[8,16,384]{2,1,0:T(8,128)(2,1)}, u32[]{:S(2)}) copy-start(bf16[8,16,384]{2,1,0:T(8,128)(2,1)} %copy-done.23) | copy-start | bytes 294916
  865.9 43.2 %copy-start.33 = (bf16[384,288]{0,1:T(8,128)(2,1)S(1)}, bf16[384,288]{0,1:T(8,128)(2,1)}, u32[]{:S(2)}) copy-start(bf16[384,288]{0,1:T(8,128)(2,1)} %param.22) | copy-start | bytes 663556
  865.9 119.5 %copy-start.30 = (bf16[384,1152]{1,0:T(8,128)(2,1)S(1)}, bf16[384,1152]{1,0:T(8,128)(2,1)}, u32[]{:S(2)}) copy-start(bf16[384,1152]{1,0:T(8,128)(2,1)} %param.21) | copy-start | bytes 2654212
  907.7 79.1 %copy-start.9 = (bf16[8,16,384]{2,1,0:T(8,128)(2,1)S(1)}, bf16[8,16,384]{2,1,0:T(8,128)(2,1)}, u32[]{:S(2)}) copy-start(bf16[8,16,384]{2,1,0:T(8,128)(2,1)} %copy-done.8) | copy-start | bytes 294916
  907.8 79.1 %copy-start.66 = (f32[8,16]{1,0:T(8,128)S(1)}, f32[8,16]{1,0:T(8,128)}, u32[]{:S(2)}) copy-start(f32[8,16]{1,0:T(8,128)} %copy-done.65) | copy-start | bytes 1540
  907.8 79.2 %copy-start.79 = (f32[8,16]{1,0:T(8,128)S(1)}, f32[8,16]{1,0:T(8,128)}, u32[]{:S(2)}) copy-start(f32[8,16]{1,0:T(8,128)} %copy-done.78) | copy-start | bytes 1540
  907.8 79.3 %copy-start.75 = (f32[8,16]{1,0:T(8,128)S(1)}, f32[8,16]{1,0:T(8,128)}, u32[]{:S(2)}) copy-start(f32[8,16]{1,0:T(8,128)} %copy-done.74) | copy-start | bytes 1540
  908.0 79.4 %copy-start.27 = (bf16[384,384]{1,0:T(8,128)(2,1)S(1)}, bf16[384,384]{1,0:T(8,128)(2,1)}, u32[]{:S(2)}) copy-start(bf16[384,384]{1,0:T(8,128)(2,1)} %param.20) | copy-start | bytes 884740
  945.9 54.6 %copy-start.89 = (bf16[8,16,384]{2,1,0:T(8,128)(2,1)S(1)}, bf16[8,16,384]{2,1,0:T(8,128)(2,1)}, u32[]{:S(2)}) copy-start(bf16[8,16,384]{2,1,0:T(8,128)(2,1)} %reduce-scatter.8.cloned.1.call-done) | copy-start | bytes 294916
  985.4 15.1 %copy-start.90 = (bf16[8,16,384]{2,1,0:T(8,128)(2,1)S(1)}, bf16[8,16,384]{2,1,0:T(8,128)(2,1)}, u32[]{:S(2)}) copy-start(bf16[8,16,384]{2,1,0:T(8,128)(2,1)} %reduce-scatter.6.cloned.1.call-done) | copy-start | bytes 294916
  988.3 19.5 %all-to-all-start.4 = ((bf16[8,16,384]{2,0,1:T(8,128)(2,1)}), bf16[8,16,384]{2,0,1:T(8,128)(2,1)S(1)}, u32[]{:S(2)}, u32[]{:S(2)}) async-start(bf16[8,16,384]{2,0,1:T(8,128)(2,1)} %copy.192), calls=%async_computation.7 | async-start | bytes 196608 | tf_op jit(solution)/shard_map/all_to_all | solution.py:236
  1000.5 7.5 copy-start.29
  1000.5 7.8 copy-start.4
  1000.5 7.8 copy-start.62
  1008.6 6.8 copy-start.35
  1009.3 17.4 %copy-start.15 = (bf16[1,12,128,128]{2,3,1,0:T(8,128)(2,1)S(1)}, bf16[1,12,128,128]{2,3,1,0:T(8,128)(2,1)}, u32[]{:S(2)}) copy-start(bf16[1,12,128,128]{2,3,1,0:T(8,128)(2,1)} %copy-done.14) | copy-start | bytes 1179652
  1011.4 26.6 %copy-start.52 = (bf16[128,1,384]{2,0,1:T(8,128)(2,1)S(1)}, bf16[128,1,384]{2,0,1:T(8,128)(2,1)}, u32[]{:S(2)}) copy-start(bf16[128,1,384]{2,0,1:T(8,128)(2,1)} %copy-done.51) | copy-start | bytes 294916
  1011.4 11.4 all-to-all-start.7
  1022.8 11.3 all-to-all-start.6
  1034.1 11.3 all-to-all-start.5
  1038.0 175.2 %all-reduce.11.cloned.1.call-start = ((), (), s32[]{:S(2)}) async-start(), calls=%async_computation.14 | async-start | bytes 19759104 | tf_op jit(solution)/shard_map/psum | solution.py:247
  1038.0 7.5 copy-start.50
  1047.2 63.7 %copy-start.7 = (bf16[8,16,384]{2,1,0:T(8,128)(2,1)S(1)}, bf16[8,16,384]{2,1,0:T(8,128)(2,1)}, u32[]{:S(2)}) copy-start(bf16[8,16,384]{2,1,0:T(8,128)(2,1)} %copy-done.6) | copy-start | bytes 294916
  1047.2 63.7 %copy-start.13 = (bf16[1536,384]{1,0:T(8,128)(2,1)S(1)}, bf16[1536,384]{1,0:T(8,128)(2,1)}, u32[]{:S(2)}) copy-start(bf16[1536,384]{1,0:T(8,128)(2,1)} %param.26) | copy-start | bytes 3538948
  1047.2 64.7 %copy-start.31 = (bf16[384,1152]{1,0:T(8,128)(2,1)S(1)}, bf16[384,1152]{1,0:T(8,128)(2,1)}, u32[]{:S(2)}) copy-start(bf16[384,1152]{1,0:T(8,128)(2,1)} %param.19) | copy-start | bytes 2654212
  1047.2 65.1 %copy-start.11 = (bf16[8,16,384]{2,1,0:T(8,128)(2,1)S(1)}, bf16[8,16,384]{2,1,0:T(8,128)(2,1)}, u32[]{:S(2)}) copy-start(bf16[8,16,384]{2,1,0:T(8,128)(2,1)} %param.16) | copy-start | bytes 294916
  1047.2 65.1 %copy-start.64 = (f32[8,16]{1,0:T(8,128)S(1)}, f32[8,16]{1,0:T(8,128)}, u32[]{:S(2)}) copy-start(f32[8,16]{1,0:T(8,128)} %copy-done.63) | copy-start | bytes 1540
  (112 other events, 396.2 us)
Sparse Core Ops, SparseCore 0:
  858.9 47.1 reduce-scatter.3
  908.6 37.2 reduce-scatter.7
  948.3 37.0 reduce-scatter.5
  1047.3 165.8 all-reduce.10
where the time goes:
time: 1240 us; the launch traced here: 1230 us
  local copies, waits for them, and re-layouts  349 us (28%)
  waiting for transfers between devices  263 us (21%)
  matrix products  222 us (18%)
  other arithmetic  170 us (14%)
  blocking collectives  134 us (11%)
  starting transfers between devices  45.2 us (4%)
  loops' own time  31.8 us (3%)
  between operations  15.4 us (1%)
    dot_general x24, matrix products, ipa_mix(): jnp.einsum('frhd,frnhd->frhn', queries, near_keys, precision=PRECISE)  114 us
    another operation x114, local copies, waits for them, and re-layouts  103 us
    psum x1, waiting for transfers between devices, body(): lax.psum((time_qkv_grad, time_out_grad, ipa_grads[0], ipa_grads[1], ipa_g...  99.7 us
    dot_general x16, matrix products, ipa_mix(): jnp.einsum('frhn,frnhd->frhd', shares, near_values, precision=PRECISE)  80.7 us
    psum x1, blocking collectives, body(): lax.psum((time_qkv_grad, time_out_grad, ipa_grads[0], ipa_grads[1], ipa_g...  63 us
    reduce_scatter x1, waiting for transfers between devices, body(): lax.psum_scatter(tail_grads[5].astype(jnp.bfloat16), 'res', scatter_dimen...  40.2 us
    reduce_scatter x1, waiting for transfers between devices, body(): lax.psum_scatter(tail_grads[4].astype(jnp.bfloat16), 'res', scatter_dimen...  39.5 us
    reduce_scatter x1, waiting for transfers between devices, body(): lax.psum_scatter(tail_grads[3].astype(jnp.bfloat16), 'res', scatter_dimen...  36.6 us
  transfers between devices with their start and end apart: 12, of which 12 were waited for; matrix products, arithmetic and copies ran while one was open for 2% of the time, Pallas kernels for 0%

commit v1 on v0

v1 whole, which is shorter than its diff:
```python
import math

import jax
import jax.numpy as jnp
import numpy as np
from jax import lax
from jax.experimental import pallas as pl
from jax.experimental.pallas import tpu as pltpu
from jax.sharding import PartitionSpec as P

H = 12
P_SIZE = 4
NB = 32
C = 384
HID = 1536
N = 128
POINTS = H * P_SIZE
EPSILON = 1e-05
SCALE = 1.0 / math.sqrt(C // H)
STRENGTH = math.sqrt(2.0 / (9.0 * P_SIZE)) * math.sqrt(0.5)
F32 = jnp.float32
BF16 = jnp.bfloat16
PARAMS = pltpu.CompilerParams(vmem_limit_bytes=48 * 1024 * 1024)


def mm(left, right):
    return lax.dot_general(left, right, (((1,), (0,)), ((), ())), preferred_element_type=F32)


def mt(left, right):
    return lax.dot_general(left, right, (((1,), (1,)), ((), ())), preferred_element_type=F32)


def tm(left, right):
    return lax.dot_general(left, right, (((0,), (0,)), ((), ())), preferred_element_type=F32)


def norm(values):
    centered = values - jnp.mean(values, axis=-1, keepdims=True)
    inverse = lax.rsqrt(jnp.mean(centered * centered, axis=-1, keepdims=True) + EPSILON)
    return centered * inverse, inverse


def norm_pull(cotangent, normed, inverse):
    return inverse * (
        cotangent
        - jnp.mean(cotangent, axis=-1, keepdims=True)
        - normed * jnp.mean(cotangent * normed, axis=-1, keepdims=True)
    )


def split_two(values):
    high = values.astype(BF16)
    return high, (values - high.astype(F32)).astype(BF16)


def split_three(values):
    high, rest = values.astype(BF16), None
    rest = values - high.astype(F32)
    middle = rest.astype(BF16)
    return high, middle, (rest - middle.astype(F32)).astype(BF16)


def tile_masks():
    lane = lax.broadcasted_iota(jnp.int32, (1, 128), 1)
    return [jnp.where(lane // 32 == m, 1.0, 0.0).astype(BF16) for m in range(4)]


def masked_stack(tile, masks):
    return jnp.concatenate([tile * mask for mask in masks], axis=0)


def time_forward(x_ref, wqkv_ref, wout_ref, x1_ref, qkv_ref, shares_ref, mix_ref):
    x = x_ref[...].astype(F32)
    normed, _ = norm(x)
    qkv_ref[...] = mm(normed.astype(BF16), wqkv_ref[...]).astype(BF16)
    masks = tile_masks()
    for g in range(3):
        q = qkv_ref[:, g * 128 : (g + 1) * 128]
        k = qkv_ref[:, C + g * 128 : C + (g + 1) * 128]
        v = qkv_ref[:, 2 * C + g * 128 : 2 * C + (g + 1) * 128]
        for m in range(4):
            h = 4 * g + m
            scores = mt(q * masks[m], k) * SCALE
            raised = jnp.exp(scores - jnp.max(scores, axis=-1, keepdims=True))
            shares = raised / jnp.sum(raised, axis=-1, keepdims=True)
            shares_ref[:, h * 128 : (h + 1) * 128] = shares.astype(BF16)
        mixed = mm(shares_ref[:, g * 512 : (g + 1) * 512], masked_stack(v, masks))
        mix_ref[:, g * 128 : (g + 1) * 128] = mixed.astype(BF16)
    x1_ref[...] = (x + mm(mix_ref[...], wout_ref[...])).astype(BF16)


def time_backward(
    dx1_ref, x_ref, qkv_ref, shares_ref, mix_ref, wqkv_ref, wout_ref,
    dx_ref, gqkv_ref, gout_ref, dqkv_ref, dcol_ref, pcol_ref,
):
    dx1 = dx1_ref[...]
    normed, inverse = norm(x_ref[...].astype(F32))
    dmix = mt(dx1, wout_ref[...]).astype(BF16)
    gout_ref[...] = tm(mix_ref[...], dx1).astype(gout_ref.dtype)
    masks = tile_masks()
    for g in range(3):
        q = qkv_ref[:, g * 128 : (g + 1) * 128]
        k = qkv_ref[:, C + g * 128 : C + (g + 1) * 128]
        v = qkv_ref[:, 2 * C + g * 128 : 2 * C + (g + 1) * 128]
        dm = dmix[:, g * 128 : (g + 1) * 128]
        rows = []
        for m in range(4):
            h = 4 * g + m
            kept = shares_ref[:, h * 128 : (h + 1) * 128]
            pcol_ref[m * 128 : (m + 1) * 128, :] = kept
            shares = kept.astype(F32)
            dshares = mt(dm * masks[m], v)
            inner = jnp.sum(shares * dshares, axis=-1, keepdims=True)
            dlogit = (shares * (dshares - inner) * SCALE).astype(BF16)
            dcol_ref[m * 128 : (m + 1) * 128, :] = dlogit
            rows.append(dlogit)
        dq = mm(jnp.concatenate(rows, axis=1), masked_stack(k, masks))
        dk = tm(dcol_ref[...], masked_stack(q, masks))
        dv = tm(pcol_ref[...], masked_stack(dm, masks))
        dqkv_ref[:, g * 128 : (g + 1) * 128] = dq.astype(BF16)
        dqkv_ref[:, C + g * 128 : C + (g + 1) * 128] = dk.astype(BF16)
        dqkv_ref[:, 2 * C + g * 128 : 2 * C + (g + 1) * 128] = dv.astype(BF16)
    gqkv_ref[...] = tm(normed.astype(BF16), dqkv_ref[...]).astype(gqkv_ref.dtype)
    dnormed = mt(dqkv_ref[...], wqkv_ref[...]).astype(BF16).astype(F32)
    pulled = norm_pull(dnormed, normed, inverse).astype(BF16).astype(F32)
    dx_ref[...] = (dx1.astype(F32) + pulled).astype(BF16)


def selectors():
    lane = np.arange(256)
    inside = lane < 3 * POINTS
    head = np.where(inside, (lane % POINTS) // P_SIZE, -1)
    heads = (head[None, :] == np.arange(16)[:, None]).astype(np.float32)
    turn = np.zeros((128, 4 * 256), np.float32)
    for a in range(3):
        at = a * POINTS + np.arange(POINTS)
        for b in range(3):
            turn[3 * a + b, b * 256 + at] = 1.0
        turn[9 + a, 3 * 256 + at] = 1.0
    spread = np.zeros((128, 256), np.float32)
    spread[16:32] = heads
    gather = np.zeros((6 * 256, 6 * POINTS), np.float32)
    for c in range(2):
        for b in range(3):
            for a in range(3):
                for p in range(POINTS):
                    gather[(3 * c + b) * 256 + a * POINTS + p, (3 * c + b) * POINTS + p] = 1.0
    return [jnp.asarray(item, BF16) for item in (heads, turn, spread, gather)]


def point_attention(
    weight_ref, x1_ref, side_ref, wqkv_ref, wpts_ref, wrep_ref, wout_ref, wup_ref, wdown_ref,
    heads_ref, turn_ref, spread_ref, gather_ref,
    updated_ref, dx1_ref, gqkv_ref, gpts_ref, gout_ref, gup_ref, gdown_ref, gweight_ref,
    qkv_ref, mix_ref, shares_ref, point_ref, prow_ref, pcol_ref, drow_ref, dcol_ref,
    dqkv_ref, dlocal_ref, keys_ref, queries_ref,
):
    masks = tile_masks()
    row = lax.broadcasted_iota(jnp.int32, (N, N), 0)
    col = lax.broadcasted_iota(jnp.int32, (N, N), 1)
    order = jnp.where((col // 8 == row % 16) & (col % 8 == row // 16), 1.0, 0.0).astype(BF16)
    x1 = mm(order, x1_ref[...])
    normed, inverse = norm(x1)
    n2 = normed.astype(BF16)
    qkv_ref[...] = mm(n2, wqkv_ref[...]).astype(BF16)

    lane = lax.broadcasted_iota(jnp.int32, (1, 256), 1)
    lane_head = jnp.where(lane < 3 * POINTS, (lane % POINTS) // P_SIZE, lane - 3 * POINTS)
    raw = jnp.zeros((1, 256), F32)
    for h in range(H):
        raw = jnp.where((lane < 3 * POINTS) & (lane_head == h), weight_ref[h], raw)
    soft = jnp.maximum(raw, 0.0) + jnp.log(1.0 + jnp.exp(-jnp.abs(raw)))
    strength = jnp.where(lane < 3 * POINTS, soft * STRENGTH, 0.0)
    head_masks = [jnp.where(lane_head == h, 1.0, 0.0).astype(BF16) for h in range(H)]

    turned = mm(side_ref[:, 512:640], turn_ref[...])
    turns = [turned[:, b * 256 : (b + 1) * 256] for b in range(3)]
    local = mm(n2, wrep_ref[...])
    placed = []
    for c in range(2):
        total = turned[:, 768:1024]
        for b in range(3):
            total = total + turns[b] * local[:, (3 * c + b) * 256 : (3 * c + b + 1) * 256]
        placed.append(total)
    gq = placed[0]
    gk_bf = placed[1].astype(BF16)
    gk = gk_bf.astype(F32)
    heads = heads_ref[...]
    own = sum(mt(part, heads) for part in split_three(gq * gq * (0.5 * strength)))
    other = sum(mt(heads, part) for part in split_three(gk * gk * (0.5 * strength)))
    q_high, q_low = split_two(gq * strength)
    ones = (lane >= 3 * POINTS) & (lane < 3 * POINTS + 16)
    keys_one = jnp.where(ones, 1.0, gk).astype(BF16)
    queries_one = jnp.where(ones, 1.0, gq).astype(BF16)
    two_keys = jnp.concatenate([gk_bf, gk_bf], axis=1)
    count = side_ref[:, 384:512].astype(F32)
    near = count > 0.0

    for g in range(3):
        q = qkv_ref[:, g * 128 : (g + 1) * 128]
        k = qkv_ref[:, C + g * 128 : C + (g + 1) * 128]
        v = qkv_ref[:, 2 * C + g * 128 : 2 * C + (g + 1) * 128]
        for m in range(4):
            h = 4 * g + m
            at = slice(h * 128, (h + 1) * 128)
            direct = mt(q * masks[m], k) * (SCALE * math.sqrt(0.5))
            cross = mt(
                jnp.concatenate([q_high * head_masks[h], q_low * head_masks[h]], axis=1), two_keys
            )
            spot = cross - own[:, h : h + 1] - other[h : h + 1, :]
            point_ref[:, at] = spot
            logits = jnp.where(near, direct + spot, -1e30)
            raised = jnp.exp(logits - jnp.max(logits, axis=-1, keepdims=True)) * count
            shares = raised / jnp.sum(raised, axis=-1, keepdims=True)
            shares_ref[:, at] = shares
            prow_ref[:, at] = shares.astype(BF16)
            pcol_ref[at, :] = shares.astype(BF16)
            keys_ref[at, :] = keys_one * head_masks[h]
            queries_ref[at, :] = queries_one * head_masks[h]
        mixed = mm(prow_ref[:, g * 512 : (g + 1) * 512], masked_stack(v, masks))
        mix_ref[:, g * 128 : (g + 1) * 128] = mixed.astype(BF16)

    cot = side_ref[:, 0:384]
    x2 = (x1 + mm(mix_ref[...], wout_ref[...])).astype(BF16).astype(F32)
    normed2, inverse2 = norm(x2)
    n3 = normed2.astype(BF16)
    u = mm(n3, wup_ref[...])
    root = math.sqrt(2.0 / math.pi)
    bent = jnp.tanh(root * (u + 0.044715 * u * u * u))
    hidden = (0.5 * u * (1.0 + bent)).astype(BF16)
    slope = 0.5 * (1.0 + bent) + 0.5 * u * (1.0 - bent * bent) * root * (
        1.0 + 3.0 * 0.044715 * u * u
    )
    updated_ref[...] = (x2 + mm(hidden, wdown_ref[...])).astype(BF16)
    gdown_ref[...] = tm(hidden, cot).astype(gdown_ref.dtype)
    dhidden = mt(cot, wdown_ref[...]).astype(BF16).astype(F32)
    du = (dhidden * slope).astype(BF16)
    gup_ref[...] = tm(n3, du).astype(gup_ref.dtype)
    dn3 = mt(du, wup_ref[...]).astype(BF16).astype(F32)
    dx2 = (cot.astype(F32) + norm_pull(dn3, normed2, inverse2).astype(BF16).astype(F32)).astype(
        BF16
    )
    dmix = mt(dx2, wout_ref[...]).astype(BF16)
    gout_ref[...] = tm(mix_ref[...], dx2).astype(gout_ref.dtype)

    gains = []
    for g in range(3):
        q = qkv_ref[:, g * 128 : (g + 1) * 128]
        k = qkv_ref[:, C + g * 128 : C + (g + 1) * 128]
        v = qkv_ref[:, 2 * C + g * 128 : 2 * C + (g + 1) * 128]
        dm = dmix[:, g * 128 : (g + 1) * 128]
        for m in range(4):
            h = 4 * g + m
            at = slice(h * 128, (h + 1) * 128)
            shares = shares_ref[:, at]
            dshares = mt(dm * masks[m], v)
            dlogit = shares * (dshares - jnp.sum(shares * dshares, axis=-1, keepdims=True))
            gains.append(jnp.sum(dlogit * point_ref[:, at], axis=0, keepdims=True))
            drow_ref[:, at] = dlogit.astype(BF16)
            dcol_ref[at, :] = dlogit.astype(BF16)
        group = slice(g * 512, (g + 1) * 512)
        dq = mm(drow_ref[:, group], masked_stack(k, masks)) * (SCALE * math.sqrt(0.5))
        dk = tm(dcol_ref[group, :], masked_stack(q, masks)) * (SCALE * math.sqrt(0.5))
        dv = tm(pcol_ref[group, :], masked_stack(dm, masks))
        dqkv_ref[:, g * 128 : (g + 1) * 128] = dq.astype(BF16)
        dqkv_ref[:, C + g * 128 : C + (g + 1) * 128] = dk.astype(BF16)
        dqkv_ref[:, 2 * C + g * 128 : 2 * C + (g + 1) * 128] = dv.astype(BF16)

    gain = jnp.sum(jnp.concatenate(gains + gains[:4], axis=0), axis=1, keepdims=True)
    row16 = lax.broadcasted_iota(jnp.int32, (16, 128), 0)
    raw16 = jnp.zeros((16, 128), F32)
    for h in range(H):
        raw16 = jnp.where(row16 == h, weight_ref[h], raw16)
    soft16 = jnp.maximum(raw16, 0.0) + jnp.log(1.0 + jnp.exp(-jnp.abs(raw16)))
    gweight_ref[...] = (gain / ((1.0 + jnp.exp(-raw16)) * soft16)).astype(gweight_ref.dtype)

    from_keys = mm(drow_ref[...], keys_ref[...])
    from_queries = tm(dcol_ref[...], queries_ref[...])
    spread = spread_ref[...]
    own_sum = sum(mm(part, spread) for part in split_two(from_keys[:, 128:256]))
    other_sum = sum(mm(part, spread) for part in split_two(from_queries[:, 128:256]))
    dgq = strength * (from_keys - gq * own_sum)
    dgk = (strength * (from_queries - gk * other_sum)).astype(BF16).astype(F32)
    for b in range(3):
        dlocal_ref[:, b * 256 : (b + 1) * 256] = (turns[b] * dgq).astype(BF16)
        dlocal_ref[:, (3 + b) * 256 : (4 + b) * 256] = (turns[b] * dgk).astype(BF16)
    dpoints = mm(dlocal_ref[...], gather_ref[...]).astype(BF16)
    dqkv = dqkv_ref[...]
    gqkv_ref[...] = tm(n2, dqkv).astype(gqkv_ref.dtype)
    gpts_ref[...] = tm(n2, dpoints).astype(gpts_ref.dtype)
    dn2 = (mt(dqkv, wqkv_ref[...]) + mt(dpoints, wpts_ref[...])).astype(BF16).astype(F32)
    dx1 = (dx2.astype(F32) + norm_pull(dn2, normed, inverse).astype(BF16).astype(F32)).astype(BF16)
    dx1_ref[...] = tm(order, dx1).astype(BF16)


def like(shape, dtype):
    return jax.ShapeDtypeStruct(shape, dtype)


GRAD = F32


def call_time_forward(x, w_qkv, w_out):
    return pl.pallas_call(
        time_forward,
        out_shape=(
            like((N, C), BF16), like((N, 3 * C), BF16), like((N, H * N), BF16), like((N, C), BF16),
        ),
        compiler_params=PARAMS,
        name="time_forward",
    )(x, w_qkv, w_out)


def call_time_backward(dx1, x, qkv, shares, mix, w_qkv, w_out):
    return pl.pallas_call(
        time_backward,
        out_shape=(like((N, C), BF16), like((C, 3 * C), GRAD), like((C, C), GRAD)),
        scratch_shapes=[
            pltpu.VMEM((N, 3 * C), BF16), pltpu.VMEM((4 * N, N), BF16), pltpu.VMEM((4 * N, N), BF16),
        ],
        compiler_params=PARAMS,
        name="time_backward",
    )(dx1, x, qkv, shares, mix, w_qkv, w_out)


def call_point_attention(weight, x1, side, w_qkv, w_pts, w_rep, w_out, w_up, w_down):
    whole = pl.BlockSpec(memory_space=pltpu.VMEM)
    return pl.pallas_call(
        point_attention,
        in_specs=[pl.BlockSpec(memory_space=pltpu.SMEM)] + [whole] * 12,
        out_shape=(
            like((N, C), BF16), like((N, C), BF16), like((C, 3 * C), GRAD),
            like((C, 6 * POINTS), GRAD), like((C, C), GRAD), like((C, HID), GRAD),
            like((HID, C), GRAD), like((16, 128), GRAD),
        ),
        scratch_shapes=[
            pltpu.VMEM((N, 3 * C), BF16), pltpu.VMEM((N, C), BF16),
            pltpu.VMEM((N, H * N), F32), pltpu.VMEM((N, H * N), F32),
            pltpu.VMEM((N, H * N), BF16), pltpu.VMEM((H * N, N), BF16),
            pltpu.VMEM((N, H * N), BF16), pltpu.VMEM((H * N, N), BF16),
            pltpu.VMEM((N, 3 * C), BF16), pltpu.VMEM((N, 6 * 256), BF16),
            pltpu.VMEM((H * N, 256), BF16), pltpu.VMEM((H * N, 256), BF16),
        ],
        compiler_params=PARAMS,
        name="point_attention",
    )(weight, x1, side, w_qkv, w_pts, w_rep, w_out, w_up, w_down, *selectors())


def repeat_points(weight):
    parts = weight.reshape(C, 6, POINTS)
    tripled = jnp.concatenate([parts, parts, parts], axis=2)
    return jnp.pad(tripled, ((0, 0), (0, 0), (0, 256 - 3 * POINTS))).reshape(C, 6 * 256)


def side_rows(cotangent, neighbors, rigid_frames):
    frames, residues, _ = cotangent.shape
    hits = neighbors[:, :, None] == lax.broadcasted_iota(jnp.int32, (1, 1, N), 2)
    count = jnp.sum(hits.astype(F32), axis=1).astype(BF16)
    return jnp.concatenate(
        [
            cotangent,
            jnp.broadcast_to(count[None], (frames, residues, N)),
            jnp.pad(jnp.transpose(rigid_frames, (1, 2, 0)), ((0, 0), (0, 0), (0, 116))),
        ],
        axis=2,
    )


def body(
    tokens, rigid_frames, neighbors, w_time_qkv, w_time_out, w_ipa_qkv, w_ipa_points,
    point_weight, w_ipa_out, w_up, w_down, cotangent,
):
    everyone = ("frame", "res")
    x = lax.all_to_all(tokens, "frame", split_axis=1, concat_axis=0, tiled=True).reshape(N, C)
    side = lax.all_to_all(
        side_rows(cotangent, neighbors, rigid_frames), "res", split_axis=0, concat_axis=0, tiled=True
    ).reshape(N, 640)
    x1, qkv, shares, mix = call_time_forward(x, w_time_qkv, w_time_out)
    x1 = lax.all_to_all(x1, everyone, split_axis=0, concat_axis=0, tiled=True)
    updated, dx1, g_ipa_qkv, g_pts, g_ipa_out, g_up, g_down, g_weight = call_point_attention(
        point_weight, x1, side, w_ipa_qkv, w_ipa_points, repeat_points(w_ipa_points), w_ipa_out,
        w_up, w_down,
    )
    dx1 = lax.all_to_all(dx1, everyone, split_axis=0, concat_axis=0, tiled=True)
    dx, g_time_qkv, g_time_out = call_time_backward(
        dx1, x, qkv, shares, mix, w_time_qkv, w_time_out
    )
    frames, residues = tokens.shape[:2]
    output = lax.all_to_all(
        updated.reshape(frames, residues, C), "res", split_axis=0, concat_axis=0, tiled=True
    )
    token_grad = lax.all_to_all(
        dx.reshape(N, 1, C), "frame", split_axis=0, concat_axis=1, tiled=True
    )
    early = lax.psum((g_ipa_qkv, g_pts, g_ipa_out, g_up, g_down, g_weight), everyone)
    late = lax.psum((g_time_qkv, g_time_out), everyone)
    return (
        output, token_grad, late[0], late[1], early[0], early[1], early[5][:H, 0], early[2],
        early[3], early[4],
    )


def solution(mesh):
    rows = P("frame", "res", None)
    placed = (rows, P(None, "frame", "res"), P("res", None)) + (P(),) * 8 + (rows,)
    return jax.shard_map(
        body,
        mesh=mesh,
        in_specs=placed,
        out_specs=(rows, rows) + (P(),) * 8,
        check_vma=False,
    )
```

time: 1240 us -> 280 us (0.23)
  local copies, waits for them, and re-layouts: 349 us -> 32.5 us
  matrix products: 222 us -> 0 us
  other arithmetic: 170 us -> 4.73 us
  waiting for transfers between devices: 263 us -> 102 us
  blocking collectives: 134 us -> 80.4 us
  loops' own time: 31.8 us -> 0 us
  starting transfers between devices: 45.2 us -> 27 us
  Pallas kernels: 0 us -> 17.7 us
    dot_general x69 -> x0, matrix products: 222 us -> none  [the longest x24 114 us: ipa_mix(): jnp.einsum('frhd,frnhd->frhn', queries, near_keys, precision=PRECISE)]
    reduce_scatter x3 -> x0, waiting for transfers between devices: 116 us -> none  [the longest x1 40.2 us: body(): lax.psum_scatter(tail_grads[5].astype(jnp.bfloat16), 'res', scatter_dimen...]
    another operation x122 -> x0, local copies, waits for them, and re-layouts: 104 us -> none
    scatter-add x24 -> x0, other arithmetic: 84.9 us -> none  [the longest x8 29.1 us: ipa_mix(): value_table[:, neighbor_rows].reshape(frames, members, NB, H, channels // H)]
    gather x72 -> x0, local copies, waits for them, and re-layouts: 81.2 us -> none  [the longest x40 30.2 us: ipa_mix(): point_table[:, neighbor_rows].reshape(frames, members, NB, 3, H, P_SIZE)]
    all_gather x3 -> x0, blocking collectives: 70.8 us -> none  [the longest x1 24.6 us: body(): lax.all_gather(ipa_parts[1], 'res', axis=1, tiled=True)]
    reshape x53 -> x1, local copies, waits for them, and re-layouts: 53.6 us -> 1.66 us  [repeat_points(): jnp.pad(tripled, ((0, 0), (0, 0), (0, 256 - 3 * POINTS)))]
    transpose x17 -> x0, other arithmetic: 34.4 us -> none  [the longest x8 17.2 us: ipa_mix(): jnp.einsum('frhn,frnhd->frhd', shares, near_values, precision=PRECISE)]
  transfers between devices with their start and end apart: 12 -> 6, of which waited for: 12 -> 5; matrix products, arithmetic and copies ran while one was open for 2% -> 4% of each run, Pallas kernels for 0% -> 0%
where the time goes in v1:
time: 280 us; the launch traced here: 279 us
  waiting for transfers between devices  102 us (36%)
  blocking collectives  80.4 us (29%)
  local copies, waits for them, and re-layouts  32.5 us (12%)
  starting transfers between devices  27 us (10%)
  Pallas kernels  17.7 us (6%)
  between operations  14.3 us (5%)
  other arithmetic  4.73 us (2%)
    psum x1, waiting for transfers between devices, body(): late = lax.psum((g_time_qkv, g_time_out), everyone)  80.1 us
    psum x1, blocking collectives, body(): lax.psum((g_ipa_qkv, g_pts, g_ipa_out, g_up, g_down, g_weight), everyone)  65 us
    unnamed x65, local copies, waits for them, and re-layouts  29.7 us
    all_to_all x1, blocking collectives, body(): dx1 = lax.all_to_all(dx1, everyone, split_axis=0, concat_axis=0, tiled=True)  15.4 us
    pallas_call x1, Pallas kernels, call_point_attention(): pl.pallas_call(point_attention, in_specs=[pl.BlockSpec(memory_space=pltpu...  12.7 us
    all_to_all x1, starting transfers between devices, body(): lax.all_to_all(tokens, 'frame', split_axis=1, concat_axis=0, tiled=True)  9.59 us
    all_to_all x1, waiting for transfers between devices, body(): x1 = lax.all_to_all(x1, everyone, split_axis=0, concat_axis=0, tiled=True)  9.01 us
    all_to_all x1, waiting for transfers between devices, body(): lax.all_to_all(dx.reshape(N, 1, C), 'frame', split_axis=0, concat_axis=1,...  6.72 us
  transfers between devices with their start and end apart: 6, of which 5 were waited for; matrix products, arithmetic and copies ran while one was open for 4% of the time, Pallas kernels for 0%

profile of v1, /device:TPU:1, one launch (start us, length us, event | category | flops | bytes accessed | tf_op | source)
XLA Modules:
  0.0 278.6 jit_solution(14421602348671383631)
XLA Ops:
  7.2 0.0 copy-start.21
  7.2 1.6 copy.58
  8.8 9.6 %all-to-all-start = ((bf16[8,16,384]{2,0,1:T(8,128)(2,1)}), bf16[8,16,384]{2,0,1:T(8,128)(2,1)S(1)}, u32[]{:S(2)}, u32[]{:S(2)}) async-start(bf16[8,16,384]{2,0,1:T(8,128)(2,1)} %copy.58), calls=%async_computation | async-start | bytes 196608 | tf_op jit(solution)/shard_map/all_to_all | solution.py:375
  18.4 0.9 copy.60
  19.2 1.1 copy.61.wpts_ref
  20.4 0.8 convert_reduce_fusion
  21.2 4.5 %all-to-all-done = bf16[8,16,384]{2,0,1:T(8,128)(2,1)S(1)} async-done(((bf16[8,16,384]{2,0,1:T(8,128)(2,1)}), bf16[8,16,384]{2,0,1:T(8,128)(2,1)S(1)}, u32[]{:S(2)}, u32[]{:S(2)}) %all-to-all-start) | async-done | bytes 98336 | tf_op jit(solution)/shard_map/all_to_all | solution.py:375
  25.7 1.2 copy-done
  26.9 1.0 copy-done.2
  27.8 1.9 time_forward.1
  29.7 0.0 copy-start.6
  29.7 0.7 copy-done.6
  30.5 0.7 copy-done.8
  31.2 0.5 broadcast.19
  31.7 0.7 reduce.2
  32.4 0.8 reshape.54
  33.1 5.5 %all-to-all-start.1 = ((bf16[128,2,192]{2,1,0:T(2,128)(2,1)}), bf16[128,2,192]{2,1,0:T(2,128)(2,1)}, u32[]{:S(2)}, u32[]{:S(2)}) async-start(bf16[128,2,192]{2,1,0:T(2,128)(2,1)} %reshape.54), calls=%async_computation.1 | async-start | bytes 262144 | tf_op jit(solution)/shard_map/all_to_all | solution.py:380
  38.7 0.0 copy-done.21
  38.7 0.7 fusion.6
  39.4 9.0 %all-to-all-done.1 = bf16[128,2,192]{2,1,0:T(2,128)(2,1)} async-done(((bf16[128,2,192]{2,1,0:T(2,128)(2,1)}), bf16[128,2,192]{2,1,0:T(2,128)(2,1)}, u32[]{:S(2)}, u32[]{:S(2)}) %all-to-all-start.1) | async-done | bytes 98336 | tf_op jit(solution)/shard_map/all_to_all | solution.py:380
  48.4 3.4 %all-to-all-start.2 = ((bf16[8,16,640]{2,1,0:T(8,128)(2,1)}), bf16[8,16,640]{2,1,0:T(8,128)(2,1)S(1)}, u32[]{:S(2)}, u32[]{:S(2)}) async-start(bf16[8,16,640]{2,1,0:T(8,128)(2,1)} %fusion.6), calls=%async_computation.2 | async-start | bytes 327680 | tf_op jit(solution)/shard_map/all_to_all | solution.py:376
  51.8 0.0 all-reduce.5.cloned.1.call-start
  51.9 1.1 fusion.4
  53.0 1.7 copy.62.wrep_ref
  54.6 1.1 reshape.55
  55.8 1.6 all-to-all-done.2
  57.3 0.0 copy-done.13
  57.4 0.0 copy-start.5
  57.4 1.2 copy-done.5
  58.5 1.0 copy-done.10
  59.5 0.9 copy-done.11
  60.4 0.8 copy-done.12
  61.3 12.7 %point_attention.1 = (bf16[128,384]{1,0:T(8,128)(2,1)}, bf16[128,384]{1,0:T(8,128)(2,1)S(1)}, f32[384,1152]{1,0:T(8,128)}, f32[384,288]{1,0:T(8,128)}, f32[384,3...) custom-call(f32[12]{0:T(128)S(1)} %copy-done.14, ...), custom_call_target="tpu_custom_call" | custom-call | tf_op jit(solution)/shard_map/point_attention/pallas_call | solution.py:329
  74.0 0.7 reduce.3
  74.8 0.1 reshape.56
  74.9 15.4 %all_to_all.65 = bf16[128,2,192]{2,1,0:T(2,128)(2,1)S(1)} all-to-all(bf16[128,2,192]{2,1,0:T(2,128)(2,1)S(1)} %reshape.56), channel_id=1, replica_groups=mesh['frame'=16,'res'=8] {'frame','res'}, dimensions={0} | all-to-all | bytes 196608 | tf_op jit(solution)/shard_map/all_to_all | solution.py:385
  90.3 0.2 reshape.57
  90.5 0.0 copy-start.7
  90.5 1.0 copy-done.7
  91.5 1.0 copy-done.9
  92.5 3.2 %time_backward.1 = (bf16[128,384]{1,0:T(8,128)(2,1)S(1)}, f32[384,1152]{1,0:T(8,128)}, f32[384,384]{1,0:T(8,128)}) custom-call(bf16[128,384]{1,0:T(8,128)(2,1)S(1)} %bitcast.29, bf16[128,384]{1,0:T(8,128)(2,1)S(1)} %bitcast.27, bf16[128,1152]{1,0:T(8,128)(2,1)S(1)} %copy-done.9, bf16[128,1536]{1,0:T(8,128)(2,1)S(1)} %copy-done.7, ...), custom_call_target="tpu_custom_call" | custom-call | tf_op jit(solution)/shard_map/time_backward/pallas_call | solution.py:316
  95.7 0.0 all-reduce.5.cloned.1.call-update
  95.7 3.4 %all-to-all-start.3 = ((bf16[8,16,384]{2,1,0:T(8,128)(2,1)}), bf16[8,16,384]{2,1,0:T(8,128)(2,1)S(1)}, u32[]{:S(2)}, u32[]{:S(2)}) async-start(bf16[8,16,384]{2,1,0:T(8,128)(2,1)} %bitcast.8), calls=%async_computation.3 | async-start | bytes 196608 | tf_op jit(solution)/shard_map/all_to_all | solution.py:390
  99.1 65.0 %psum.60 = f32[16,128]{1,0:T(8,128)S(1)} all-reduce(f32[16,128]{1,0:T(8,128)S(1)} %get-tuple-element.36), channel_id=1, replica_groups=mesh['frame'=16,'res'=8] {'frame','res'}, use_global_device_ids=true, to_apply=%region_5.6 | all-reduce | flops 2048 | bytes 16384 | tf_op jit(solution)/shard_map/psum | solution.py:396
  164.1 0.7 reduce.4
  164.8 0.7 reshape.58
  165.4 0.0 all-to-all-done.3
  165.5 5.0 %all-to-all-start.5 = ((bf16[16,2,1536]{2,1,0:T(2,128)(2,1)}), bf16[16,2,1536]{2,1,0:T(2,128)(2,1)S(1)}, u32[]{:S(2)}, u32[]{:S(2)}) async-start(bf16[16,2,1536]{2,1,0:T(2,128)(2,1)} %reshape.58), calls=%async_computation.5 | async-start | bytes 196608 | tf_op jit(solution)/shard_map/all_to_all | solution.py:393
  170.5 0.6 slice_reduce_fusion
  171.1 6.7 %all-to-all-done.5 = bf16[16,2,1536]{2,1,0:T(2,128)(2,1)S(1)} async-done(((bf16[16,2,1536]{2,1,0:T(2,128)(2,1)}), bf16[16,2,1536]{2,1,0:T(2,128)(2,1)S(1)}, u32[]{:S(2)}, u32[]{:S(2)}) %all-to-all-start.5) | async-done | bytes 98336 | tf_op jit(solution)/shard_map/all_to_all | solution.py:393
  177.8 0.1 reshape.59
  177.9 0.7 copy.65
  178.6 80.1 %all-reduce.5.cloned.1.call-done = (f32[384,1152]{1,0:T(8,128)}, f32[384,384]{1,0:T(8,128)}, f32[384,1152]{1,0:T(8,128)}, f32[384,288]{1,0:T(8,128)}, f32[384,38...) async-done(((f32[384,1152]{1,0:T(8,128)}, f32[384,384]{1,0:T(8,128)}, f32[384,1152]{1,0:T(8,128)}, f32[384,288]{1,0:T(8,128)}, f32[384,384]{1,0:T(8,128)}, ...) | async-done | bytes 9879568 | tf_op jit(solution)/shard_map/psum | solution.py:397
  258.7 2.0 copy.66
  260.8 0.6 copy.87
  261.4 2.9 %copy.88 = f32[384,1152]{1,0:T(8,128)} copy(f32[384,1152]{1,0:T(8,128)} %get-tuple-element.109) | data formatting | bytes 3538944
  264.4 0.8 copy.89
  265.2 1.2 copy.90
  266.4 0.2 copy-done.19
  266.6 0.8 copy.91
  267.4 0.4 copy-done.16
  267.9 1.4 copy.92
  269.3 1.1 copy-done.15
  270.4 1.4 copy.93
  (29 shorter events, 0.1 us)
Async XLA Ops:
  7.2 31.5 %copy-start.21 = (bf16[8,16,384]{2,1,0:T(8,128)(2,1)S(1)}, bf16[8,16,384]{2,1,0:T(8,128)(2,1)}, u32[]{:S(2)}) copy-start(bf16[8,16,384]{2,1,0:T(8,128)(2,1)} %param.27) | copy-start | bytes 294916
  8.8 43.1 %copy-start.18 = (bf16[384,288]{0,1:T(8,128)(2,1)S(1)}, bf16[384,288]{0,1:T(8,128)(2,1)}, u32[]{:S(2)}) copy-start(bf16[384,288]{0,1:T(8,128)(2,1)} %param.22) | copy-start | bytes 663556
  8.8 16.9 %all-to-all-start = ((bf16[8,16,384]{2,0,1:T(8,128)(2,1)}), bf16[8,16,384]{2,0,1:T(8,128)(2,1)S(1)}, u32[]{:S(2)}, u32[]{:S(2)}) async-start(bf16[8,16,384]{2,0,1:T(8,128)(2,1)} %copy.58), calls=%async_computation | async-start | bytes 196608 | tf_op jit(solution)/shard_map/all_to_all | solution.py:375
  25.7 1.2 copy-start
  26.9 1.0 copy-start.2
  29.7 0.7 copy-start.6
  30.5 0.7 copy-start.8
  33.1 15.3 %all-to-all-start.1 = ((bf16[128,2,192]{2,1,0:T(2,128)(2,1)}), bf16[128,2,192]{2,1,0:T(2,128)(2,1)}, u32[]{:S(2)}, u32[]{:S(2)}) async-start(bf16[128,2,192]{2,1,0:T(2,128)(2,1)} %reshape.54), calls=%async_computation.1 | async-start | bytes 262144 | tf_op jit(solution)/shard_map/all_to_all | solution.py:380
  48.4 8.9 %all-to-all-start.2 = ((bf16[8,16,640]{2,1,0:T(8,128)(2,1)}), bf16[8,16,640]{2,1,0:T(8,128)(2,1)S(1)}, u32[]{:S(2)}, u32[]{:S(2)}) async-start(bf16[8,16,640]{2,1,0:T(8,128)(2,1)} %fusion.6), calls=%async_computation.2 | async-start | bytes 327680 | tf_op jit(solution)/shard_map/all_to_all | solution.py:376
  51.8 206.9 %all-reduce.5.cloned.1.call-start = ((), (), s32[]{:S(2)}) async-start(), calls=%async_computation.6 | async-start | bytes 20054016 | tf_op jit(solution)/shard_map/psum | solution.py:397
  53.0 4.4 %copy-start.4 = (bf16[384,1536]{1,0:T(8,128)(2,1)S(1)}, bf16[384,1536]{1,0:T(8,128)(2,1)}, u32[]{:S(2)}) copy-start(bf16[384,1536]{1,0:T(8,128)(2,1)} %wup_ref.1) | copy-start | bytes 3538948
  53.0 4.4 %copy-start.13 = (bf16[16,256]{1,0:T(8,128)(2,1)S(1)}, bf16[16,256]{1,0:T(8,128)(2,1)}, u32[]{:S(2)}) copy-start(bf16[16,256]{1,0:T(8,128)(2,1)} %constant.13.clone.heads_ref) | copy-start | bytes 24580
  53.0 4.4 %copy-start.14 = (f32[12]{0:T(128)S(1)}, f32[12]{0:T(128)}, u32[]{:S(2)}) copy-start(f32[12]{0:T(128)} %weight_ref.1) | copy-start | bytes 148
  57.4 1.2 copy-start.5
  58.5 1.0 copy-start.10
  59.5 0.9 copy-start.11
  60.4 0.8 copy-start.12
  61.3 29.2 %copy-start.3 = (bf16[384,384]{1,0:T(8,128)(2,1)S(1)}, bf16[384,384]{1,0:T(8,128)(2,1)}, u32[]{:S(2)}) copy-start(bf16[384,384]{1,0:T(8,128)(2,1)} %wout_ref.5) | copy-start | bytes 884740
  74.0 16.5 %copy-start.1 = (bf16[384,1152]{1,0:T(8,128)(2,1)S(1)}, bf16[384,1152]{1,0:T(8,128)(2,1)}, u32[]{:S(2)}) copy-start(bf16[384,1152]{1,0:T(8,128)(2,1)} %wqkv_ref.5) | copy-start | bytes 2654212
  90.5 1.0 copy-start.7
  91.5 1.0 copy-start.9
  95.7 69.8 %all-to-all-start.3 = ((bf16[8,16,384]{2,1,0:T(8,128)(2,1)}), bf16[8,16,384]{2,1,0:T(8,128)(2,1)S(1)}, u32[]{:S(2)}, u32[]{:S(2)}) async-start(bf16[8,16,384]{2,1,0:T(8,128)(2,1)} %bitcast.8), calls=%async_computation.3 | async-start | bytes 196608 | tf_op jit(solution)/shard_map/all_to_all | solution.py:390
  165.5 12.4 %all-to-all-start.5 = ((bf16[16,2,1536]{2,1,0:T(2,128)(2,1)}), bf16[16,2,1536]{2,1,0:T(2,128)(2,1)S(1)}, u32[]{:S(2)}, u32[]{:S(2)}) async-start(bf16[16,2,1536]{2,1,0:T(2,128)(2,1)} %reshape.58), calls=%async_computation.5 | async-start | bytes 196608 | tf_op jit(solution)/shard_map/all_to_all | solution.py:393
  261.4 3.0 %copy-start.20 = (f32[384,384]{1,0:T(8,128)S(1)}, f32[384,384]{1,0:T(8,128)}, u32[]{:S(2)}) copy-start(f32[384,384]{1,0:T(8,128)} %get-tuple-element.110) | copy-start | bytes 1769476
  261.4 3.8 %copy-start.17 = (f32[384,1152]{1,0:T(8,128)S(1)}, f32[384,1152]{1,0:T(8,128)}, u32[]{:S(2)}) copy-start(f32[384,1152]{1,0:T(8,128)} %get-tuple-element.111) | copy-start | bytes 5308420
  265.2 1.4 copy-start.19
  265.2 2.7 copy-start.16
  267.9 2.5 copy-start.15
Sparse Core Ops, SparseCore 0:
  95.8 162.8 all-reduce.4

commit v2 on v1

--- a/solution.py
+++ b/solution.py
@@ -6,7 +6,7 @@
 from jax import lax
 from jax.experimental import pallas as pl
 from jax.experimental.pallas import tpu as pltpu
-from jax.sharding import PartitionSpec as P
+from jax.sharding import Mesh, PartitionSpec as P
 
 H = 12
 P_SIZE = 4
@@ -20,6 +20,62 @@
 STRENGTH = math.sqrt(2.0 / (9.0 * P_SIZE)) * math.sqrt(0.5)
 F32 = jnp.float32
 BF16 = jnp.bfloat16
+EVERYONE = ("line", "core", "res")
+SHARERS = 64
+GAIN_LANE = 6 * POINTS - 256
+
+PIECES = {
+    "up": (C, HID),
+    "ipa_out": (C, C),
+    "ipa_points": (C, C),
+    "ipa_qkv": (C, 3 * C),
+    "down": (HID, C),
+    "time_qkv": (C, 3 * C),
+    "time_out": (C, C),
+}
+EARLY_UNITS = [20, 19]
+LATE_UNITS = [6, 6]
+EARLY = max(EARLY_UNITS) * C
+LATE = max(LATE_UNITS) * C
+HALF = -(-(EARLY + LATE) // (SHARERS * 16)) * SHARERS * 16
+
+
+def place_units():
+    units, taken = {}, {True: [0, 0], False: [0, 0]}
+    for name, (rows, columns) in PIECES.items():
+        late = name.startswith("time")
+        room = LATE_UNITS if late else EARLY_UNITS
+        units[name] = []
+        for _ in range(rows * columns // (C * 128)):
+            half = 0 if taken[late][0] < room[0] else 1
+            units[name].append((half, (EARLY if late else 0) + taken[late][half] * C))
+            taken[late][half] += 1
+    return units
+
+
+UNITS = place_units()
+
+
+def halves(core, keep_ref, give_ref):
+    def put(name, value):
+        tiles = value.shape[1] // 128
+        base = EARLY if name.startswith("time") else 0
+        pieces = [[], []]
+        for unit, (half, at) in enumerate(UNITS[name]):
+            down, across = (unit // tiles) * C, (unit % tiles) * 128
+            part = value[down : down + C, across : across + 128].astype(BF16)
+            pieces[half].append((at - base, part))
+
+        for half in range(2):
+            for ref, mine in ((keep_ref, True), (give_ref, False)):
+                @pl.when((core == half) == mine)
+                def store(ref=ref, parts=pieces[half]):
+                    for at, part in parts:
+                        ref[at : at + C, :] = part
+
+    return put
+
+
 PARAMS = pltpu.CompilerParams(vmem_limit_bytes=48 * 1024 * 1024)
 
 
@@ -70,8 +126,10 @@
     return jnp.concatenate([tile * mask for mask in masks], axis=0)
 
 
-def time_forward(x_ref, wqkv_ref, wout_ref, x1_ref, qkv_ref, shares_ref, mix_ref):
-    x = x_ref[...].astype(F32)
+def time_forward(
+    place_ref, neighbors_ref, rows_ref, wqkv_ref, wout_ref, sent_ref, qkv_ref, shares_ref, mix_ref
+):
+    x = rows_ref[:, 0:C].astype(F32)
     normed, _ = norm(x)
     qkv_ref[...] = mm(normed.astype(BF16), wqkv_ref[...]).astype(BF16)
     masks = tile_masks()
@@ -87,17 +145,24 @@
             shares_ref[:, h * 128 : (h + 1) * 128] = shares.astype(BF16)
         mixed = mm(shares_ref[:, g * 512 : (g + 1) * 512], masked_stack(v, masks))
         mix_ref[:, g * 128 : (g + 1) * 128] = mixed.astype(BF16)
-    x1_ref[...] = (x + mm(mix_ref[...], wout_ref[...])).astype(BF16)
+    sent_ref[:, 0:C] = (x + mm(mix_ref[...], wout_ref[...])).astype(BF16)
+    sent_ref[:, C : C + 512] = rows_ref[:, C : C + 512]
+    lane = lax.broadcasted_iota(jnp.int32, (N, 128), 1)
+    count = jnp.zeros((N, 128), F32)
+    for n in range(NB):
+        count = count + jnp.where(lane == neighbors_ref[place_ref[0], n], 1.0, 0.0)
+    sent_ref[:, C + 512 : C + 640] = count.astype(BF16)
 
 
 def time_backward(
-    dx1_ref, x_ref, qkv_ref, shares_ref, mix_ref, wqkv_ref, wout_ref,
-    dx_ref, gqkv_ref, gout_ref, dqkv_ref, dcol_ref, pcol_ref,
+    core_ref, back_ref, rows_ref, qkv_ref, shares_ref, mix_ref, wqkv_ref, wout_ref,
+    sent_ref, keep_ref, give_ref, dqkv_ref, dcol_ref, pcol_ref,
 ):
-    dx1 = dx1_ref[...]
-    normed, inverse = norm(x_ref[...].astype(F32))
+    put = halves(core_ref[0], keep_ref, give_ref)
+    dx1 = back_ref[:, 0:C]
+    normed, inverse = norm(rows_ref[:, 0:C].astype(F32))
     dmix = mt(dx1, wout_ref[...]).astype(BF16)
-    gout_ref[...] = tm(mix_ref[...], dx1).astype(gout_ref.dtype)
+    put("time_out", tm(mix_ref[...], dx1))
     masks = tile_masks()
     for g in range(3):
         q = qkv_ref[:, g * 128 : (g + 1) * 128]
@@ -121,10 +186,11 @@
         dqkv_ref[:, g * 128 : (g + 1) * 128] = dq.astype(BF16)
         dqkv_ref[:, C + g * 128 : C + (g + 1) * 128] = dk.astype(BF16)
         dqkv_ref[:, 2 * C + g * 128 : 2 * C + (g + 1) * 128] = dv.astype(BF16)
-    gqkv_ref[...] = tm(normed.astype(BF16), dqkv_ref[...]).astype(gqkv_ref.dtype)
+    put("time_qkv", tm(normed.astype(BF16), dqkv_ref[...]))
     dnormed = mt(dqkv_ref[...], wqkv_ref[...]).astype(BF16).astype(F32)
     pulled = norm_pull(dnormed, normed, inverse).astype(BF16).astype(F32)
-    dx_ref[...] = (dx1.astype(F32) + pulled).astype(BF16)
+    sent_ref[:, 0:C] = (dx1.astype(F32) + pulled).astype(BF16)
+    sent_ref[:, C : 2 * C] = back_ref[:, C : 2 * C]
 
 
 def selectors():
@@ -140,7 +206,7 @@
         turn[9 + a, 3 * 256 + at] = 1.0
     spread = np.zeros((128, 256), np.float32)
     spread[16:32] = heads
-    gather = np.zeros((6 * 256, 6 * POINTS), np.float32)
+    gather = np.zeros((6 * 256, C), np.float32)
     for c in range(2):
         for b in range(3):
             for a in range(3):
@@ -150,17 +216,21 @@
 
 
 def point_attention(
-    weight_ref, x1_ref, side_ref, wqkv_ref, wpts_ref, wrep_ref, wout_ref, wup_ref, wdown_ref,
+    core_ref, weight_ref, rows_ref, wqkv_ref, wpts_ref, wrep_ref, wout_ref, wup_ref, wdown_ref,
     heads_ref, turn_ref, spread_ref, gather_ref,
-    updated_ref, dx1_ref, gqkv_ref, gpts_ref, gout_ref, gup_ref, gdown_ref, gweight_ref,
+    back_ref, keep_ref, give_ref,
     qkv_ref, mix_ref, shares_ref, point_ref, prow_ref, pcol_ref, drow_ref, dcol_ref,
-    dqkv_ref, dlocal_ref, keys_ref, queries_ref,
+    dqkv_ref, dlocal_ref, keys_ref, queries_ref, side_ref,
 ):
+    put = halves(core_ref[0], keep_ref, give_ref)
+    for ref in (keep_ref, give_ref):
+        ref[EARLY - C : EARLY, :] = jnp.zeros((C, 128), BF16)
     masks = tile_masks()
     row = lax.broadcasted_iota(jnp.int32, (N, N), 0)
     col = lax.broadcasted_iota(jnp.int32, (N, N), 1)
     order = jnp.where((col // 8 == row % 16) & (col % 8 == row // 16), 1.0, 0.0).astype(BF16)
-    x1 = mm(order, x1_ref[...])
+    x1 = mm(order, rows_ref[:, 0:C])
+    side_ref[...] = mm(order, rows_ref[:, C : C + 640]).astype(BF16)
     normed, inverse = norm(x1)
     n2 = normed.astype(BF16)
     qkv_ref[...] = mm(n2, wqkv_ref[...]).astype(BF16)
@@ -174,7 +244,7 @@
     strength = jnp.where(lane < 3 * POINTS, soft * STRENGTH, 0.0)
     head_masks = [jnp.where(lane_head == h, 1.0, 0.0).astype(BF16) for h in range(H)]
 
-    turned = mm(side_ref[:, 512:640], turn_ref[...])
+    turned = mm(side_ref[:, C : C + 128], turn_ref[...])
     turns = [turned[:, b * 256 : (b + 1) * 256] for b in range(3)]
     local = mm(n2, wrep_ref[...])
     placed = []
@@ -194,7 +264,7 @@
     keys_one = jnp.where(ones, 1.0, gk).astype(BF16)
     queries_one = jnp.where(ones, 1.0, gq).astype(BF16)
     two_keys = jnp.concatenate([gk_bf, gk_bf], axis=1)
-    count = side_ref[:, 384:512].astype(F32)
+    count = side_ref[:, C + 128 : C + 256].astype(F32)
     near = count > 0.0
 
     for g in range(3):
@@ -221,7 +291,7 @@
         mixed = mm(prow_ref[:, g * 512 : (g + 1) * 512], masked_stack(v, masks))
         mix_ref[:, g * 128 : (g + 1) * 128] = mixed.astype(BF16)
 
-    cot = side_ref[:, 0:384]
+    cot = side_ref[:, 0:C]
     x2 = (x1 + mm(mix_ref[...], wout_ref[...])).astype(BF16).astype(F32)
     normed2, inverse2 = norm(x2)
     n3 = normed2.astype(BF16)
@@ -232,17 +302,18 @@
     slope = 0.5 * (1.0 + bent) + 0.5 * u * (1.0 - bent * bent) * root * (
         1.0 + 3.0 * 0.044715 * u * u
     )
-    updated_ref[...] = (x2 + mm(hidden, wdown_ref[...])).astype(BF16)
-    gdown_ref[...] = tm(hidden, cot).astype(gdown_ref.dtype)
+    updated = (x2 + mm(hidden, wdown_ref[...])).astype(BF16)
+    back_ref[:, C : 2 * C] = tm(order, updated).astype(BF16)
+    put("down", tm(hidden, cot))
     dhidden = mt(cot, wdown_ref[...]).astype(BF16).astype(F32)
     du = (dhidden * slope).astype(BF16)
-    gup_ref[...] = tm(n3, du).astype(gup_ref.dtype)
+    put("up", tm(n3, du))
     dn3 = mt(du, wup_ref[...]).astype(BF16).astype(F32)
     dx2 = (cot.astype(F32) + norm_pull(dn3, normed2, inverse2).astype(BF16).astype(F32)).astype(
         BF16
     )
     dmix = mt(dx2, wout_ref[...]).astype(BF16)
-    gout_ref[...] = tm(mix_ref[...], dx2).astype(gout_ref.dtype)
+    put("ipa_out", tm(mix_ref[...], dx2))
 
     gains = []
     for g in range(3):
@@ -267,13 +338,15 @@
         dqkv_ref[:, C + g * 128 : C + (g + 1) * 128] = dk.astype(BF16)
         dqkv_ref[:, 2 * C + g * 128 : 2 * C + (g + 1) * 128] = dv.astype(BF16)
 
-    gain = jnp.sum(jnp.concatenate(gains + gains[:4], axis=0), axis=1, keepdims=True)
-    row16 = lax.broadcasted_iota(jnp.int32, (16, 128), 0)
-    raw16 = jnp.zeros((16, 128), F32)
+    lane128 = lax.broadcasted_iota(jnp.int32, (1, 128), 1)
+    gain = jnp.zeros((1, 128), F32)
+    raw_row = jnp.zeros((1, 128), F32)
     for h in range(H):
-        raw16 = jnp.where(row16 == h, weight_ref[h], raw16)
-    soft16 = jnp.maximum(raw16, 0.0) + jnp.log(1.0 + jnp.exp(-jnp.abs(raw16)))
-    gweight_ref[...] = (gain / ((1.0 + jnp.exp(-raw16)) * soft16)).astype(gweight_ref.dtype)
+        here = lane128 == GAIN_LANE + h
+        gain = jnp.where(here, jnp.sum(gains[h], axis=1, keepdims=True), gain)
+        raw_row = jnp.where(here, weight_ref[h], raw_row)
+    soft_row = jnp.maximum(raw_row, 0.0) + jnp.log(1.0 + jnp.exp(-jnp.abs(raw_row)))
+    gain = gain / ((1.0 + jnp.exp(-raw_row)) * soft_row)
 
     from_keys = mm(drow_ref[...], keys_ref[...])
     from_queries = tm(dcol_ref[...], queries_ref[...])
@@ -287,53 +360,54 @@
         dlocal_ref[:, (3 + b) * 256 : (4 + b) * 256] = (turns[b] * dgk).astype(BF16)
     dpoints = mm(dlocal_ref[...], gather_ref[...]).astype(BF16)
     dqkv = dqkv_ref[...]
-    gqkv_ref[...] = tm(n2, dqkv).astype(gqkv_ref.dtype)
-    gpts_ref[...] = tm(n2, dpoints).astype(gpts_ref.dtype)
-    dn2 = (mt(dqkv, wqkv_ref[...]) + mt(dpoints, wpts_ref[...])).astype(BF16).astype(F32)
+    put("ipa_qkv", tm(n2, dqkv))
+    gpts = tm(n2, dpoints)
+    first = lax.broadcasted_iota(jnp.int32, (C, 128), 0) == 0
+    last = gpts[:, 256:384] + jnp.where(first, gain, 0.0)
+    put("ipa_points", jnp.concatenate([gpts[:, 0:256], last], axis=1))
+    dn2 = (mt(dqkv, wqkv_ref[...]) + mt(dpoints[:, 0 : 6 * POINTS], wpts_ref[...])).astype(BF16).astype(F32)
     dx1 = (dx2.astype(F32) + norm_pull(dn2, normed, inverse).astype(BF16).astype(F32)).astype(BF16)
-    dx1_ref[...] = tm(order, dx1).astype(BF16)
+    back_ref[:, 0:C] = tm(order, dx1).astype(BF16)
 
 
 def like(shape, dtype):
     return jax.ShapeDtypeStruct(shape, dtype)
 
 
-GRAD = F32
-
-
-def call_time_forward(x, w_qkv, w_out):
+def call_time_forward(place, neighbors, rows, w_qkv, w_out):
+    smem, vmem = pl.BlockSpec(memory_space=pltpu.SMEM), pl.BlockSpec(memory_space=pltpu.VMEM)
     return pl.pallas_call(
         time_forward,
+        in_specs=[smem, smem, vmem, vmem, vmem],
         out_shape=(
-            like((N, C), BF16), like((N, 3 * C), BF16), like((N, H * N), BF16), like((N, C), BF16),
+            like((N, 1024), BF16), like((N, 3 * C), BF16), like((N, H * N), BF16),
+            like((N, C), BF16),
         ),
         compiler_params=PARAMS,
         name="time_forward",
-    )(x, w_qkv, w_out)
-
-
-def call_time_backward(dx1, x, qkv, shares, mix, w_qkv, w_out):
+    )(place, neighbors, rows, w_qkv, w_out)
+
+
+def call_time_backward(core, back, rows, qkv, shares, mix, w_qkv, w_out):
+    smem, vmem = pl.BlockSpec(memory_space=pltpu.SMEM), pl.BlockSpec(memory_space=pltpu.VMEM)
     return pl.pallas_call(
         time_backward,
-        out_shape=(like((N, C), BF16), like((C, 3 * C), GRAD), like((C, C), GRAD)),
+        in_specs=[smem] + [vmem] * 7,
+        out_shape=(like((N, 2 * C), BF16), like((LATE, 128), BF16), like((LATE, 128), BF16)),
         scratch_shapes=[
             pltpu.VMEM((N, 3 * C), BF16), pltpu.VMEM((4 * N, N), BF16), pltpu.VMEM((4 * N, N), BF16),
         ],
         compiler_params=PARAMS,
         name="time_backward",
-    )(dx1, x, qkv, shares, mix, w_qkv, w_out)
-
-
-def call_point_attention(weight, x1, side, w_qkv, w_pts, w_rep, w_out, w_up, w_down):
-    whole = pl.BlockSpec(memory_space=pltpu.VMEM)
+    )(core, back, rows, qkv, shares, mix, w_qkv, w_out)
+
+
+def call_point_attention(core, weight, rows, w_qkv, w_pts, w_rep, w_out, w_up, w_down):
+    smem, vmem = pl.BlockSpec(memory_space=pltpu.SMEM), pl.BlockSpec(memory_space=pltpu.VMEM)
     return pl.pallas_call(
         point_attention,
-        in_specs=[pl.BlockSpec(memory_space=pltpu.SMEM)] + [whole] * 12,
-        out_shape=(
-            like((N, C), BF16), like((N, C), BF16), like((C, 3 * C), GRAD),
-            like((C, 6 * POINTS), GRAD), like((C, C), GRAD), like((C, HID), GRAD),
-            like((HID, C), GRAD), like((16, 128), GRAD),
-        ),
+        in_specs=[smem, smem] + [vmem] * 11,
+        out_shape=(like((N, 2 * C), BF16), like((EARLY, 128), BF16), like((EARLY, 128), BF16)),
         scratch_shapes=[
             pltpu.VMEM((N, 3 * C), BF16), pltpu.VMEM((N, C), BF16),
             pltpu.VMEM((N, H * N), F32), pltpu.VMEM((N, H * N), F32),
@@ -341,10 +415,81 @@
             pltpu.VMEM((N, H * N), BF16), pltpu.VMEM((H * N, N), BF16),
             pltpu.VMEM((N, 3 * C), BF16), pltpu.VMEM((N, 6 * 256), BF16),
             pltpu.VMEM((H * N, 256), BF16), pltpu.VMEM((H * N, 256), BF16),
+            pltpu.VMEM((N, 640), BF16),
         ],
         compiler_params=PARAMS,
         name="point_attention",
-    )(weight, x1, side, w_qkv, w_pts, w_rep, w_out, w_up, w_down, *selectors())
+    )(core, weight, rows, w_qkv, w_pts, w_rep, w_out, w_up, w_down, *selectors())
+
+
+def add_halves(keep_early_ref, got_early_ref, keep_late_ref, got_late_ref, total_ref):
+    early = keep_early_ref[...].astype(F32) + got_early_ref[...].astype(F32)
+    total_ref[0:EARLY, :] = early.astype(BF16)
+    late = keep_late_ref[...].astype(F32) + got_late_ref[...].astype(F32)
+    total_ref[EARLY : EARLY + LATE, :] = late.astype(BF16)
+    total_ref[EARLY + LATE :, :] = jnp.zeros((HALF - EARLY - LATE, 128), BF16)
+
+
+def call_add_halves(*parts):
+    return pl.pallas_call(
+        add_halves, out_shape=like((HALF, 128), BF16), compiler_params=PARAMS, name="add_halves"
+    )(*parts)
+
+
+def add_parts(parts_ref, copies_ref):
+    count = parts_ref.shape[0]
+    total = parts_ref[0].astype(F32)
+    for k in range(1, count):
+        total = total + parts_ref[k].astype(F32)
+    total = total.astype(BF16)
+    for k in range(count):
+        copies_ref[k] = total
+
+
+def call_add_parts(parts):
+    return pl.pallas_call(
+        add_parts, out_shape=like(parts.shape, BF16), compiler_params=PARAMS, name="add_parts"
+    )(parts)
+
+
+def unpack(core_ref, mine_ref, other_ref, *out_refs):
+    outs = dict(zip(PIECES, out_refs))
+    gain_ref = out_refs[-1]
+
+    def read(halves_refs):
+        for name, (rows, columns) in PIECES.items():
+            for unit, (half, at) in enumerate(UNITS[name]):
+                value = halves_refs[half][at : at + C, :].astype(F32)
+                tiles = columns // 128
+                down, across = (unit // tiles) * C, (unit % tiles) * 128
+                if name == "ipa_points" and across == 256:
+                    outs[name][down : down + C, across:] = value[:, : 6 * POINTS - 256]
+                    gain_ref[...] = value[0:1, :]
+                else:
+                    outs[name][down : down + C, across : across + 128] = value
+
+    @pl.when(core_ref[0] == 0)
+    def first():
+        read((mine_ref, other_ref))
+
+    @pl.when(core_ref[0] != 0)
+    def second():
+        read((other_ref, mine_ref))
+
+
+def call_unpack(core, mine, other):
+    smem, vmem = pl.BlockSpec(memory_space=pltpu.SMEM), pl.BlockSpec(memory_space=pltpu.VMEM)
+    shapes = [
+        like((rows, 6 * POINTS if name == "ipa_points" else columns), F32)
+        for name, (rows, columns) in PIECES.items()
+    ]
+    return pl.pallas_call(
+        unpack,
+        in_specs=[smem, vmem, vmem],
+        out_shape=(*shapes, like((1, 128), F32)),
+        compiler_params=PARAMS,
+        name="unpack",
+    )(core, mine, other)
 
 
 def repeat_points(weight):
@@ -353,60 +498,63 @@
     return jnp.pad(tripled, ((0, 0), (0, 0), (0, 256 - 3 * POINTS))).reshape(C, 6 * 256)
 
 
-def side_rows(cotangent, neighbors, rigid_frames):
-    frames, residues, _ = cotangent.shape
-    hits = neighbors[:, :, None] == lax.broadcasted_iota(jnp.int32, (1, 1, N), 2)
-    count = jnp.sum(hits.astype(F32), axis=1).astype(BF16)
-    return jnp.concatenate(
-        [
-            cotangent,
-            jnp.broadcast_to(count[None], (frames, residues, N)),
-            jnp.pad(jnp.transpose(rigid_frames, (1, 2, 0)), ((0, 0), (0, 0), (0, 116))),
-        ],
-        axis=2,
-    )
-
-
 def body(
     tokens, rigid_frames, neighbors, w_time_qkv, w_time_out, w_ipa_qkv, w_ipa_points,
     point_weight, w_ipa_out, w_up, w_down, cotangent,
 ):
-    everyone = ("frame", "res")
-    x = lax.all_to_all(tokens, "frame", split_axis=1, concat_axis=0, tiled=True).reshape(N, C)
-    side = lax.all_to_all(
-        side_rows(cotangent, neighbors, rigid_frames), "res", split_axis=0, concat_axis=0, tiled=True
-    ).reshape(N, 640)
-    x1, qkv, shares, mix = call_time_forward(x, w_time_qkv, w_time_out)
-    x1 = lax.all_to_all(x1, everyone, split_axis=0, concat_axis=0, tiled=True)
-    updated, dx1, g_ipa_qkv, g_pts, g_ipa_out, g_up, g_down, g_weight = call_point_attention(
-        point_weight, x1, side, w_ipa_qkv, w_ipa_points, repeat_points(w_ipa_points), w_ipa_out,
+    frames, residues = tokens.shape[:2]
+    place = lax.axis_index(("line", "core")).astype(jnp.int32).reshape(1)
+    core = lax.axis_index("core").astype(jnp.int32).reshape(1)
+    rigid = jnp.pad(jnp.transpose(rigid_frames, (1, 2, 0)), ((0, 0), (0, 0), (0, 116)))
+    rows = lax.all_to_all(
+        jnp.concatenate([tokens, cotangent, rigid], axis=2),
+        ("line", "core"), split_axis=1, concat_axis=0, tiled=True,
+    ).reshape(N, 2 * C + 128)
+    sent, qkv, shares, mix = call_time_forward(place, neighbors, rows, w_time_qkv, w_time_out)
+    moved = lax.all_to_all(sent, EVERYONE, split_axis=0, concat_axis=0, tiled=True)
+    back, keep_early, give_early = call_point_attention(
+        core, point_weight, moved, w_ipa_qkv, w_ipa_points, repeat_points(w_ipa_points), w_ipa_out,
         w_up, w_down,
     )
-    dx1 = lax.all_to_all(dx1, everyone, split_axis=0, concat_axis=0, tiled=True)
-    dx, g_time_qkv, g_time_out = call_time_backward(
-        dx1, x, qkv, shares, mix, w_time_qkv, w_time_out
-    )
-    frames, residues = tokens.shape[:2]
-    output = lax.all_to_all(
-        updated.reshape(frames, residues, C), "res", split_axis=0, concat_axis=0, tiled=True
-    )
-    token_grad = lax.all_to_all(
-        dx.reshape(N, 1, C), "frame", split_axis=0, concat_axis=1, tiled=True
-    )
-    early = lax.psum((g_ipa_qkv, g_pts, g_ipa_out, g_up, g_down, g_weight), everyone)
-    late = lax.psum((g_time_qkv, g_time_out), everyone)
+    swap = [(0, 1), (1, 0)]
+    got_early = lax.ppermute(give_early, "core", swap)
+    back = lax.all_to_all(back, EVERYONE, split_axis=0, concat_axis=0, tiled=True)
+    ended, keep_late, give_late = call_time_backward(
+        core, back, rows, qkv, shares, mix, w_time_qkv, w_time_out
+    )
+    got_late = lax.ppermute(give_late, "core", swap)
+    ended = lax.all_to_all(
+        ended.reshape(N, 1, 2 * C), ("line", "core"), split_axis=0, concat_axis=1, tiled=True
+    )
+    packed = call_add_halves(keep_early, got_early, keep_late, got_late)
+    parts = lax.all_to_all(
+        packed.reshape(SHARERS, HALF // SHARERS, 128), ("line", "res"), split_axis=0, concat_axis=0,
+        tiled=True,
+    )
+    mine = lax.all_to_all(
+        call_add_parts(parts), ("line", "res"), split_axis=0, concat_axis=0, tiled=True
+    ).reshape(HALF, 128)
+    other = lax.ppermute(mine, "core", swap)
+    *grads, gain = call_unpack(core, mine, other)
+    grads = dict(zip(PIECES, grads))
     return (
-        output, token_grad, late[0], late[1], early[0], early[1], early[5][:H, 0], early[2],
-        early[3], early[4],
+        ended[:, :, C:], ended[:, :, :C], grads["time_qkv"], grads["time_out"], grads["ipa_qkv"],
+        grads["ipa_points"], gain[0, GAIN_LANE : GAIN_LANE + H], grads["ipa_out"], grads["up"],
+        grads["down"],
     )
 
 
 def solution(mesh):
-    rows = P("frame", "res", None)
-    placed = (rows, P(None, "frame", "res"), P("res", None)) + (P(),) * 8 + (rows,)
+    devices = mesh.devices
+    split = Mesh(
+        devices.reshape(devices.shape[0] // 2, 2, devices.shape[1]), ("line", "core", "res")
+    )
+    frame = ("line", "core")
+    rows = P(frame, "res", None)
+    placed = (rows, P(None, frame, "res"), P("res", None)) + (P(),) * 8 + (rows,)
     return jax.shard_map(
         body,
-        mesh=mesh,
+        mesh=split,
         in_specs=placed,
         out_specs=(rows, rows) + (P(),) * 8,
         check_vma=False,

time: 280 us -> 199 us (0.71)
  waiting for transfers between devices: 102 us -> 17.7 us
  blocking collectives: 80.4 us -> 103 us
  between operations: 14.3 us -> 0.88 us
  Pallas kernels: 17.7 us -> 28.2 us
  local copies, waits for them, and re-layouts: 32.5 us -> 23.2 us
  starting transfers between devices: 27 us -> 19.6 us
    all_to_all x1 -> x4, blocking collectives: 15.4 us -> 103 us  [the longest x1 39.8 us: body(): lax.all_to_all(packed.reshape(SHARERS, HALF // SHARERS, 128), ('line', 'r...]
    psum x1 -> x0, waiting for transfers between devices: 80.1 us -> none  [body(): late = lax.psum((g_time_qkv, g_time_out), everyone)]
    psum x1 -> x0, blocking collectives: 65 us -> none  [body(): lax.psum((g_ipa_qkv, g_pts, g_ipa_out, g_up, g_down, g_weight), everyone)]
    all_to_all x5 -> x2, starting transfers between devices: 26.9 us -> 15.1 us  [the longest x1 9.46 us: body(): lax.all_to_all(jnp.concatenate([tokens, cotangent, rigid], axis=2), ('lin...]
    pallas_call x3 -> x6, Pallas kernels: 17.7 us -> 28.2 us  [the longest x1 12.8 us: call_point_attention(): pl.pallas_call(point_attention, in_specs=[smem, smem] + [vmem] * 11, out_...]
    unnamed x65 -> x58, local copies, waits for them, and re-layouts: 29.7 us -> 20.4 us
    all_to_all x5 -> x2, waiting for transfers between devices: 21.8 us -> 16.1 us  [the longest x1 8.45 us: body(): lax.all_to_all(jnp.concatenate([tokens, cotangent, rigid], axis=2), ('lin...]
    ppermute x0 -> x3, starting transfers between devices: none -> 4.52 us  [the longest x1 3.12 us: body(): other = lax.ppermute(mine, 'core', swap)]
  transfers between devices with their start and end apart: 6 -> 5, of which waited for: 5 -> 3; matrix products, arithmetic and copies ran while one was open for 4% -> 4% of each run, Pallas kernels for 0% -> 1%
where the time goes in v2:
time: 199 us; the launch traced here: 198 us
  blocking collectives  103 us (52%)
  Pallas kernels  28.2 us (14%)
  local copies, waits for them, and re-layouts  23.2 us (12%)
  starting transfers between devices  19.6 us (10%)
  waiting for transfers between devices  17.7 us (9%)
  other arithmetic  4.99 us (3%)
    all_to_all x1, blocking collectives, body(): lax.all_to_all(packed.reshape(SHARERS, HALF // SHARERS, 128), ('line', 'r...  39.8 us
    all_to_all x1, blocking collectives, body(): lax.all_to_all(call_add_parts(parts), ('line', 'res'), split_axis=0, conc...  37.9 us
    unnamed x58, local copies, waits for them, and re-layouts  20.4 us
    all_to_all x1, blocking collectives, body(): lax.all_to_all(back, EVERYONE, split_axis=0, concat_axis=0, tiled=True)  13.9 us
    pallas_call x1, Pallas kernels, call_point_attention(): pl.pallas_call(point_attention, in_specs=[smem, smem] + [vmem] * 11, out_...  12.8 us
    all_to_all x1, blocking collectives, body(): lax.all_to_all(ended.reshape(N, 1, 2 * C), ('line', 'core'), split_axis=0...  11.3 us
    all_to_all x1, starting transfers between devices, body(): lax.all_to_all(jnp.concatenate([tokens, cotangent, rigid], axis=2), ('lin...  9.46 us
    all_to_all x1, waiting for transfers between devices, body(): lax.all_to_all(jnp.concatenate([tokens, cotangent, rigid], axis=2), ('lin...  8.45 us
  transfers between devices with their start and end apart: 5, of which 3 were waited for; matrix products, arithmetic and copies ran while one was open for 4% of the time, Pallas kernels for 1%

profile of v2, /device:TPU:1, one launch (start us, length us, event | category | flops | bytes accessed | tf_op | source)
XLA Modules:
  0.0 197.5 jit_solution(1261745862371621367)
XLA Ops:
  0.6 0.0 copy-start
  0.7 1.0 copy.50
  1.6 0.9 copy.51
  2.5 0.9 copy.52
  3.4 0.0 copy-start.20
  3.5 0.7 fusion.6
  4.2 9.5 %all-to-all-start = ((bf16[8,16,896]{2,0,1:T(8,128)(2,1)}), bf16[8,16,896]{2,0,1:T(8,128)(2,1)S(1)}, u32[]{:S(2)}, u32[]{:S(2)}) async-start(bf16[8,16,896]{2,0,1:T(8,128)(2,1)} %fusion.6), calls=%async_computation | async-start | bytes 458752 | tf_op jit(solution)/shard_map/all_to_all | solution.py:509
  13.6 8.4 %all-to-all-done = bf16[8,16,896]{2,0,1:T(8,128)(2,1)S(1)} async-done(((bf16[8,16,896]{2,0,1:T(8,128)(2,1)}), bf16[8,16,896]{2,0,1:T(8,128)(2,1)S(1)}, u32[]{:S(2)}, u32[]{:S(2)}) %all-to-all-start) | async-done | bytes 229408 | tf_op jit(solution)/shard_map/all_to_all | solution.py:509
  22.1 0.0 copy-done
  22.1 1.0 copy-done.2
  23.0 0.7 copy-done.17
  23.7 2.5 %time_forward.1 = (bf16[128,1024]{1,0:T(8,128)(2,1)S(1)}, bf16[128,1152]{1,0:T(8,128)(2,1)S(1)}, bf16[128,1536]{1,0:T(8,128)(2,1)S(1)}, bf16[128,384]{1,0:T(8,128)(2,1)S(1)}) custom-call(s32[1]{0:T(128)} %bitcast.1.place_ref, s32[16,32]{1,0:T(8,128)S(1)} %copy-done.17, bf16[128,896]{1,0:T(8,128)(2,1)S(1)} %bitcast.32, bf16[384,1152]{1,0:T(8,128)(2,1)S(1)} %copy-done, ...), custom_call_target="tpu_custom_call" | custom-call | tf_op jit(solution)/shard_map/time_forward/pallas_call | solution.py:379
  26.3 0.0 copy-start.7
  26.3 0.7 copy-done.7
  27.0 0.7 copy-done.10
  27.7 0.5 broadcast.16
  28.3 0.8 reduce
  29.1 0.9 reshape.57
  30.0 5.6 %all-to-all-start.1 = ((bf16[128,2,512]{2,1,0:T(2,128)(2,1)}), bf16[128,2,512]{2,1,0:T(2,128)(2,1)}, u32[]{:S(2)}, u32[]{:S(2)}) async-start(bf16[128,2,512]{2,1,0:T(2,128)(2,1)} %reshape.57), calls=%async_computation.1 | async-start | bytes 524288 | tf_op jit(solution)/shard_map/all_to_all | solution.py:514
  35.6 0.0 copy-done.20
  35.6 0.2 copy.54.wpts_ref
  35.8 1.1 fusion.4
  36.9 0.0 copy-done.14
  36.9 0.0 copy-start.19
  36.9 1.6 copy.55.wrep_ref
  38.6 7.7 %all-to-all-done.1 = bf16[128,2,512]{2,1,0:T(2,128)(2,1)} async-done(((bf16[128,2,512]{2,1,0:T(2,128)(2,1)}), bf16[128,2,512]{2,1,0:T(2,128)(2,1)}, u32[]{:S(2)}, u32[]{:S(2)}) %all-to-all-start.1) | async-done | bytes 262176 | tf_op jit(solution)/shard_map/all_to_all | solution.py:514
  46.3 2.8 %reshape.58 = bf16[128,1,1024]{2,1,0:T(2,128)(2,1)} reshape(bf16[128,2,512]{2,1,0:T(2,128)(2,1)} %all-to-all-done.1) | data formatting | bytes 524288
  49.0 1.1 copy.67
  50.2 0.0 copy-start.4
  50.2 1.3 copy-done.4
  51.5 1.3 copy-done.5
  52.8 1.0 copy-done.9
  53.7 0.9 copy-done.12
  54.7 12.8 %point_attention.1 = (bf16[128,768]{1,0:T(8,128)(2,1)S(1)}, bf16[7680,128]{1,0:T(8,128)(2,1)}, bf16[7680,128]{1,0:T(8,128)(2,1)}) custom-call(s32[1]{0:T(128)} %bitcast.core_ref, f32[12]{0:T(128)S(1)} %copy-done.19, bf16[128,1024]{1,0:T(8,128)(2,1)S(1)} %bitcast.34, bf16[384,1152]{1,0:T(8,128)(2,1)S(1)} %copy-done.6, bf16[384,288]{1,0:T(8,128)(2,1)S(1)} %copy.54.wpts_ref, ...), custom_call_target="tpu_custom_call" | custom-call | tf_op jit(solution)/shard_map/point_attention/pallas_call | solution.py:407
  67.4 0.7 copy-done.13
  68.1 0.7 collective-permute-start
  68.8 1.6 reduce.1
  70.4 0.1 reshape.59
  70.5 13.9 %all_to_all.65 = bf16[128,2,384]{2,1,0:T(2,128)(2,1)S(1)} all-to-all(bf16[128,2,384]{2,1,0:T(2,128)(2,1)S(1)} %reshape.59), channel_id=1, replica_groups=mesh['line'=8,'core'=2,'res'=8] {'line','core','res'}, dimensions={0} | all-to-all | bytes 393216 | tf_op jit(solution)/shard_map/all_to_all | solution.py:521
  84.4 0.1 reshape.60
  84.6 0.0 copy-done.3
  84.6 0.0 copy-done.8
  84.6 0.0 copy-done.11
  84.6 0.0 copy-done.15
  84.6 2.7 %time_backward.1 = (bf16[128,768]{1,0:T(8,128)(2,1)S(1)}, bf16[2304,128]{1,0:T(8,128)(2,1)S(1)}, bf16[2304,128]{1,0:T(8,128)(2,1)S(1)}) custom-call(s32[1]{0:T(128)} %bitcast.core_ref, bf16[128,768]{1,0:T(8,128)(2,1)S(1)} %bitcast.35, bf16[128,896]{1,0:T(8,128)(2,1)S(1)} %bitcast.33, bf16[128,1152]{1,0:T(8,128)(2,1)S(1)} %copy-done.11, ...), custom_call_target="tpu_custom_call" | custom-call | tf_op jit(solution)/shard_map/time_backward/pallas_call | solution.py:393
  87.3 0.7 collective-permute-start.1
  88.0 1.6 collective-permute-done.1.got_late_ref
  89.6 0.0 collective-permute-done.got_early_ref
  89.7 1.5 copy-done.1
  91.2 3.6 %add_halves.1 = bf16[10240,128]{1,0:T(8,128)(2,1)} custom-call(bf16[7680,128]{1,0:T(8,128)(2,1)S(1)} %copy-done.1, bf16[7680,128]{1,0:T(8,128)(2,1)} %collective-permute-done.got_early_ref, bf16[2304,128]{1,0:T(8,128)(2,1)S(1)} %get-tuple-element.36.keep_late_ref, bf16[2304,128]{1,0:T(8,128)(2,1)S(1)} %collective-permute-done.1.got_late_ref), custom_call_target="tpu_custom_call" | custom-call | tf_op jit(solution)/shard_map/add_halves/pallas_call | solution.py:434
  94.8 39.8 %all_to_all.66.parts_ref = bf16[64,160,128]{2,1,0:T(8,128)(2,1)S(1)} all-to-all(bf16[64,160,128]{2,1,0:T(8,128)(2,1)} %bitcast.39), channel_id=1, replica_groups=mesh['line'=8,'core'=2,'res'=8] {'line','res'}, dimensions={0} | all-to-all | bytes 5242880 | tf_op jit(solution)/shard_map/all_to_all | solution.py:530
  134.7 0.4 add_parts.1
  135.1 37.9 %all_to_all.67 = bf16[64,160,128]{2,1,0:T(8,128)(2,1)S(1)} all-to-all(bf16[64,160,128]{2,1,0:T(8,128)(2,1)S(1)} %add_parts.1), channel_id=1, replica_groups=mesh['line'=8,'core'=2,'res'=8] {'line','res'}, dimensions={0} | all-to-all | bytes 5242880 | tf_op jit(solution)/shard_map/all_to_all | solution.py:534
  173.1 3.1 %collective-permute-start.2 = (bf16[10240,128]{1,0:T(8,128)(2,1)S(1)}, bf16[10240,128]{1,0:T(8,128)(2,1)}, u32[]{:S(2)}, u32[]{:S(2)}) collective-permute-start(bf16[10240,128]{1,0:T(8,128)(2,1)S(1)} %bitcast.30), channel_id=1, source_target_pairs={{0,8},{8,0},{1,9},{9,1},{2,10},{10,2},{3,11},{11,3},{4,12},{12,4},... | collective-permute-start | bytes 7864328 | tf_op jit(solution)/shard_map/ppermute | solution.py:537
  176.2 0.7 reduce.2
  176.9 0.1 reshape.61
  177.0 11.3 %all_to_all.68 = bf16[16,2,3072]{2,1,0:T(2,128)(2,1)S(1)} all-to-all(bf16[16,2,3072]{2,1,0:T(2,128)(2,1)S(1)} %reshape.61), channel_id=1, replica_groups=mesh['line'=8,'core'=2,'res'=8] {'line','core'}, dimensions={0} | all-to-all | bytes 393216 | tf_op jit(solution)/shard_map/all_to_all | solution.py:526
  188.3 0.1 reshape.62
  188.5 0.7 copy.59
  189.1 0.7 copy.58
  189.8 0.0 collective-permute-done.2.other_ref
  189.8 6.2 %unpack.1 = (f32[384,1536]{1,0:T(8,128)}, f32[384,384]{1,0:T(8,128)}, f32[384,288]{1,0:T(8,128)S(1)}, f32[384,1152]{1,0:T(8,128)}, f32[1536,384]{1,0:T(8,128)}, ...) custom-call(s32[1]{0:T(128)} %bitcast.core_ref, bf16[10240,128]{1,0:T(8,128)(2,1)S(1)} %bitcast.31, ...), custom_call_target="tpu_custom_call" | custom-call | tf_op jit(solution)/shard_map/unpack/pallas_call | solution.py:486
  196.0 0.6 slice_bitcast_fusion
  196.5 1.0 copy.60
  (23 shorter events, 0.1 us)
Async XLA Ops:
  0.6 21.4 %copy-start = (bf16[384,1152]{1,0:T(8,128)(2,1)S(1)}, bf16[384,1152]{1,0:T(8,128)(2,1)}, u32[]{:S(2)}) copy-start(bf16[384,1152]{1,0:T(8,128)(2,1)} %wqkv_ref.5) | copy-start | bytes 2654212
  3.4 32.1 %copy-start.20 = (bf16[384,288]{0,1:T(8,128)(2,1)S(1)}, bf16[384,288]{0,1:T(8,128)(2,1)}, u32[]{:S(2)}) copy-start(bf16[384,288]{0,1:T(8,128)(2,1)} %param.22) | copy-start | bytes 663556
  4.2 17.9 %all-to-all-start = ((bf16[8,16,896]{2,0,1:T(8,128)(2,1)}), bf16[8,16,896]{2,0,1:T(8,128)(2,1)S(1)}, u32[]{:S(2)}, u32[]{:S(2)}) async-start(bf16[8,16,896]{2,0,1:T(8,128)(2,1)} %fusion.6), calls=%async_computation | async-start | bytes 458752 | tf_op jit(solution)/shard_map/all_to_all | solution.py:509
  22.1 1.0 copy-start.2
  23.0 0.7 copy-start.17
  26.3 0.7 copy-start.7
  27.0 0.7 copy-start.10
  27.7 9.2 %copy-start.14 = (bf16[128,384]{1,0:T(8,128)(2,1)}, bf16[128,384]{1,0:T(8,128)(2,1)S(1)}, u32[]{:S(2)}) copy-start(bf16[128,384]{1,0:T(8,128)(2,1)S(1)} %get-tuple-element.32.mix_ref) | copy-start | bytes 294916
  30.0 16.3 %all-to-all-start.1 = ((bf16[128,2,512]{2,1,0:T(2,128)(2,1)}), bf16[128,2,512]{2,1,0:T(2,128)(2,1)}, u32[]{:S(2)}, u32[]{:S(2)}) async-start(bf16[128,2,512]{2,1,0:T(2,128)(2,1)} %reshape.57), calls=%async_computation.1 | async-start | bytes 524288 | tf_op jit(solution)/shard_map/all_to_all | solution.py:514
  36.9 13.3 %copy-start.6 = (bf16[384,1152]{1,0:T(8,128)(2,1)S(1)}, bf16[384,1152]{1,0:T(8,128)(2,1)}, u32[]{:S(2)}) copy-start(bf16[384,1152]{1,0:T(8,128)(2,1)} %wqkv_ref.4) | copy-start | bytes 2654212
  36.9 13.3 %copy-start.16 = (bf16[128,256]{1,0:T(8,128)(2,1)S(1)}, bf16[128,256]{1,0:T(8,128)(2,1)}, u32[]{:S(2)}) copy-start(bf16[128,256]{1,0:T(8,128)(2,1)} %constant.26.clone.spread_ref) | copy-start | bytes 196612
  36.9 13.3 %copy-start.18 = (bf16[16,256]{1,0:T(8,128)(2,1)S(1)}, bf16[16,256]{1,0:T(8,128)(2,1)}, u32[]{:S(2)}) copy-start(bf16[16,256]{1,0:T(8,128)(2,1)} %constant.24.clone.heads_ref) | copy-start | bytes 24580
  36.9 13.3 %copy-start.19 = (f32[12]{0:T(128)S(1)}, f32[12]{0:T(128)}, u32[]{:S(2)}) copy-start(f32[12]{0:T(128)} %weight_ref.1) | copy-start | bytes 148
  50.2 1.3 copy-start.4
  51.5 1.3 copy-start.5
  52.7 1.0 copy-start.9
  53.7 0.9 copy-start.12
  67.4 0.7 copy-start.13
  68.1 16.5 %copy-start.3 = (bf16[384,384]{1,0:T(8,128)(2,1)S(1)}, bf16[384,384]{1,0:T(8,128)(2,1)}, u32[]{:S(2)}) copy-start(bf16[384,384]{1,0:T(8,128)(2,1)} %wout_ref.5) | copy-start | bytes 884740
  68.1 16.5 %copy-start.8 = (bf16[128,1536]{1,0:T(8,128)(2,1)S(1)}, bf16[128,1536]{1,0:T(8,128)(2,1)}, u32[]{:S(2)}) copy-start(bf16[128,1536]{1,0:T(8,128)(2,1)} %copy-done.7) | copy-start | bytes 1179652
  68.1 16.5 %copy-start.11 = (bf16[128,1152]{1,0:T(8,128)(2,1)S(1)}, bf16[128,1152]{1,0:T(8,128)(2,1)}, u32[]{:S(2)}) copy-start(bf16[128,1152]{1,0:T(8,128)(2,1)} %copy-done.10) | copy-start | bytes 884740
  68.1 16.5 %copy-start.15 = (bf16[128,384]{1,0:T(8,128)(2,1)S(1)}, bf16[128,384]{1,0:T(8,128)(2,1)}, u32[]{:S(2)}) copy-start(bf16[128,384]{1,0:T(8,128)(2,1)} %copy-done.14) | copy-start | bytes 294916
  68.1 21.6 %collective-permute-start = (bf16[7680,128]{1,0:T(8,128)(2,1)}, bf16[7680,128]{1,0:T(8,128)(2,1)}, u32[]{:S(2)}, u32[]{:S(2)}) collective-permute-start(bf16[7680,128]{1,0:T(8,128)(2,1)} %get-tuple-element.35), channel_id=1, source_target_pairs={{0,8},{8,0},{1,9},{9,1},{2,10},{10,2},{3,11},{11,3},{4,12},{12,4},... | collective-permute-start | bytes 5898248 | tf_op jit(solution)/shard_map/ppermute | solution.py:520
  87.3 2.3 %collective-permute-start.1 = (bf16[2304,128]{1,0:T(8,128)(2,1)S(1)}, bf16[2304,128]{1,0:T(8,128)(2,1)S(1)}, u32[]{:S(2)}, u32[]{:S(2)}) collective-permute-start(bf16[2304,128]{1,0:T(8,128)(2,1)S(1)} %get-tuple-element.37), channel_id=1, source_target_pairs={{0,8},{8,0},{1,9},{9,1},{2,10},{10,2},{3,11},{11,3},{4,12},{12,4},... | collective-permute-start | bytes 1769480 | tf_op jit(solution)/shard_map/ppermute | solution.py:525
  89.7 1.5 copy-start.1
  173.1 16.7 %collective-permute-start.2 = (bf16[10240,128]{1,0:T(8,128)(2,1)S(1)}, bf16[10240,128]{1,0:T(8,128)(2,1)}, u32[]{:S(2)}, u32[]{:S(2)}) collective-permute-start(bf16[10240,128]{1,0:T(8,128)(2,1)S(1)} %bitcast.30), channel_id=1, source_target_pairs={{0,8},{8,0},{1,9},{9,1},{2,10},{10,2},{3,11},{11,3},{4,12},{12,4},... | collective-permute-start | bytes 7864328 | tf_op jit(solution)/shard_map/ppermute | solution.py:537

commit v3 on v2

--- a/solution.py
+++ b/solution.py
@@ -22,7 +22,7 @@
 BF16 = jnp.bfloat16
 EVERYONE = ("line", "core", "res")
 SHARERS = 64
-GAIN_LANE = 6 * POINTS - 256
+GAIN_ROW = 6 * POINTS
 
 PIECES = {
     "up": (C, HID),
@@ -76,7 +76,46 @@
     return put
 
 
-PARAMS = pltpu.CompilerParams(vmem_limit_bytes=48 * 1024 * 1024)
+def staged(core, stage_ref, keep_ref, give_ref, sems):
+    waits = []
+
+    def put(name, value):
+        tiles = value.shape[1] // 128
+        spans = {}
+        for unit, (half, at) in enumerate(UNITS[name]):
+            down, across = (unit // tiles) * C, (unit % tiles) * 128
+            stage_ref[half, at : at + C, :] = value[down : down + C, across : across + 128].astype(
+                BF16
+            )
+            low, _ = spans.get(half, (at, at))
+            spans[half] = (low, at + C)
+        for half, (low, high) in spans.items():
+            sem = sems.at[len(waits)]
+            source = stage_ref.at[half, low:high]
+
+            @pl.when(core == half)
+            def keep(source=source, low=low, high=high, sem=sem):
+                pltpu.make_async_copy(source, keep_ref.at[low:high], sem).start()
+
+            @pl.when(core != half)
+            def give(source=source, low=low, high=high, sem=sem):
+                pltpu.make_async_copy(source, give_ref.at[low:high], sem).start()
+
+            waits.append(pltpu.make_async_copy(source, keep_ref.at[low:high], sem))
+
+    return put, waits
+
+
+MEGA = 1024 * 1024
+
+
+def limit(megabytes):
+    return pltpu.CompilerParams(vmem_limit_bytes=megabytes * MEGA)
+
+
+SMEM = pl.BlockSpec(memory_space=pltpu.SMEM)
+VMEM = pl.BlockSpec(memory_space=pltpu.VMEM)
+HBM = pl.BlockSpec(memory_space=pltpu.HBM)
 
 
 def mm(left, right):
@@ -117,6 +156,12 @@
     return high, middle, (rest - middle.astype(F32)).astype(BF16)
 
 
+def order_matrix():
+    row = lax.broadcasted_iota(jnp.int32, (N, N), 0)
+    col = lax.broadcasted_iota(jnp.int32, (N, N), 1)
+    return jnp.where((col // 8 == row % 16) & (col % 8 == row // 16), 1.0, 0.0).astype(BF16)
+
+
 def tile_masks():
     lane = lax.broadcasted_iota(jnp.int32, (1, 128), 1)
     return [jnp.where(lane // 32 == m, 1.0, 0.0).astype(BF16) for m in range(4)]
@@ -124,6 +169,22 @@
 
 def masked_stack(tile, masks):
     return jnp.concatenate([tile * mask for mask in masks], axis=0)
+
+
+def pack_rows(tokens_ref, cotangent_ref, rigid_ref, packed_ref):
+    frames, residues, _ = tokens_ref.shape
+    order = order_matrix()
+    for at, ref in ((0, tokens_ref), (C, cotangent_ref)):
+        turned = tm(order, ref[...].reshape(N, C))
+        packed_ref[:, :, at : at + C] = turned.reshape(residues, frames, C).astype(BF16)
+    row = lax.broadcasted_iota(jnp.int32, (N, residues), 0)
+    col = lax.broadcasted_iota(jnp.int32, (N, residues), 1)
+    rigid = jnp.zeros((N, 12), F32)
+    for f in range(frames):
+        pick = jnp.where(row == col * frames + f, 1.0, 0.0).astype(BF16)
+        rigid = rigid + mt(pick, rigid_ref[:, f, :])
+    packed_ref[:, :, 2 * C :] = jnp.zeros((residues, frames, 128), BF16)
+    packed_ref[:, :, 2 * C : 2 * C + 12] = rigid.reshape(residues, frames, 12).astype(BF16)
 
 
 def time_forward(
@@ -145,21 +206,41 @@
             shares_ref[:, h * 128 : (h + 1) * 128] = shares.astype(BF16)
         mixed = mm(shares_ref[:, g * 512 : (g + 1) * 512], masked_stack(v, masks))
         mix_ref[:, g * 128 : (g + 1) * 128] = mixed.astype(BF16)
-    sent_ref[:, 0:C] = (x + mm(mix_ref[...], wout_ref[...])).astype(BF16)
-    sent_ref[:, C : C + 512] = rows_ref[:, C : C + 512]
+    x1 = (x + mm(mix_ref[...], wout_ref[...])).astype(BF16)
     lane = lax.broadcasted_iota(jnp.int32, (N, 128), 1)
     count = jnp.zeros((N, 128), F32)
     for n in range(NB):
         count = count + jnp.where(lane == neighbors_ref[place_ref[0], n], 1.0, 0.0)
-    sent_ref[:, C + 512 : C + 640] = count.astype(BF16)
+    sent = jnp.concatenate([x1, rows_ref[:, C:], count.astype(BF16)], axis=1)
+    sent_ref[...] = sent.reshape(N, 8, 128)
 
 
 def time_backward(
     core_ref, back_ref, rows_ref, qkv_ref, shares_ref, mix_ref, wqkv_ref, wout_ref,
-    sent_ref, keep_ref, give_ref, dqkv_ref, dcol_ref, pcol_ref,
+    keep_early_ref, got_early_ref,
+    sent_ref, keep_ref, give_ref, total_ref,
+    dqkv_ref, dcol_ref, pcol_ref, early_ref, got_ref, sems,
 ):
+    part = EARLY // 3
+    spans = [slice(g * part, (g + 1) * part) for g in range(3)]
+    arriving = []
+    for g, span in enumerate(spans):
+        arriving.append(
+            (
+                pltpu.make_async_copy(keep_early_ref.at[span], early_ref.at[span], sems.at[3 * g]),
+                pltpu.make_async_copy(got_early_ref.at[span], got_ref.at[span], sems.at[3 * g + 1]),
+            )
+        )
+    for pair in arriving:
+        for copy in pair:
+            copy.start()
+    leaving = [
+        pltpu.make_async_copy(early_ref.at[span], total_ref.at[span], sems.at[3 * g + 2])
+        for g, span in enumerate(spans)
+    ]
     put = halves(core_ref[0], keep_ref, give_ref)
-    dx1 = back_ref[:, 0:C]
+    back = back_ref[...].reshape(N, 1024)
+    dx1 = back[:, 0:C]
     normed, inverse = norm(rows_ref[:, 0:C].astype(F32))
     dmix = mt(dx1, wout_ref[...]).astype(BF16)
     put("time_out", tm(mix_ref[...], dx1))
@@ -186,11 +267,18 @@
         dqkv_ref[:, g * 128 : (g + 1) * 128] = dq.astype(BF16)
         dqkv_ref[:, C + g * 128 : C + (g + 1) * 128] = dk.astype(BF16)
         dqkv_ref[:, 2 * C + g * 128 : 2 * C + (g + 1) * 128] = dv.astype(BF16)
+        for copy in arriving[g]:
+            copy.wait()
+        summed = early_ref[spans[g], :].astype(F32) + got_ref[spans[g], :].astype(F32)
+        early_ref[spans[g], :] = summed.astype(BF16)
+        leaving[g].start()
     put("time_qkv", tm(normed.astype(BF16), dqkv_ref[...]))
     dnormed = mt(dqkv_ref[...], wqkv_ref[...]).astype(BF16).astype(F32)
     pulled = norm_pull(dnormed, normed, inverse).astype(BF16).astype(F32)
     sent_ref[:, 0:C] = (dx1.astype(F32) + pulled).astype(BF16)
-    sent_ref[:, C : 2 * C] = back_ref[:, C : 2 * C]
+    sent_ref[:, C : 2 * C] = back[:, C : 2 * C]
+    for copy in leaving:
+        copy.wait()
 
 
 def selectors():
@@ -216,23 +304,50 @@
 
 
 def point_attention(
-    core_ref, weight_ref, rows_ref, wqkv_ref, wpts_ref, wrep_ref, wout_ref, wup_ref, wdown_ref,
-    heads_ref, turn_ref, spread_ref, gather_ref,
-    back_ref, keep_ref, give_ref,
-    qkv_ref, mix_ref, shares_ref, point_ref, prow_ref, pcol_ref, drow_ref, dcol_ref,
-    dqkv_ref, dlocal_ref, keys_ref, queries_ref, side_ref,
+    core_ref, weight_ref, rows_ref, *refs
 ):
-    put = halves(core_ref[0], keep_ref, give_ref)
-    for ref in (keep_ref, give_ref):
-        ref[EARLY - C : EARLY, :] = jnp.zeros((C, 128), BF16)
+    sources, refs = refs[:10], refs[10:]
+    back_ref, keep_ref, give_ref = refs[:3]
+    (
+        qkv_ref, mix_ref, shares_ref, point_ref, prow_ref, pcol_ref, drow_ref, dcol_ref,
+        dqkv_ref, dlocal_ref, keys_ref, queries_ref, side_ref, stage_ref,
+    ) = refs[3:17]
+    held, sems, out_sems = refs[17:27], refs[27], refs[28]
+    fetched = [
+        pltpu.make_async_copy(source, target, sems.at[k])
+        for k, (source, target) in enumerate(zip(sources, held))
+    ]
+    for copy in fetched:
+        copy.start()
+    (
+        wqkv_ref, turn_ref, wrep_ref, heads_ref, wout_ref, wup_ref, wdown_ref, spread_ref,
+        gather_ref, wpts_ref,
+    ) = held
+    put, leaving = staged(core_ref[0], stage_ref, keep_ref, give_ref, out_sems)
+    stage_ref[1, EARLY_UNITS[1] * C : EARLY, :] = jnp.zeros((EARLY - EARLY_UNITS[1] * C, 128), BF16)
+    spare = stage_ref.at[1, EARLY_UNITS[1] * C : EARLY]
+    spare_copy = pltpu.make_async_copy(
+        spare, keep_ref.at[EARLY_UNITS[1] * C : EARLY], out_sems.at[8]
+    )
+
+    @pl.when(core_ref[0] == 1)
+    def keep_spare():
+        spare_copy.start()
+
+    @pl.when(core_ref[0] != 1)
+    def give_spare():
+        pltpu.make_async_copy(
+            spare, give_ref.at[EARLY_UNITS[1] * C : EARLY], out_sems.at[8]
+        ).start()
+
     masks = tile_masks()
-    row = lax.broadcasted_iota(jnp.int32, (N, N), 0)
-    col = lax.broadcasted_iota(jnp.int32, (N, N), 1)
-    order = jnp.where((col // 8 == row % 16) & (col % 8 == row // 16), 1.0, 0.0).astype(BF16)
-    x1 = mm(order, rows_ref[:, 0:C])
-    side_ref[...] = mm(order, rows_ref[:, C : C + 640]).astype(BF16)
+    order = order_matrix()
+    rows = mm(order, rows_ref[...].reshape(N, 1024))
+    x1 = rows[:, 0:C]
+    side_ref[...] = rows[:, C:].astype(BF16)
     normed, inverse = norm(x1)
     n2 = normed.astype(BF16)
+    fetched[0].wait()
     qkv_ref[...] = mm(n2, wqkv_ref[...]).astype(BF16)
 
     lane = lax.broadcasted_iota(jnp.int32, (1, 256), 1)
@@ -244,9 +359,11 @@
     strength = jnp.where(lane < 3 * POINTS, soft * STRENGTH, 0.0)
     head_masks = [jnp.where(lane_head == h, 1.0, 0.0).astype(BF16) for h in range(H)]
 
+    for copy in fetched[1:4]:
+        copy.wait()
     turned = mm(side_ref[:, C : C + 128], turn_ref[...])
     turns = [turned[:, b * 256 : (b + 1) * 256] for b in range(3)]
-    local = mm(n2, wrep_ref[...])
+    local = mt(n2, wrep_ref[...])
     placed = []
     for c in range(2):
         total = turned[:, 768:1024]
@@ -291,6 +408,8 @@
         mixed = mm(prow_ref[:, g * 512 : (g + 1) * 512], masked_stack(v, masks))
         mix_ref[:, g * 128 : (g + 1) * 128] = mixed.astype(BF16)
 
+    for copy in fetched[4:7]:
+        copy.wait()
     cot = side_ref[:, 0:C]
     x2 = (x1 + mm(mix_ref[...], wout_ref[...])).astype(BF16).astype(F32)
     normed2, inverse2 = norm(x2)
@@ -303,7 +422,6 @@
         1.0 + 3.0 * 0.044715 * u * u
     )
     updated = (x2 + mm(hidden, wdown_ref[...])).astype(BF16)
-    back_ref[:, C : 2 * C] = tm(order, updated).astype(BF16)
     put("down", tm(hidden, cot))
     dhidden = mt(cot, wdown_ref[...]).astype(BF16).astype(F32)
     du = (dhidden * slope).astype(BF16)
@@ -342,12 +460,14 @@
     gain = jnp.zeros((1, 128), F32)
     raw_row = jnp.zeros((1, 128), F32)
     for h in range(H):
-        here = lane128 == GAIN_LANE + h
+        here = lane128 == h
         gain = jnp.where(here, jnp.sum(gains[h], axis=1, keepdims=True), gain)
         raw_row = jnp.where(here, weight_ref[h], raw_row)
     soft_row = jnp.maximum(raw_row, 0.0) + jnp.log(1.0 + jnp.exp(-jnp.abs(raw_row)))
     gain = gain / ((1.0 + jnp.exp(-raw_row)) * soft_row)
 
+    for copy in fetched[7:10]:
+        copy.wait()
     from_keys = mm(drow_ref[...], keys_ref[...])
     from_queries = tm(dcol_ref[...], queries_ref[...])
     spread = spread_ref[...]
@@ -361,53 +481,72 @@
     dpoints = mm(dlocal_ref[...], gather_ref[...]).astype(BF16)
     dqkv = dqkv_ref[...]
     put("ipa_qkv", tm(n2, dqkv))
-    gpts = tm(n2, dpoints)
-    first = lax.broadcasted_iota(jnp.int32, (C, 128), 0) == 0
-    last = gpts[:, 256:384] + jnp.where(first, gain, 0.0)
-    put("ipa_points", jnp.concatenate([gpts[:, 0:256], last], axis=1))
-    dn2 = (mt(dqkv, wqkv_ref[...]) + mt(dpoints[:, 0 : 6 * POINTS], wpts_ref[...])).astype(BF16).astype(F32)
+    gpts = tm(dpoints, n2)
+    spare_row = lax.broadcasted_iota(jnp.int32, (C, 128), 0) == GAIN_ROW
+    first = gpts[:, 0:128] + jnp.where(spare_row, gain, 0.0)
+    put("ipa_points", jnp.concatenate([first, gpts[:, 128:]], axis=1))
+    dn2 = (mt(dqkv, wqkv_ref[...]) + mm(dpoints[:, 0 : 6 * POINTS], wpts_ref[...])).astype(BF16).astype(F32)
     dx1 = (dx2.astype(F32) + norm_pull(dn2, normed, inverse).astype(BF16).astype(F32)).astype(BF16)
-    back_ref[:, 0:C] = tm(order, dx1).astype(BF16)
+    back = jnp.concatenate([dx1, updated, jnp.zeros((N, 256), BF16)], axis=1)
+    back_ref[...] = tm(order, back).astype(BF16).reshape(N, 8, 128)
+    for copy in leaving + [spare_copy]:
+        copy.wait()
 
 
 def like(shape, dtype):
     return jax.ShapeDtypeStruct(shape, dtype)
 
 
+def call_pack_rows(tokens, cotangent, rigid):
+    frames, residues, _ = tokens.shape
+    return pl.pallas_call(
+        pack_rows,
+        out_shape=like((residues, frames, 2 * C + 128), BF16),
+        compiler_params=limit(60),
+        name="pack_rows",
+    )(tokens, cotangent, rigid)
+
+
 def call_time_forward(place, neighbors, rows, w_qkv, w_out):
-    smem, vmem = pl.BlockSpec(memory_space=pltpu.SMEM), pl.BlockSpec(memory_space=pltpu.VMEM)
     return pl.pallas_call(
         time_forward,
-        in_specs=[smem, smem, vmem, vmem, vmem],
+        in_specs=[SMEM, SMEM, VMEM, VMEM, VMEM],
         out_shape=(
-            like((N, 1024), BF16), like((N, 3 * C), BF16), like((N, H * N), BF16),
+            like((N, 8, 128), BF16), like((N, 3 * C), BF16), like((N, H * N), BF16),
             like((N, C), BF16),
         ),
-        compiler_params=PARAMS,
+        compiler_params=limit(60),
         name="time_forward",
     )(place, neighbors, rows, w_qkv, w_out)
 
 
-def call_time_backward(core, back, rows, qkv, shares, mix, w_qkv, w_out):
-    smem, vmem = pl.BlockSpec(memory_space=pltpu.SMEM), pl.BlockSpec(memory_space=pltpu.VMEM)
+def call_time_backward(core, back, rows, qkv, shares, mix, w_qkv, w_out, keep_early, got_early):
     return pl.pallas_call(
         time_backward,
-        in_specs=[smem] + [vmem] * 7,
-        out_shape=(like((N, 2 * C), BF16), like((LATE, 128), BF16), like((LATE, 128), BF16)),
+        in_specs=[SMEM] + [VMEM] * 7 + [HBM] * 2,
+        out_specs=(VMEM, VMEM, VMEM, HBM),
+        out_shape=(
+            like((N, 2 * C), BF16), like((LATE, 128), BF16), like((LATE, 128), BF16),
+            like((HALF, 128), BF16),
+        ),
         scratch_shapes=[
             pltpu.VMEM((N, 3 * C), BF16), pltpu.VMEM((4 * N, N), BF16), pltpu.VMEM((4 * N, N), BF16),
+            pltpu.VMEM((EARLY, 128), BF16), pltpu.VMEM((EARLY, 128), BF16),
+            pltpu.SemaphoreType.DMA((9,)),
         ],
-        compiler_params=PARAMS,
+        compiler_params=limit(20),
         name="time_backward",
-    )(core, back, rows, qkv, shares, mix, w_qkv, w_out)
+    )(core, back, rows, qkv, shares, mix, w_qkv, w_out, keep_early, got_early)
 
 
 def call_point_attention(core, weight, rows, w_qkv, w_pts, w_rep, w_out, w_up, w_down):
-    smem, vmem = pl.BlockSpec(memory_space=pltpu.SMEM), pl.BlockSpec(memory_space=pltpu.VMEM)
+    heads, turn, spread, gather = selectors()
+    sources = [w_qkv, turn, w_rep, heads, w_out, w_up, w_down, spread, gather, w_pts]
     return pl.pallas_call(
         point_attention,
-        in_specs=[smem, smem] + [vmem] * 11,
-        out_shape=(like((N, 2 * C), BF16), like((EARLY, 128), BF16), like((EARLY, 128), BF16)),
+        in_specs=[SMEM, SMEM, VMEM] + [HBM] * len(sources),
+        out_specs=(VMEM, HBM, HBM),
+        out_shape=(like((N, 8, 128), BF16), like((EARLY, 128), BF16), like((EARLY, 128), BF16)),
         scratch_shapes=[
             pltpu.VMEM((N, 3 * C), BF16), pltpu.VMEM((N, C), BF16),
             pltpu.VMEM((N, H * N), F32), pltpu.VMEM((N, H * N), F32),
@@ -415,25 +554,35 @@
             pltpu.VMEM((N, H * N), BF16), pltpu.VMEM((H * N, N), BF16),
             pltpu.VMEM((N, 3 * C), BF16), pltpu.VMEM((N, 6 * 256), BF16),
             pltpu.VMEM((H * N, 256), BF16), pltpu.VMEM((H * N, 256), BF16),
-            pltpu.VMEM((N, 640), BF16),
+            pltpu.VMEM((N, 640), BF16), pltpu.VMEM((2, EARLY, 128), BF16),
+            *[pltpu.VMEM(source.shape, BF16) for source in sources],
+            pltpu.SemaphoreType.DMA((len(sources),)), pltpu.SemaphoreType.DMA((9,)),
         ],
-        compiler_params=PARAMS,
+        compiler_params=limit(60),
         name="point_attention",
-    )(core, weight, rows, w_qkv, w_pts, w_rep, w_out, w_up, w_down, *selectors())
-
-
-def add_halves(keep_early_ref, got_early_ref, keep_late_ref, got_late_ref, total_ref):
-    early = keep_early_ref[...].astype(F32) + got_early_ref[...].astype(F32)
-    total_ref[0:EARLY, :] = early.astype(BF16)
-    late = keep_late_ref[...].astype(F32) + got_late_ref[...].astype(F32)
-    total_ref[EARLY : EARLY + LATE, :] = late.astype(BF16)
-    total_ref[EARLY + LATE :, :] = jnp.zeros((HALF - EARLY - LATE, 128), BF16)
-
-
-def call_add_halves(*parts):
+    )(core, weight, rows, *sources)
+
+
+def add_late(total_in_ref, keep_ref, got_ref, total_ref, late_ref, sem):
+    late = keep_ref[...].astype(F32) + got_ref[...].astype(F32)
+    late_ref[0:LATE, :] = late.astype(BF16)
+    late_ref[LATE:, :] = jnp.zeros((HALF - EARLY - LATE, 128), BF16)
+    copy = pltpu.make_async_copy(late_ref, total_ref.at[EARLY:HALF], sem)
+    copy.start()
+    copy.wait()
+
+
+def call_add_late(total, keep, got):
     return pl.pallas_call(
-        add_halves, out_shape=like((HALF, 128), BF16), compiler_params=PARAMS, name="add_halves"
-    )(*parts)
+        add_late,
+        in_specs=[HBM, VMEM, VMEM],
+        out_specs=HBM,
+        out_shape=like((HALF, 128), BF16),
+        scratch_shapes=[pltpu.VMEM((HALF - EARLY, 128), BF16), pltpu.SemaphoreType.DMA],
+        input_output_aliases={0: 0},
+        compiler_params=limit(8),
+        name="add_late",
+    )(total, keep, got)
 
 
 def add_parts(parts_ref, copies_ref):
@@ -448,54 +597,75 @@
 
 def call_add_parts(parts):
     return pl.pallas_call(
-        add_parts, out_shape=like(parts.shape, BF16), compiler_params=PARAMS, name="add_parts"
+        add_parts, out_shape=like(parts.shape, BF16), compiler_params=limit(12), name="add_parts"
     )(parts)
 
 
-def unpack(core_ref, mine_ref, other_ref, *out_refs):
-    outs = dict(zip(PIECES, out_refs))
-    gain_ref = out_refs[-1]
-
-    def read(halves_refs):
-        for name, (rows, columns) in PIECES.items():
-            for unit, (half, at) in enumerate(UNITS[name]):
-                value = halves_refs[half][at : at + C, :].astype(F32)
-                tiles = columns // 128
-                down, across = (unit // tiles) * C, (unit % tiles) * 128
-                if name == "ipa_points" and across == 256:
-                    outs[name][down : down + C, across:] = value[:, : 6 * POINTS - 256]
-                    gain_ref[...] = value[0:1, :]
-                else:
-                    outs[name][down : down + C, across : across + 128] = value
-
-    @pl.when(core_ref[0] == 0)
-    def first():
-        read((mine_ref, other_ref))
-
-    @pl.when(core_ref[0] != 0)
-    def second():
-        read((other_ref, mine_ref))
-
-
-def call_unpack(core, mine, other):
-    smem, vmem = pl.BlockSpec(memory_space=pltpu.SMEM), pl.BlockSpec(memory_space=pltpu.VMEM)
+def unpack(core_ref, mine_ref, other_ref, ended_ref, *refs):
+    out_refs, gain_ref, output_ref, token_ref = refs[:7], refs[7], refs[8], refs[9]
+    half_ref, stages, in_sems, out_sems = refs[10], refs[11:18], refs[18], refs[19]
+    core = core_ref[0]
+    mine = pltpu.make_async_copy(mine_ref, half_ref.at[core], in_sems.at[0])
+    other = pltpu.make_async_copy(other_ref, half_ref.at[1 - core], in_sems.at[1])
+    mine.start()
+    other.start()
+    residues, frames, _ = ended_ref.shape
+    ended = mm(order_matrix(), ended_ref[...].reshape(N, 2 * C)).astype(BF16)
+    token_ref[...] = ended[:, 0:C].reshape(frames, residues, C)
+    output_ref[...] = ended[:, C:].reshape(frames, residues, C)
+    mine.wait()
+    other.wait()
+    leaving = []
+    for k, (name, (rows, columns)) in enumerate(PIECES.items()):
+        tiles = columns // 128
+        for unit, (half, at) in enumerate(UNITS[name]):
+            down, across = (unit // tiles) * C, (unit % tiles) * 128
+            value = half_ref[half, at : at + C, :].astype(F32)
+            if name == "ipa_points":
+                stages[k][:, across : across + 128] = value[0:GAIN_ROW]
+                if across == 0:
+                    gain = value[GAIN_ROW : GAIN_ROW + 1, :]
+            else:
+                stages[k][down : down + C, across : across + 128] = value
+        leaving.append(pltpu.make_async_copy(stages[k], out_refs[k], out_sems.at[k]))
+        leaving[-1].start()
+    lane = lax.broadcasted_iota(jnp.int32, (1, 128), 1)
+    for h in range(H):
+        gain_ref[h] = jnp.sum(jnp.where(lane == h, gain, 0.0))
+    for copy in leaving:
+        copy.wait()
+
+
+def call_unpack(core, mine, other, ended):
+    residues, frames, _ = ended.shape
     shapes = [
-        like((rows, 6 * POINTS if name == "ipa_points" else columns), F32)
+        (GAIN_ROW if name == "ipa_points" else rows, columns)
         for name, (rows, columns) in PIECES.items()
     ]
+    rows = like((frames, residues, C), BF16)
     return pl.pallas_call(
         unpack,
-        in_specs=[smem, vmem, vmem],
-        out_shape=(*shapes, like((1, 128), F32)),
-        compiler_params=PARAMS,
+        in_specs=[SMEM, HBM, HBM, VMEM],
+        out_specs=(*[HBM] * 7, SMEM, VMEM, VMEM),
+        out_shape=(*[like(shape, F32) for shape in shapes], like((H,), F32), rows, rows),
+        scratch_shapes=[
+            pltpu.VMEM((2, HALF, 128), BF16),
+            *[pltpu.VMEM(shape, F32) for shape in shapes],
+            pltpu.SemaphoreType.DMA((2,)), pltpu.SemaphoreType.DMA((7,)),
+        ],
+        compiler_params=limit(24),
         name="unpack",
-    )(core, mine, other)
+    )(core, mine, other, ended)
 
 
 def repeat_points(weight):
-    parts = weight.reshape(C, 6, POINTS)
-    tripled = jnp.concatenate([parts, parts, parts], axis=2)
-    return jnp.pad(tripled, ((0, 0), (0, 0), (0, 256 - 3 * POINTS))).reshape(C, 6 * 256)
+    parts = weight.reshape(6, POINTS, C)
+    tripled = jnp.concatenate([parts, parts, parts], axis=1)
+    return jnp.pad(tripled, ((0, 0), (0, 256 - 3 * POINTS), (0, 0))).reshape(6 * 256, C)
+
+
+def swap_rows(rows, axes):
+    return lax.all_to_all(rows, axes, split_axis=0, concat_axis=0, tiled=True)
 
 
 def body(
@@ -505,42 +675,31 @@
     frames, residues = tokens.shape[:2]
     place = lax.axis_index(("line", "core")).astype(jnp.int32).reshape(1)
     core = lax.axis_index("core").astype(jnp.int32).reshape(1)
-    rigid = jnp.pad(jnp.transpose(rigid_frames, (1, 2, 0)), ((0, 0), (0, 0), (0, 116)))
-    rows = lax.all_to_all(
-        jnp.concatenate([tokens, cotangent, rigid], axis=2),
-        ("line", "core"), split_axis=1, concat_axis=0, tiled=True,
-    ).reshape(N, 2 * C + 128)
+    swap = [(0, 1), (1, 0)]
+    points = w_ipa_points.T
+    rows = swap_rows(call_pack_rows(tokens, cotangent, rigid_frames), ("line", "core"))
+    rows = rows.reshape(N, 2 * C + 128)
     sent, qkv, shares, mix = call_time_forward(place, neighbors, rows, w_time_qkv, w_time_out)
-    moved = lax.all_to_all(sent, EVERYONE, split_axis=0, concat_axis=0, tiled=True)
     back, keep_early, give_early = call_point_attention(
-        core, point_weight, moved, w_ipa_qkv, w_ipa_points, repeat_points(w_ipa_points), w_ipa_out,
-        w_up, w_down,
-    )
-    swap = [(0, 1), (1, 0)]
+        core, point_weight, swap_rows(sent, EVERYONE), w_ipa_qkv, points, repeat_points(points),
+        w_ipa_out, w_up, w_down,
+    )
     got_early = lax.ppermute(give_early, "core", swap)
-    back = lax.all_to_all(back, EVERYONE, split_axis=0, concat_axis=0, tiled=True)
-    ended, keep_late, give_late = call_time_backward(
-        core, back, rows, qkv, shares, mix, w_time_qkv, w_time_out
+    ended, keep_late, give_late, total = call_time_backward(
+        core, swap_rows(back, EVERYONE), rows, qkv, shares, mix, w_time_qkv, w_time_out,
+        keep_early, got_early,
     )
     got_late = lax.ppermute(give_late, "core", swap)
-    ended = lax.all_to_all(
-        ended.reshape(N, 1, 2 * C), ("line", "core"), split_axis=0, concat_axis=1, tiled=True
-    )
-    packed = call_add_halves(keep_early, got_early, keep_late, got_late)
-    parts = lax.all_to_all(
-        packed.reshape(SHARERS, HALF // SHARERS, 128), ("line", "res"), split_axis=0, concat_axis=0,
-        tiled=True,
-    )
-    mine = lax.all_to_all(
-        call_add_parts(parts), ("line", "res"), split_axis=0, concat_axis=0, tiled=True
-    ).reshape(HALF, 128)
+    total = call_add_late(total, keep_late, got_late)
+    parts = swap_rows(total.reshape(SHARERS, HALF // SHARERS, 128), ("line", "res"))
+    mine = swap_rows(call_add_parts(parts), ("line", "res")).reshape(HALF, 128)
     other = lax.ppermute(mine, "core", swap)
-    *grads, gain = call_unpack(core, mine, other)
+    ended = swap_rows(ended.reshape(residues, frames, 2 * C), ("line", "core"))
+    *grads, gain, output, token_grad = call_unpack(core, mine, other, ended)
     grads = dict(zip(PIECES, grads))
     return (
-        ended[:, :, C:], ended[:, :, :C], grads["time_qkv"], grads["time_out"], grads["ipa_qkv"],
-        grads["ipa_points"], gain[0, GAIN_LANE : GAIN_LANE + H], grads["ipa_out"], grads["up"],
-        grads["down"],
+        output, token_grad, grads["time_qkv"], grads["time_out"], grads["ipa_qkv"],
+        grads["ipa_points"].T, gain, grads["ipa_out"], grads["up"], grads["down"],
     )
 
 

time: 199 us -> 180 us (0.905)
  local copies, waits for them, and re-layouts: 23.2 us -> 2.96 us
  other arithmetic: 4.99 us -> 1.12 us
  waiting for transfers between devices: 17.7 us -> 20 us
  Pallas kernels: 28.2 us -> 30.3 us
  blocking collectives: 103 us -> 105 us
    unnamed x58 -> x20, local copies, waits for them, and re-layouts: 20.4 us -> 2.96 us
    all_to_all x2 -> x0, other arithmetic: 2.43 us -> none  [the longest x1 1.65 us: body(): lax.all_to_all(back, EVERYONE, split_axis=0, concat_axis=0, tiled=True)]
    all_to_all x4, blocking collectives: 103 us -> 105 us  [swap_rows(): return lax.all_to_all(rows, axes, split_axis=0, concat_axis=0, tiled=True)]
    all_to_all x2, waiting for transfers between devices: 16.1 us -> 18.4 us  [swap_rows(): return lax.all_to_all(rows, axes, split_axis=0, concat_axis=0, tiled=True)]
    pallas_call x5 -> x6, Pallas kernels: 27.7 us -> 29.9 us  [the longest x1 12.4 us: call_point_attention(): pl.pallas_call(point_attention, in_specs=[SMEM, SMEM, VMEM] + [HBM] * len...]
  transfers between devices with their start and end apart: 5 -> 5, of which waited for: 3 -> 3; matrix products, arithmetic and copies ran while one was open for 4% -> 1% of each run, Pallas kernels for 1% -> 0%
where the time goes in v3:
time: 180 us; the launch traced here: 179 us
  blocking collectives  105 us (58%)
  Pallas kernels  30.3 us (17%)
  waiting for transfers between devices  20 us (11%)
  starting transfers between devices  18.9 us (10%)
  local copies, waits for them, and re-layouts  2.96 us (2%)
    all_to_all x4, blocking collectives, swap_rows(): return lax.all_to_all(rows, axes, split_axis=0, concat_axis=0, tiled=True)  105 us
    all_to_all x2, waiting for transfers between devices, swap_rows(): return lax.all_to_all(rows, axes, split_axis=0, concat_axis=0, tiled=True)  18.4 us
    all_to_all x2, starting transfers between devices, swap_rows(): return lax.all_to_all(rows, axes, split_axis=0, concat_axis=0, tiled=True)  14.6 us
    pallas_call x1, Pallas kernels, call_point_attention(): pl.pallas_call(point_attention, in_specs=[SMEM, SMEM, VMEM] + [HBM] * len...  12.4 us
    pallas_call x1, Pallas kernels, call_time_backward(): pl.pallas_call(time_backward, in_specs=[SMEM] + [VMEM] * 7 + [HBM] * 2, o...  5.75 us
    pallas_call x1, Pallas kernels, call_unpack(): pl.pallas_call(unpack, in_specs=[SMEM, HBM, HBM, VMEM], out_specs=(*[HBM]...  5.37 us
    pallas_call x1, Pallas kernels, call_time_forward(): pl.pallas_call(time_forward, in_specs=[SMEM, SMEM, VMEM, VMEM, VMEM], out...  4.03 us
  transfers between devices with their start and end apart: 5, of which 3 were waited for; matrix products, arithmetic and copies ran while one was open for 1% of the time, Pallas kernels for 0%

profile of v3, /device:TPU:1, one launch (start us, length us, event | category | flops | bytes accessed | tf_op | source)
XLA Modules:
  0.0 179.5 jit_solution(8318282618130369044)
XLA Ops:
  0.6 0.0 copy-start.9
  0.7 2.0 %pack_rows.1 = bf16[16,8,896]{2,1,0:T(8,128)(2,1)} custom-call(bf16[8,16,384]{2,1,0:T(8,128)(2,1)} %tokens_ref.1, bf16[8,16,384]{2,1,0:T(8,128)(2,1)} %cotangent_ref.1, bf16[12,8,16]{2,1,0:T(8,128)(2,1)} %rigid_ref.1), custom_call_target="tpu_custom_call" | custom-call | tf_op jit(solution)/shard_map/pack_rows/pallas_call | solution.py:502
  2.6 9.5 %all-to-all-start = ((bf16[16,8,896]{2,1,0:T(8,128)(2,1)}), bf16[16,8,896]{2,1,0:T(8,128)(2,1)S(1)}, u32[]{:S(2)}, u32[]{:S(2)}) async-start(bf16[16,8,896]{2,1,0:T(8,128)(2,1)} %pack_rows.1), calls=%async_computation | async-start | bytes 458752 | tf_op jit(solution)/shard_map/all_to_all | solution.py:668
  12.1 8.4 %all-to-all-done = bf16[16,8,896]{2,1,0:T(8,128)(2,1)S(1)} async-done(((bf16[16,8,896]{2,1,0:T(8,128)(2,1)}), bf16[16,8,896]{2,1,0:T(8,128)(2,1)S(1)}, u32[]{:S(2)}, u32[]{:S(2)}) %all-to-all-start) | async-done | bytes 229408 | tf_op jit(solution)/shard_map/all_to_all | solution.py:668
  20.5 0.0 copy-start.1
  20.5 0.7 copy-done.1
  21.2 4.0 %time_forward.1 = (bf16[128,8,128]{2,1,0:T(8,128)(2,1)}, bf16[128,1152]{1,0:T(8,128)(2,1)}, bf16[128,1536]{1,0:T(8,128)(2,1)}, bf16[128,384]{1,0:T(8,128)(2,1)}) custom-call(s32[1]{0:T(128)} %bitcast.1.place_ref, s32[16,32]{1,0:T(8,128)} %neighbors_ref.1, bf16[128,896]{1,0:T(8,128)(2,1)} %bitcast.14, bf16[384,1152]{1,0:T(8,128)(2,1)} %wqkv_ref.3, ...), custom_call_target="tpu_custom_call" | custom-call | tf_op jit(solution)/shard_map/time_forward/pallas_call | solution.py:511
  25.3 5.1 %all-to-all-start.1 = ((bf16[128,8,128]{2,1,0:T(8,128)(2,1)}), bf16[128,8,128]{2,1,0:T(8,128)(2,1)S(1)}, u32[]{:S(2)}, u32[]{:S(2)}) async-start(bf16[128,8,128]{2,1,0:T(8,128)(2,1)} %get-tuple-element.31), calls=%async_computation.1 | async-start | bytes 524288 | tf_op jit(solution)/shard_map/all_to_all | solution.py:668
  30.4 0.0 copy-done.9
  30.4 1.1 fusion.4
  31.5 9.9 %all-to-all-done.1.rows_ref = bf16[128,8,128]{2,1,0:T(8,128)(2,1)S(1)} async-done(((bf16[128,8,128]{2,1,0:T(8,128)(2,1)}), bf16[128,8,128]{2,1,0:T(8,128)(2,1)S(1)}, u32[]{:S(2)}, u32[]{:S(2)}) %all-to-all-start.1) | async-done | bytes 262176 | tf_op jit(solution)/shard_map/all_to_all | solution.py:668
  41.5 0.0 copy-start.8
  41.5 0.7 copy-done.8
  42.2 0.0 copy-start
  42.2 0.0 copy-start.2
  42.2 0.0 copy-start.4
  42.2 0.0 copy-start.5
  42.2 0.0 copy-start.6
  42.2 0.0 copy-start.7
  42.2 12.4 %point_attention.1 = (bf16[128,8,128]{2,1,0:T(8,128)(2,1)}, bf16[7680,128]{1,0:T(8,128)(2,1)}, bf16[7680,128]{1,0:T(8,128)(2,1)}) custom-call(s32[1]{0:T(128)} %bitcast.core_ref, f32[12]{0:T(128)} %weight_ref.1, bf16[128,8,128]{2,1,0:T(8,128)(2,1)} %copy-done.8, bf16[384,1152]{1,0:T(8,128)(2,1)} %refs_0_.1, bf16[128,1024]{1,0:T(8,128)(2,1)} %constant.25.clone.refs_1_, ...), custom_call_target="tpu_custom_call" | custom-call | tf_op jit(solution)/shard_map/point_attention/pallas_call | solution.py:545
  54.6 0.6 collective-permute-start
  55.1 14.8 %all_to_all.30.back_ref = bf16[128,8,128]{2,1,0:T(8,128)(2,1)S(1)} all-to-all(bf16[128,8,128]{2,1,0:T(8,128)(2,1)} %get-tuple-element.32), channel_id=1, replica_groups=mesh['line'=8,'core'=2,'res'=8] {'line','core','res'}, dimensions={0} | all-to-all | bytes 524288 | tf_op jit(solution)/shard_map/all_to_all | solution.py:668
  70.0 0.0 collective-permute-done.got_early_ref
  70.0 0.0 copy-done
  70.0 0.0 copy-done.2
  70.0 0.0 copy-done.4
  70.0 0.0 copy-done.5
  70.0 0.0 copy-done.6
  70.0 0.0 copy-done.7
  70.0 0.0 copy-start.3
  70.1 1.5 copy-done.3
  71.6 5.8 %time_backward.1 = (bf16[128,768]{1,0:T(8,128)(2,1)S(1)}, bf16[2304,128]{1,0:T(8,128)(2,1)S(1)}, bf16[2304,128]{1,0:T(8,128)(2,1)S(1)}, bf16[10240,128]{1,0:T(8,128)(2,1)S(1)}) custom-call(s32[1]{0:T(128)} %bitcast.core_ref, bf16[128,8,128]{2,1,0:T(8,128)(2,1)S(1)} %all_to_all.30.back_ref, bf16[128,896]{1,0:T(8,128)(2,1)S(1)} %bitcast.15, ...), custom_call_target="tpu_custom_call" | custom-call | tf_op jit(solution)/shard_map/time_backward/pallas_call | solution.py:524
  77.4 0.6 collective-permute-start.1
  77.9 1.6 collective-permute-done.1.got_ref
  79.6 0.4 add_late.1
  79.9 39.6 %all_to_all.31.parts_ref = bf16[64,160,128]{2,1,0:T(8,128)(2,1)S(1)} all-to-all(bf16[64,160,128]{2,1,0:T(8,128)(2,1)S(1)} %bitcast.11), channel_id=1, replica_groups=mesh['line'=8,'core'=2,'res'=8] {'line','res'}, dimensions={0} | all-to-all | bytes 5242880 | tf_op jit(solution)/shard_map/all_to_all | solution.py:668
  119.5 0.4 add_parts.1
  120.0 39.5 %all_to_all.32 = bf16[64,160,128]{2,1,0:T(8,128)(2,1)S(1)} all-to-all(bf16[64,160,128]{2,1,0:T(8,128)(2,1)S(1)} %add_parts.1), channel_id=1, replica_groups=mesh['line'=8,'core'=2,'res'=8] {'line','res'}, dimensions={0} | all-to-all | bytes 5242880 | tf_op jit(solution)/shard_map/all_to_all | solution.py:668
  159.5 3.2 %collective-permute-start.2 = (bf16[10240,128]{1,0:T(8,128)(2,1)S(1)}, bf16[10240,128]{1,0:T(8,128)(2,1)S(1)}, u32[]{:S(2)}, u32[]{:S(2)}) collective-permute-start(bf16[10240,128]{1,0:T(8,128)(2,1)S(1)} %bitcast.12), channel_id=1, source_target_pairs={{0,8},{8,0},{1,9},{9,1},{2,10},{10,2},{3,11},{11,3},{4,12},{12,4},... | collective-permute-start | bytes 7864328 | tf_op jit(solution)/shard_map/ppermute | solution.py:696
  162.7 11.3 %all_to_all.33.ended_ref = bf16[16,8,768]{2,1,0:T(8,128)(2,1)S(1)} all-to-all(bf16[16,8,768]{2,1,0:T(8,128)(2,1)S(1)} %bitcast.16), channel_id=1, replica_groups=mesh['line'=8,'core'=2,'res'=8] {'line','core'}, dimensions={0} | all-to-all | bytes 393216 | tf_op jit(solution)/shard_map/all_to_all | solution.py:668
  174.0 0.0 collective-permute-done.2.other_ref
  174.0 5.4 %unpack.1 = (f32[384,1536]{1,0:T(8,128)}, f32[384,384]{1,0:T(8,128)}, f32[288,384]{1,0:T(8,128)}, f32[384,1152]{1,0:T(8,128)}, f32[1536,384]{1,0:T(8,128)}, /*in...) custom-call(s32[1]{0:T(128)} %bitcast.core_ref, ...), custom_call_target="tpu_custom_call" | custom-call | tf_op jit(solution)/shard_map/unpack/pallas_call | solution.py:646
Async XLA Ops:
  0.6 29.8 %copy-start.9 = (bf16[384,288]{0,1:T(8,128)(2,1)S(1)}, bf16[384,288]{0,1:T(8,128)(2,1)}, u32[]{:S(2)}) copy-start(bf16[384,288]{0,1:T(8,128)(2,1)} %param.22) | copy-start | bytes 663556
  2.6 17.9 %all-to-all-start = ((bf16[16,8,896]{2,1,0:T(8,128)(2,1)}), bf16[16,8,896]{2,1,0:T(8,128)(2,1)S(1)}, u32[]{:S(2)}, u32[]{:S(2)}) async-start(bf16[16,8,896]{2,1,0:T(8,128)(2,1)} %pack_rows.1), calls=%async_computation | async-start | bytes 458752 | tf_op jit(solution)/shard_map/all_to_all | solution.py:668
  20.5 0.7 copy-start.1
  25.3 16.2 %all-to-all-start.1 = ((bf16[128,8,128]{2,1,0:T(8,128)(2,1)}), bf16[128,8,128]{2,1,0:T(8,128)(2,1)S(1)}, u32[]{:S(2)}, u32[]{:S(2)}) async-start(bf16[128,8,128]{2,1,0:T(8,128)(2,1)} %get-tuple-element.31), calls=%async_computation.1 | async-start | bytes 524288 | tf_op jit(solution)/shard_map/all_to_all | solution.py:668
  41.5 0.7 copy-start.8
  42.2 27.8 %copy-start = (bf16[384,1152]{1,0:T(8,128)(2,1)S(1)}, bf16[384,1152]{1,0:T(8,128)(2,1)}, u32[]{:S(2)}) copy-start(bf16[384,1152]{1,0:T(8,128)(2,1)} %wqkv_ref.3) | copy-start | bytes 2654212
  42.2 27.8 %copy-start.2 = (bf16[16,8,896]{2,1,0:T(8,128)(2,1)S(1)}, bf16[16,8,896]{2,1,0:T(8,128)(2,1)}, u32[]{:S(2)}) copy-start(bf16[16,8,896]{2,1,0:T(8,128)(2,1)} %copy-done.1) | copy-start | bytes 688132
  42.2 27.8 %copy-start.4 = (bf16[384,384]{1,0:T(8,128)(2,1)S(1)}, bf16[384,384]{1,0:T(8,128)(2,1)}, u32[]{:S(2)}) copy-start(bf16[384,384]{1,0:T(8,128)(2,1)} %wout_ref.3) | copy-start | bytes 884740
  42.2 27.9 %copy-start.5 = (bf16[128,1536]{1,0:T(8,128)(2,1)S(1)}, bf16[128,1536]{1,0:T(8,128)(2,1)}, u32[]{:S(2)}) copy-start(bf16[128,1536]{1,0:T(8,128)(2,1)} %get-tuple-element.34.shares_ref) | copy-start | bytes 1179652
  42.2 27.9 %copy-start.6 = (bf16[128,1152]{1,0:T(8,128)(2,1)S(1)}, bf16[128,1152]{1,0:T(8,128)(2,1)}, u32[]{:S(2)}) copy-start(bf16[128,1152]{1,0:T(8,128)(2,1)} %get-tuple-element.33.qkv_ref) | copy-start | bytes 884740
  42.2 27.9 %copy-start.7 = (bf16[128,384]{1,0:T(8,128)(2,1)S(1)}, bf16[128,384]{1,0:T(8,128)(2,1)}, u32[]{:S(2)}) copy-start(bf16[128,384]{1,0:T(8,128)(2,1)} %get-tuple-element.35.mix_ref) | copy-start | bytes 294916
  54.6 15.4 %collective-permute-start = (bf16[7680,128]{1,0:T(8,128)(2,1)}, bf16[7680,128]{1,0:T(8,128)(2,1)S(1)}, u32[]{:S(2)}, u32[]{:S(2)}) collective-permute-start(bf16[7680,128]{1,0:T(8,128)(2,1)} %get-tuple-element.37), channel_id=1, source_target_pairs={{0,8},{8,0},{1,9},{9,1},{2,10},{10,2},{3,11},{11,3},{4,12},{12,4},... | collective-permute-start | bytes 5898248 | tf_op jit(solution)/shard_map/ppermute | solution.py:687
  70.0 1.5 copy-start.3
  77.4 2.2 %collective-permute-start.1 = (bf16[2304,128]{1,0:T(8,128)(2,1)S(1)}, bf16[2304,128]{1,0:T(8,128)(2,1)S(1)}, u32[]{:S(2)}, u32[]{:S(2)}) collective-permute-start(bf16[2304,128]{1,0:T(8,128)(2,1)S(1)} %get-tuple-element.40), channel_id=1, source_target_pairs={{0,8},{8,0},{1,9},{9,1},{2,10},{10,2},{3,11},{11,3},{4,12},{12,4},... | collective-permute-start | bytes 1769480 | tf_op jit(solution)/shard_map/ppermute | solution.py:692
  159.5 14.4 %collective-permute-start.2 = (bf16[10240,128]{1,0:T(8,128)(2,1)S(1)}, bf16[10240,128]{1,0:T(8,128)(2,1)S(1)}, u32[]{:S(2)}, u32[]{:S(2)}) collective-permute-start(bf16[10240,128]{1,0:T(8,128)(2,1)S(1)} %bitcast.12), channel_id=1, source_target_pairs={{0,8},{8,0},{1,9},{9,1},{2,10},{10,2},{3,11},{11,3},{4,12},{12,4},... | collective-permute-start | bytes 7864328 | tf_op jit(solution)/shard_map/ppermute | solution.py:696

commit v4 on v3

--- a/solution.py
+++ b/solution.py
@@ -21,7 +21,7 @@
 F32 = jnp.float32
 BF16 = jnp.bfloat16
 EVERYONE = ("line", "core", "res")
-SHARERS = 64
+SHARERS = 32
 GAIN_ROW = 6 * POINTS
 
 PIECES = {
@@ -37,7 +37,24 @@
 LATE_UNITS = [6, 6]
 EARLY = max(EARLY_UNITS) * C
 LATE = max(LATE_UNITS) * C
-HALF = -(-(EARLY + LATE) // (SHARERS * 16)) * SHARERS * 16
+QUARTER = -(-(EARLY + LATE) // (2 * SHARERS * 16)) * SHARERS * 16
+CHUNK = QUARTER // SHARERS
+
+
+def pair_groups():
+    bits = (2, 1)
+    place = lambda line, core, res: (line * 2 + core) * 8 + res
+    spots = [(line, core, res) for line in range(8) for core in range(2) for res in range(8)]
+    pairs = [(place(*spot), place(spot[0], spot[1], spot[2] ^ bits[spot[1]])) for spot in spots]
+    groups = [
+        [place(line, core, res) for line in range(8) for res in range(8) if bool(res & bits[core]) == odd]
+        for core in range(2)
+        for odd in (False, True)
+    ]
+    return pairs, groups
+
+
+PAIRS, GROUPS = pair_groups()
 
 
 def place_units():
@@ -217,27 +234,8 @@
 
 def time_backward(
     core_ref, back_ref, rows_ref, qkv_ref, shares_ref, mix_ref, wqkv_ref, wout_ref,
-    keep_early_ref, got_early_ref,
-    sent_ref, keep_ref, give_ref, total_ref,
-    dqkv_ref, dcol_ref, pcol_ref, early_ref, got_ref, sems,
+    sent_ref, keep_ref, give_ref, dqkv_ref, dcol_ref, pcol_ref,
 ):
-    part = EARLY // 3
-    spans = [slice(g * part, (g + 1) * part) for g in range(3)]
-    arriving = []
-    for g, span in enumerate(spans):
-        arriving.append(
-            (
-                pltpu.make_async_copy(keep_early_ref.at[span], early_ref.at[span], sems.at[3 * g]),
-                pltpu.make_async_copy(got_early_ref.at[span], got_ref.at[span], sems.at[3 * g + 1]),
-            )
-        )
-    for pair in arriving:
-        for copy in pair:
-            copy.start()
-    leaving = [
-        pltpu.make_async_copy(early_ref.at[span], total_ref.at[span], sems.at[3 * g + 2])
-        for g, span in enumerate(spans)
-    ]
     put = halves(core_ref[0], keep_ref, give_ref)
     back = back_ref[...].reshape(N, 1024)
     dx1 = back[:, 0:C]
@@ -267,18 +265,11 @@
         dqkv_ref[:, g * 128 : (g + 1) * 128] = dq.astype(BF16)
         dqkv_ref[:, C + g * 128 : C + (g + 1) * 128] = dk.astype(BF16)
         dqkv_ref[:, 2 * C + g * 128 : 2 * C + (g + 1) * 128] = dv.astype(BF16)
-        for copy in arriving[g]:
-            copy.wait()
-        summed = early_ref[spans[g], :].astype(F32) + got_ref[spans[g], :].astype(F32)
-        early_ref[spans[g], :] = summed.astype(BF16)
-        leaving[g].start()
     put("time_qkv", tm(normed.astype(BF16), dqkv_ref[...]))
     dnormed = mt(dqkv_ref[...], wqkv_ref[...]).astype(BF16).astype(F32)
     pulled = norm_pull(dnormed, normed, inverse).astype(BF16).astype(F32)
     sent_ref[:, 0:C] = (dx1.astype(F32) + pulled).astype(BF16)
     sent_ref[:, C : 2 * C] = back[:, C : 2 * C]
-    for copy in leaving:
-        copy.wait()
 
 
 def selectors():
@@ -520,23 +511,17 @@
     )(place, neighbors, rows, w_qkv, w_out)
 
 
-def call_time_backward(core, back, rows, qkv, shares, mix, w_qkv, w_out, keep_early, got_early):
+def call_time_backward(core, back, rows, qkv, shares, mix, w_qkv, w_out):
     return pl.pallas_call(
         time_backward,
-        in_specs=[SMEM] + [VMEM] * 7 + [HBM] * 2,
-        out_specs=(VMEM, VMEM, VMEM, HBM),
-        out_shape=(
-            like((N, 2 * C), BF16), like((LATE, 128), BF16), like((LATE, 128), BF16),
-            like((HALF, 128), BF16),
-        ),
+        in_specs=[SMEM] + [VMEM] * 7,
+        out_shape=(like((N, 2 * C), BF16), like((LATE, 128), BF16), like((LATE, 128), BF16)),
         scratch_shapes=[
             pltpu.VMEM((N, 3 * C), BF16), pltpu.VMEM((4 * N, N), BF16), pltpu.VMEM((4 * N, N), BF16),
-            pltpu.VMEM((EARLY, 128), BF16), pltpu.VMEM((EARLY, 128), BF16),
-            pltpu.SemaphoreType.DMA((9,)),
         ],
         compiler_params=limit(20),
         name="time_backward",
-    )(core, back, rows, qkv, shares, mix, w_qkv, w_out, keep_early, got_early)
+    )(core, back, rows, qkv, shares, mix, w_qkv, w_out)
 
 
 def call_point_attention(core, weight, rows, w_qkv, w_pts, w_rep, w_out, w_up, w_down):
@@ -563,26 +548,82 @@
     )(core, weight, rows, *sources)
 
 
-def add_late(total_in_ref, keep_ref, got_ref, total_ref, late_ref, sem):
-    late = keep_ref[...].astype(F32) + got_ref[...].astype(F32)
-    late_ref[0:LATE, :] = late.astype(BF16)
-    late_ref[LATE:, :] = jnp.zeros((HALF - EARLY - LATE, 128), BF16)
-    copy = pltpu.make_async_copy(late_ref, total_ref.at[EARLY:HALF], sem)
-    copy.start()
-    copy.wait()
-
-
-def call_add_late(total, keep, got):
+def add_early(side_ref, keep_ref, got_ref, mine_ref, give_ref, one_ref, two_ref, sems):
+    part = EARLY // 2
+    steps = []
+    for step, target in enumerate((give_ref, mine_ref)):
+        start = pl.multiple_of((side_ref[0] if step else 1 - side_ref[0]) * part, part)
+        span = slice(step * part, (step + 1) * part)
+        steps.append(
+            (
+                pltpu.make_async_copy(keep_ref.at[pl.ds(start, part)], one_ref.at[span], sems.at[3 * step]),
+                pltpu.make_async_copy(got_ref.at[pl.ds(start, part)], two_ref.at[span], sems.at[3 * step + 1]),
+                pltpu.make_async_copy(one_ref.at[span], target, sems.at[3 * step + 2]),
+            )
+        )
+    for first, second, _ in steps:
+        first.start()
+        second.start()
+    for step, (first, second, out) in enumerate(steps):
+        first.wait()
+        second.wait()
+        span = slice(step * part, (step + 1) * part)
+        summed = one_ref[span, :].astype(F32) + two_ref[span, :].astype(F32)
+        one_ref[span, :] = summed.astype(BF16)
+        out.start()
+    for _, _, out in steps:
+        out.wait()
+
+
+def call_add_early(side, keep, got):
+    part = like((EARLY // 2, 128), BF16)
+    return pl.pallas_call(
+        add_early,
+        in_specs=[SMEM, HBM, HBM],
+        out_specs=(HBM, HBM),
+        out_shape=(part, part),
+        scratch_shapes=[
+            pltpu.VMEM((EARLY, 128), BF16), pltpu.VMEM((EARLY, 128), BF16),
+            pltpu.SemaphoreType.DMA((6,)),
+        ],
+        compiler_params=limit(60),
+        cost_estimate=pl.CostEstimate(flops=EARLY * 128, bytes_accessed=EARLY * 128 * 6, transcendentals=0),
+        name="add_early",
+    )(side, keep, got)
+
+
+def add_late(side_ref, keep_ref, got_ref, mine_ref, give_ref):
+    part = LATE // 2
+    for ref, index in ((mine_ref, side_ref[0]), (give_ref, 1 - side_ref[0])):
+        span = pl.ds(pl.multiple_of(index * part, part), part)
+        summed = keep_ref[span, :].astype(F32) + got_ref[span, :].astype(F32)
+        ref[...] = summed.astype(BF16)
+
+
+def call_add_late(side, keep, got):
+    part = like((LATE // 2, 128), BF16)
     return pl.pallas_call(
         add_late,
-        in_specs=[HBM, VMEM, VMEM],
-        out_specs=HBM,
-        out_shape=like((HALF, 128), BF16),
-        scratch_shapes=[pltpu.VMEM((HALF - EARLY, 128), BF16), pltpu.SemaphoreType.DMA],
-        input_output_aliases={0: 0},
+        in_specs=[SMEM, VMEM, VMEM],
+        out_shape=(part, part),
         compiler_params=limit(8),
         name="add_late",
-    )(total, keep, got)
+    )(side, keep, got)
+
+
+def add_pairs(early_ref, got_early_ref, late_ref, got_late_ref, total_ref):
+    early, late = EARLY // 2, LATE // 2
+    summed = early_ref[...].astype(F32) + got_early_ref[...].astype(F32)
+    total_ref[0:early, :] = summed.astype(BF16)
+    summed = late_ref[...].astype(F32) + got_late_ref[...].astype(F32)
+    total_ref[early : early + late, :] = summed.astype(BF16)
+    total_ref[early + late :, :] = jnp.zeros((QUARTER - early - late, 128), BF16)
+
+
+def call_add_pairs(*parts):
+    return pl.pallas_call(
+        add_pairs, out_shape=like((QUARTER, 128), BF16), compiler_params=limit(12), name="add_pairs"
+    )(*parts)
 
 
 def add_parts(parts_ref, copies_ref):
@@ -591,71 +632,134 @@
     for k in range(1, count):
         total = total + parts_ref[k].astype(F32)
     total = total.astype(BF16)
-    for k in range(count):
+    for k in range(copies_ref.shape[0]):
         copies_ref[k] = total
 
 
 def call_add_parts(parts):
     return pl.pallas_call(
-        add_parts, out_shape=like(parts.shape, BF16), compiler_params=limit(12), name="add_parts"
+        add_parts, out_shape=like((2 * SHARERS, *parts.shape[1:]), BF16), compiler_params=limit(12),
+        name="add_parts",
     )(parts)
 
 
-def unpack(core_ref, mine_ref, other_ref, ended_ref, *refs):
-    out_refs, gain_ref, output_ref, token_ref = refs[:7], refs[7], refs[8], refs[9]
-    half_ref, stages, in_sems, out_sems = refs[10], refs[11:18], refs[18], refs[19]
-    core = core_ref[0]
-    mine = pltpu.make_async_copy(mine_ref, half_ref.at[core], in_sems.at[0])
-    other = pltpu.make_async_copy(other_ref, half_ref.at[1 - core], in_sems.at[1])
-    mine.start()
-    other.start()
+def final_spot(late, at):
+    unit = (at - EARLY if late else at) // C
+    room = (LATE if late else EARLY) // (2 * C)
+    return unit // room, (EARLY // 2 if late else 0) + (unit % room) * C
+
+
+def segments(row):
+    begin = row
+    while begin < row + C:
+        chunk, low = divmod(begin, CHUNK)
+        size = min(CHUNK - low, row + C - begin)
+        yield chunk, low, size, begin - row
+        begin += size
+
+
+def unpack_half(own, core_ref, parts_ref, out_refs, held_ref, stage_ref, gain_ref, in_sems, out_sems):
+    for half in range(2):
+
+        @pl.when((core_ref[0] == half) == own)
+        def run(half=half):
+            for q in range(2):
+                for line in range(8):
+                    for high in range(2):
+                        source = (
+                            parts_ref.at[line, high, q] if half == 0 else parts_ref.at[line, high, :, q]
+                        )
+                        target = held_ref.at[q, pl.ds((line * 2 + high) * 2, 2)]
+                        pltpu.make_async_copy(source, target, in_sems.at[q]).start()
+            leaving = []
+            for q in range(2):
+                pltpu.make_async_copy(held_ref.at[q], held_ref.at[q], in_sems.at[q]).wait()
+                for k, name in enumerate(PIECES):
+                    tiles = PIECES[name][1] // 128
+                    for unit, (owner, at) in enumerate(UNITS[name]):
+                        quarter, row = final_spot(name.startswith("time"), at)
+                        if owner != half or quarter != q:
+                            continue
+                        slot = len(leaving)
+                        for chunk, low, size, to in segments(row):
+                            stage_ref[slot, to : to + size, :] = held_ref[
+                                q, chunk, low : low + size, :
+                            ].astype(F32)
+                        down, across = (unit // tiles) * C, (unit % tiles) * 128
+                        rows = GAIN_ROW if name == "ipa_points" else C
+                        if name == "ipa_points" and across == 0:
+                            gain_ref[...] = stage_ref[slot, GAIN_ROW : GAIN_ROW + 1, :]
+                        leaving.append(
+                            pltpu.make_async_copy(
+                                stage_ref.at[slot, 0:rows],
+                                out_refs[k].at[down : down + rows, across : across + 128],
+                                out_sems.at[slot],
+                            )
+                        )
+                        leaving[-1].start()
+            for copy in leaving:
+                copy.wait()
+
+
+def unpack_own(core_ref, parts_ref, *refs):
+    gain_ref = refs[7]
+    gain_ref[...] = jnp.zeros((1, 128), F32)
+    unpack_half(True, core_ref, parts_ref, refs[:7], refs[8], refs[9], gain_ref, refs[10], refs[11])
+
+
+def unpack_other(core_ref, parts_ref, gain_own_ref, ended_ref, *refs):
+    out_refs, gain_ref, output_ref, token_ref = refs[7:14], refs[14], refs[15], refs[16]
+    held_ref, stage_ref, part_ref, in_sems, out_sems = refs[17:]
     residues, frames, _ = ended_ref.shape
     ended = mm(order_matrix(), ended_ref[...].reshape(N, 2 * C)).astype(BF16)
     token_ref[...] = ended[:, 0:C].reshape(frames, residues, C)
     output_ref[...] = ended[:, C:].reshape(frames, residues, C)
-    mine.wait()
-    other.wait()
-    leaving = []
-    for k, (name, (rows, columns)) in enumerate(PIECES.items()):
-        tiles = columns // 128
-        for unit, (half, at) in enumerate(UNITS[name]):
-            down, across = (unit // tiles) * C, (unit % tiles) * 128
-            value = half_ref[half, at : at + C, :].astype(F32)
-            if name == "ipa_points":
-                stages[k][:, across : across + 128] = value[0:GAIN_ROW]
-                if across == 0:
-                    gain = value[GAIN_ROW : GAIN_ROW + 1, :]
-            else:
-                stages[k][down : down + C, across : across + 128] = value
-        leaving.append(pltpu.make_async_copy(stages[k], out_refs[k], out_sems.at[k]))
-        leaving[-1].start()
+    part_ref[...] = jnp.zeros((1, 128), F32)
+    unpack_half(False, core_ref, parts_ref, out_refs, held_ref, stage_ref, part_ref, in_sems, out_sems)
+    gain = gain_own_ref[...] + part_ref[...]
     lane = lax.broadcasted_iota(jnp.int32, (1, 128), 1)
     for h in range(H):
         gain_ref[h] = jnp.sum(jnp.where(lane == h, gain, 0.0))
-    for copy in leaving:
-        copy.wait()
-
-
-def call_unpack(core, mine, other, ended):
+
+
+OUTS = [
+    (GAIN_ROW if name == "ipa_points" else rows, columns) for name, (rows, columns) in PIECES.items()
+]
+UNPACK_SCRATCH = [
+    pltpu.VMEM((2, SHARERS, CHUNK, 128), BF16),
+    pltpu.VMEM((EARLY_UNITS[0] + LATE_UNITS[0], C, 128), F32),
+]
+UNPACK_SEMS = [
+    pltpu.SemaphoreType.DMA((2,)), pltpu.SemaphoreType.DMA((EARLY_UNITS[0] + LATE_UNITS[0],)),
+]
+
+
+def call_unpack_own(core, parts):
+    return pl.pallas_call(
+        unpack_own,
+        in_specs=[SMEM, HBM],
+        out_specs=(*[HBM] * 7, VMEM),
+        out_shape=(*[like(shape, F32) for shape in OUTS], like((1, 128), F32)),
+        scratch_shapes=UNPACK_SCRATCH + UNPACK_SEMS,
+        compiler_params=limit(20),
+        cost_estimate=pl.CostEstimate(flops=0, bytes_accessed=8 * MEGA, transcendentals=0),
+        name="unpack_own",
+    )(core, parts)
+
+
+def call_unpack_other(core, parts, gain, ended, grads):
     residues, frames, _ = ended.shape
-    shapes = [
-        (GAIN_ROW if name == "ipa_points" else rows, columns)
-        for name, (rows, columns) in PIECES.items()
-    ]
     rows = like((frames, residues, C), BF16)
     return pl.pallas_call(
-        unpack,
-        in_specs=[SMEM, HBM, HBM, VMEM],
+        unpack_other,
+        in_specs=[SMEM, HBM, VMEM, VMEM] + [HBM] * 7,
         out_specs=(*[HBM] * 7, SMEM, VMEM, VMEM),
-        out_shape=(*[like(shape, F32) for shape in shapes], like((H,), F32), rows, rows),
-        scratch_shapes=[
-            pltpu.VMEM((2, HALF, 128), BF16),
-            *[pltpu.VMEM(shape, F32) for shape in shapes],
-            pltpu.SemaphoreType.DMA((2,)), pltpu.SemaphoreType.DMA((7,)),
-        ],
-        compiler_params=limit(24),
-        name="unpack",
-    )(core, mine, other, ended)
+        out_shape=(*[like(shape, F32) for shape in OUTS], like((H,), F32), rows, rows),
+        scratch_shapes=UNPACK_SCRATCH + [pltpu.VMEM((1, 128), F32)] + UNPACK_SEMS,
+        input_output_aliases={4 + k: k for k in range(7)},
+        compiler_params=limit(20),
+        name="unpack_other",
+    )(core, parts, gain, ended, *grads)
 
 
 def repeat_points(weight):
@@ -675,6 +779,8 @@
     frames, residues = tokens.shape[:2]
     place = lax.axis_index(("line", "core")).astype(jnp.int32).reshape(1)
     core = lax.axis_index("core").astype(jnp.int32).reshape(1)
+    place_res = lax.axis_index("res").astype(jnp.int32)
+    side = jnp.where(core == 0, (place_res >> 1) & 1, place_res & 1)
     swap = [(0, 1), (1, 0)]
     points = w_ipa_points.T
     rows = swap_rows(call_pack_rows(tokens, cotangent, rigid_frames), ("line", "core"))
@@ -685,17 +791,24 @@
         w_ipa_out, w_up, w_down,
     )
     got_early = lax.ppermute(give_early, "core", swap)
-    ended, keep_late, give_late, total = call_time_backward(
-        core, swap_rows(back, EVERYONE), rows, qkv, shares, mix, w_time_qkv, w_time_out,
-        keep_early, got_early,
+    mine_early, give_early = call_add_early(side, keep_early, got_early)
+    got_early = lax.ppermute(give_early, EVERYONE, PAIRS)
+    ended, keep_late, give_late = call_time_backward(
+        core, swap_rows(back, EVERYONE), rows, qkv, shares, mix, w_time_qkv, w_time_out
     )
     got_late = lax.ppermute(give_late, "core", swap)
-    total = call_add_late(total, keep_late, got_late)
-    parts = swap_rows(total.reshape(SHARERS, HALF // SHARERS, 128), ("line", "res"))
-    mine = swap_rows(call_add_parts(parts), ("line", "res")).reshape(HALF, 128)
-    other = lax.ppermute(mine, "core", swap)
+    mine_late, give_late = call_add_late(side, keep_late, got_late)
+    got_late = lax.ppermute(give_late, EVERYONE, PAIRS)
+    total = call_add_pairs(mine_early, got_early, mine_late, got_late)
+    parts = lax.all_to_all(
+        total.reshape(SHARERS, CHUNK, 128), EVERYONE, split_axis=0, concat_axis=0, tiled=True,
+        axis_index_groups=GROUPS,
+    )
+    own = swap_rows(call_add_parts(parts), ("line", "res")).reshape(8, 2, 2, 2, CHUNK, 128)
+    other = lax.ppermute(own, "core", swap)
     ended = swap_rows(ended.reshape(residues, frames, 2 * C), ("line", "core"))
-    *grads, gain, output, token_grad = call_unpack(core, mine, other, ended)
+    *grads, gain = call_unpack_own(core, own)
+    *grads, gain, output, token_grad = call_unpack_other(core, other, gain, ended, grads)
     grads = dict(zip(PIECES, grads))
     return (
         output, token_grad, grads["time_qkv"], grads["time_out"], grads["ipa_qkv"],

time: 180 us -> 169 us (0.939)
  blocking collectives: 105 us -> 67.3 us
  waiting for transfers between devices: 20 us -> 35.4 us
  starting transfers between devices: 18.9 us -> 28.1 us
  Pallas kernels: 30.3 us -> 34.5 us
    all_to_all x4 -> x1, blocking collectives: 105 us -> 39.7 us  [swap_rows(): return lax.all_to_all(rows, axes, split_axis=0, concat_axis=0, tiled=True)]
    all_to_all x0 -> x1, blocking collectives: none -> 27.6 us  [body(): lax.all_to_all(total.reshape(SHARERS, CHUNK, 128), EVERYONE, split_axis=0...]
    all_to_all x2 -> x4, waiting for transfers between devices: 18.4 us -> 28.1 us  [swap_rows(): return lax.all_to_all(rows, axes, split_axis=0, concat_axis=0, tiled=True)]
    all_to_all x2 -> x4, starting transfers between devices: 14.6 us -> 21.8 us  [swap_rows(): return lax.all_to_all(rows, axes, split_axis=0, concat_axis=0, tiled=True)]
    ppermute x1 -> x3, waiting for transfers between devices: 0.01 us -> 5.53 us  [the longest x1 5.52 us: body(): got_late = lax.ppermute(give_late, EVERYONE, PAIRS)]
    pallas_call x4 -> x7, Pallas kernels: 11.9 us -> 16.3 us  [the longest x1 4.56 us: call_unpack_other(): pl.pallas_call(unpack_other, in_specs=[SMEM, HBM, VMEM, VMEM] + [HBM] * 7...]
    ppermute x1 -> x3, starting transfers between devices: 3.17 us -> 5.17 us  [the longest x1 3.17 us: body(): other = lax.ppermute(own, 'core', swap)]
  transfers between devices with their start and end apart: 5 -> 9, of which waited for: 3 -> 7; matrix products, arithmetic and copies ran while one was open for 1% -> 1% of each run, Pallas kernels for 0% -> 7%
where the time goes in v4:
time: 169 us
  blocking collectives  67.3 us (40%)
  waiting for transfers between devices  35.4 us (21%)
  Pallas kernels  34.5 us (20%)
  starting transfers between devices  28.1 us (17%)
    all_to_all x1, blocking collectives, swap_rows(): return lax.all_to_all(rows, axes, split_axis=0, concat_axis=0, tiled=True)  39.7 us
    all_to_all x4, waiting for transfers between devices, swap_rows(): return lax.all_to_all(rows, axes, split_axis=0, concat_axis=0, tiled=True)  28.1 us
    all_to_all x1, blocking collectives, body(): lax.all_to_all(total.reshape(SHARERS, CHUNK, 128), EVERYONE, split_axis=0...  27.6 us
    all_to_all x4, starting transfers between devices, swap_rows(): return lax.all_to_all(rows, axes, split_axis=0, concat_axis=0, tiled=True)  21.8 us
    pallas_call x1, Pallas kernels, call_point_attention(): pl.pallas_call(point_attention, in_specs=[SMEM, SMEM, VMEM] + [HBM] * len...  12.2 us
    ppermute x1, waiting for transfers between devices, body(): got_late = lax.ppermute(give_late, EVERYONE, PAIRS)  5.52 us
    pallas_call x1, Pallas kernels, call_unpack_other(): pl.pallas_call(unpack_other, in_specs=[SMEM, HBM, VMEM, VMEM] + [HBM] * 7...  4.56 us
    pallas_call x1, Pallas kernels, call_unpack_own(): pl.pallas_call(unpack_own, in_specs=[SMEM, HBM], out_specs=(*[HBM] * 7, V...  4.19 us
  transfers between devices with their start and end apart: 9, of which 7 were waited for; matrix products, arithmetic and copies ran while one was open for 1% of the time, Pallas kernels for 7%

profile of v4, /device:TPU:1, one launch (start us, length us, event | category | flops | bytes accessed | tf_op | source)
XLA Modules:
  0.0 168.8 jit_solution(645122343376846476)
XLA Ops:
  0.6 0.0 copy-start.9
  0.7 2.0 %pack_rows.1 = bf16[16,8,896]{2,1,0:T(8,128)(2,1)} custom-call(bf16[8,16,384]{2,1,0:T(8,128)(2,1)} %tokens_ref.1, bf16[8,16,384]{2,1,0:T(8,128)(2,1)} %cotangent_ref.1, bf16[12,8,16]{2,1,0:T(8,128)(2,1)} %rigid_ref.1), custom_call_target="tpu_custom_call" | custom-call | tf_op jit(solution)/shard_map/pack_rows/pallas_call | solution.py:493
  2.6 9.5 %all-to-all-start = ((bf16[16,8,896]{2,1,0:T(8,128)(2,1)}), bf16[16,8,896]{2,1,0:T(8,128)(2,1)S(1)}, u32[]{:S(2)}, u32[]{:S(2)}) async-start(bf16[16,8,896]{2,1,0:T(8,128)(2,1)} %pack_rows.1), calls=%async_computation | async-start | bytes 458752 | tf_op jit(solution)/shard_map/all_to_all | solution.py:772
  12.1 8.4 %all-to-all-done = bf16[16,8,896]{2,1,0:T(8,128)(2,1)S(1)} async-done(((bf16[16,8,896]{2,1,0:T(8,128)(2,1)}), bf16[16,8,896]{2,1,0:T(8,128)(2,1)S(1)}, u32[]{:S(2)}, u32[]{:S(2)}) %all-to-all-start) | async-done | bytes 229408 | tf_op jit(solution)/shard_map/all_to_all | solution.py:772
  20.5 0.0 copy-start.1
  20.5 0.7 copy-done.1
  21.2 4.0 %time_forward.1 = (bf16[128,8,128]{2,1,0:T(8,128)(2,1)}, bf16[128,1152]{1,0:T(8,128)(2,1)}, bf16[128,1536]{1,0:T(8,128)(2,1)}, bf16[128,384]{1,0:T(8,128)(2,1)}) custom-call(s32[1]{0:T(128)} %bitcast.3.place_ref, s32[16,32]{1,0:T(8,128)} %neighbors_ref.1, bf16[128,896]{1,0:T(8,128)(2,1)} %bitcast.16, bf16[384,1152]{1,0:T(8,128)(2,1)} %wqkv_ref.3, ...), custom_call_target="tpu_custom_call" | custom-call | tf_op jit(solution)/shard_map/time_forward/pallas_call | solution.py:502
  25.3 5.2 %all-to-all-start.1 = ((bf16[128,8,128]{2,1,0:T(8,128)(2,1)}), bf16[128,8,128]{2,1,0:T(8,128)(2,1)S(1)}, u32[]{:S(2)}, u32[]{:S(2)}) async-start(bf16[128,8,128]{2,1,0:T(8,128)(2,1)} %get-tuple-element.42), calls=%async_computation.1 | async-start | bytes 524288 | tf_op jit(solution)/shard_map/all_to_all | solution.py:772
  30.4 0.0 copy-done.9
  30.4 1.1 fusion.4
  31.6 9.9 %all-to-all-done.1.rows_ref = bf16[128,8,128]{2,1,0:T(8,128)(2,1)S(1)} async-done(((bf16[128,8,128]{2,1,0:T(8,128)(2,1)}), bf16[128,8,128]{2,1,0:T(8,128)(2,1)S(1)}, u32[]{:S(2)}, u32[]{:S(2)}) %all-to-all-start.1) | async-done | bytes 262176 | tf_op jit(solution)/shard_map/all_to_all | solution.py:772
  41.5 0.0 copy-start.8
  41.5 0.7 copy-done.8
  42.2 12.2 %point_attention.1 = (bf16[128,8,128]{2,1,0:T(8,128)(2,1)}, bf16[7680,128]{1,0:T(8,128)(2,1)}, bf16[7680,128]{1,0:T(8,128)(2,1)}) custom-call(s32[1]{0:T(128)} %bitcast.core_ref, f32[12]{0:T(128)} %weight_ref.1, bf16[128,8,128]{2,1,0:T(8,128)(2,1)} %copy-done.8, bf16[384,1152]{1,0:T(8,128)(2,1)} %refs_0_.1, bf16[128,1024]{1,0:T(8,128)(2,1)} %constant.31.clone.refs_1_, ...), custom_call_target="tpu_custom_call" | custom-call | tf_op jit(solution)/shard_map/point_attention/pallas_call | solution.py:530
  54.4 0.6 collective-permute-start
  55.0 3.8 %all-to-all-start.2 = ((bf16[128,8,128]{2,1,0:T(8,128)(2,1)}), bf16[128,8,128]{2,1,0:T(8,128)(2,1)S(1)}, u32[]{:S(2)}, u32[]{:S(2)}) async-start(bf16[128,8,128]{2,1,0:T(8,128)(2,1)} %get-tuple-element.47), calls=%async_computation.2 | async-start | bytes 524288 | tf_op jit(solution)/shard_map/all_to_all | solution.py:772
  58.8 0.1 collective-permute-done.got_ref
  58.9 0.0 copy-start
  58.9 0.0 copy-start.2
  58.9 0.0 copy-start.3
  58.9 0.0 copy-start.5
  58.9 0.0 copy-start.6
  58.9 0.0 copy-start.7
  58.9 3.5 %add_early.1 = (bf16[3840,128]{1,0:T(8,128)(2,1)}, bf16[3840,128]{1,0:T(8,128)(2,1)}) custom-call(s32[1]{0:T(128)S(6)} %select_n.4.side_ref, bf16[7680,128]{1,0:T(8,128)(2,1)} %get-tuple-element.43.keep_ref, bf16[7680,128]{1,0:T(8,128)(2,1)} %collective-permute-done.got_ref), custom_call_target="tpu_custom_call" | custom-call | flops 983040 | bytes 5898240 | tf_op jit(solution)/shard_map/add_early/pallas_call | solution.py:580
  62.4 1.6 collective-permute-start.1
  64.0 5.8 %all-to-all-done.2.back_ref = bf16[128,8,128]{2,1,0:T(8,128)(2,1)S(1)} async-done(((bf16[128,8,128]{2,1,0:T(8,128)(2,1)}), bf16[128,8,128]{2,1,0:T(8,128)(2,1)S(1)}, u32[]{:S(2)}, u32[]{:S(2)}) %all-to-all-start.2) | async-done | bytes 262176 | tf_op jit(solution)/shard_map/all_to_all | solution.py:772
  69.8 0.0 copy-done
  69.8 0.0 copy-done.2
  69.8 0.0 copy-done.3
  69.8 0.0 copy-done.5
  69.8 0.0 copy-done.6
  69.8 0.0 copy-done.7
  69.9 0.0 copy-start.4
  69.9 3.4 %time_backward.1 = (bf16[128,768]{1,0:T(8,128)(2,1)}, bf16[2304,128]{1,0:T(8,128)(2,1)S(1)}, bf16[2304,128]{1,0:T(8,128)(2,1)S(1)}) custom-call(s32[1]{0:T(128)} %bitcast.core_ref, bf16[128,8,128]{2,1,0:T(8,128)(2,1)S(1)} %all-to-all-done.2.back_ref, bf16[128,896]{1,0:T(8,128)(2,1)S(1)} %bitcast.17, bf16[128,1152]{1,0:T(8,128)(2,1)S(1)} %copy-done.6, ...), custom_call_target="tpu_custom_call" | custom-call | tf_op jit(solution)/shard_map/time_backward/pallas_call | solution.py:515
  73.2 0.5 collective-permute-start.2
  73.7 1.6 collective-permute-done.2.got_ref
  75.4 0.1 add_late.1
  75.5 0.4 collective-permute-start.3
  75.9 5.5 %collective-permute-done.3.got_late_ref = bf16[1152,128]{1,0:T(8,128)(2,1)S(1)} collective-permute-done((bf16[1152,128]{1,0:T(8,128)(2,1)S(1)}, bf16[1152,128]{1,0:T(8,128)(2,1)S(1)}, u32[]{:S(2)}, u32[]{:S(2)}) %collective-permute-start.3) | collective-permute-done | bytes 294944 | tf_op jit(solution)/shard_map/ppermute | solution.py:801
  81.4 0.0 collective-permute-done.1.got_early_ref
  81.4 0.0 copy-done.4
  81.5 0.3 add_pairs.1
  81.8 27.6 %all_to_all.30.parts_ref = bf16[32,160,128]{2,1,0:T(8,128)(2,1)S(1)} all-to-all(bf16[32,160,128]{2,1,0:T(8,128)(2,1)S(1)} %bitcast.15), channel_id=1, replica_groups={{0,1,4,5,16,17,20,21,32,33,36,37,48,49,52,53,64,65,68,69,80,81,84,85,96..., dimensions={0} | all-to-all | bytes 2621440 | tf_op jit(solution)/shard_map/all_to_all | solution.py:803
  109.4 0.3 add_parts.1
  109.6 39.7 %all_to_all.31 = bf16[64,160,128]{2,1,0:T(8,128)(2,1)S(1)} all-to-all(bf16[64,160,128]{2,1,0:T(8,128)(2,1)S(1)} %add_parts.1), channel_id=1, replica_groups=mesh['line'=8,'core'=2,'res'=8] {'line','res'}, dimensions={0} | all-to-all | bytes 5242880 | tf_op jit(solution)/shard_map/all_to_all | solution.py:772
  149.3 3.2 %collective-permute-start.4 = (bf16[8,2,2,2,160,128]{5,4,3,2,1,0:T(8,128)(2,1)S(1)}, bf16[8,2,2,2,160,128]{5,4,3,2,1,0:T(8,128)(2,1)}, u32[]{:S(2)}, u32[]{:S(2)}) collective-permute-start(bf16[8,2,2,2,160,128]{5,4,3,2,1,0:T(8,128)(2,1)S(1)} %bitcast.13), channel_id=1, source_target_pairs={{0,8},{8,0},{1,9},{9,1},{2,10},{10,2},{3,11},{11,3},{4,12},{12,4},... | collective-permute-start | bytes 7864328 | tf_op jit(solution)/shard_map/ppermute | solution.py:808
  152.5 3.4 %all-to-all-start.5 = ((bf16[16,8,768]{2,1,0:T(8,128)(2,1)}), bf16[16,8,768]{2,1,0:T(8,128)(2,1)S(1)}, u32[]{:S(2)}, u32[]{:S(2)}) async-start(bf16[16,8,768]{2,1,0:T(8,128)(2,1)} %bitcast.10), calls=%async_computation.5 | async-start | bytes 393216 | tf_op jit(solution)/shard_map/all_to_all | solution.py:772
  155.9 4.2 %unpack_own.1 = (f32[384,1536]{1,0:T(8,128)}, f32[384,384]{1,0:T(8,128)}, f32[288,384]{1,0:T(8,128)}, f32[384,1152]{1,0:T(8,128)}, f32[1536,384]{1,0:T(8,128)}, ...) custom-call(s32[1]{0:T(128)} %bitcast.core_ref, bf16[8,2,2,2,160,128]{5,4,3,2,1,0:T(8,128)(2,1)S(1)} %bitcast.14), custom_call_target="tpu_custom_call" | custom-call | bytes 8388608 | tf_op jit(solution)/shard_map/unpack_own/pallas_call | solution.py:738
  160.1 3.9 %all-to-all-done.5.ended_ref = bf16[16,8,768]{2,1,0:T(8,128)(2,1)S(1)} async-done(((bf16[16,8,768]{2,1,0:T(8,128)(2,1)}), bf16[16,8,768]{2,1,0:T(8,128)(2,1)S(1)}, u32[]{:S(2)}, u32[]{:S(2)}) %all-to-all-start.5) | async-done | bytes 196640 | tf_op jit(solution)/shard_map/all_to_all | solution.py:772
  164.0 0.0 collective-permute-done.4.parts_ref
  164.1 4.6 %unpack_other.1 = (f32[384,1536]{1,0:T(8,128)}, f32[384,384]{1,0:T(8,128)}, f32[288,384]{1,0:T(8,128)}, f32[384,1152]{1,0:T(8,128)}, f32[1536,384]{1,0:T(8,128)}...) custom-call(s32[1]{0:T(128)} %bitcast.core_ref, ...), custom_call_target="tpu_custom_call", output_to_operand_aliasing={{0}: (4, {}), {1}: (5, {}), {2}: (6, {}), {3}: (7, {}), {4}... | custom-call | tf_op jit(solution)/shard_map/unpack_other/pallas_call | solution.py:753
Async XLA Ops:
  0.6 29.8 %copy-start.9 = (bf16[384,288]{0,1:T(8,128)(2,1)S(1)}, bf16[384,288]{0,1:T(8,128)(2,1)}, u32[]{:S(2)}) copy-start(bf16[384,288]{0,1:T(8,128)(2,1)} %param.22) | copy-start | bytes 663556
  2.6 17.9 %all-to-all-start = ((bf16[16,8,896]{2,1,0:T(8,128)(2,1)}), bf16[16,8,896]{2,1,0:T(8,128)(2,1)S(1)}, u32[]{:S(2)}, u32[]{:S(2)}) async-start(bf16[16,8,896]{2,1,0:T(8,128)(2,1)} %pack_rows.1), calls=%async_computation | async-start | bytes 458752 | tf_op jit(solution)/shard_map/all_to_all | solution.py:772
  20.5 0.7 copy-start.1
  25.3 16.2 %all-to-all-start.1 = ((bf16[128,8,128]{2,1,0:T(8,128)(2,1)}), bf16[128,8,128]{2,1,0:T(8,128)(2,1)S(1)}, u32[]{:S(2)}, u32[]{:S(2)}) async-start(bf16[128,8,128]{2,1,0:T(8,128)(2,1)} %get-tuple-element.42), calls=%async_computation.1 | async-start | bytes 524288 | tf_op jit(solution)/shard_map/all_to_all | solution.py:772
  41.5 0.7 copy-start.8
  54.4 4.5 %collective-permute-start = (bf16[7680,128]{1,0:T(8,128)(2,1)}, bf16[7680,128]{1,0:T(8,128)(2,1)}, u32[]{:S(2)}, u32[]{:S(2)}) collective-permute-start(bf16[7680,128]{1,0:T(8,128)(2,1)} %get-tuple-element.44), channel_id=1, source_target_pairs={{0,8},{8,0},{1,9},{9,1},{2,10},{10,2},{3,11},{11,3},{4,12},{12,4},... | collective-permute-start | bytes 5898248 | tf_op jit(solution)/shard_map/ppermute | solution.py:793
  55.0 14.8 %all-to-all-start.2 = ((bf16[128,8,128]{2,1,0:T(8,128)(2,1)}), bf16[128,8,128]{2,1,0:T(8,128)(2,1)S(1)}, u32[]{:S(2)}, u32[]{:S(2)}) async-start(bf16[128,8,128]{2,1,0:T(8,128)(2,1)} %get-tuple-element.47), calls=%async_computation.2 | async-start | bytes 524288 | tf_op jit(solution)/shard_map/all_to_all | solution.py:772
  58.9 10.9 %copy-start = (bf16[384,1152]{1,0:T(8,128)(2,1)S(1)}, bf16[384,1152]{1,0:T(8,128)(2,1)}, u32[]{:S(2)}) copy-start(bf16[384,1152]{1,0:T(8,128)(2,1)} %wqkv_ref.3) | copy-start | bytes 2654212
  58.9 10.9 %copy-start.2 = (bf16[16,8,896]{2,1,0:T(8,128)(2,1)S(1)}, bf16[16,8,896]{2,1,0:T(8,128)(2,1)}, u32[]{:S(2)}) copy-start(bf16[16,8,896]{2,1,0:T(8,128)(2,1)} %copy-done.1) | copy-start | bytes 688132
  58.9 10.9 %copy-start.3 = (bf16[384,384]{1,0:T(8,128)(2,1)S(1)}, bf16[384,384]{1,0:T(8,128)(2,1)}, u32[]{:S(2)}) copy-start(bf16[384,384]{1,0:T(8,128)(2,1)} %wout_ref.3) | copy-start | bytes 884740
  58.9 10.9 %copy-start.5 = (bf16[128,1536]{1,0:T(8,128)(2,1)S(1)}, bf16[128,1536]{1,0:T(8,128)(2,1)}, u32[]{:S(2)}) copy-start(bf16[128,1536]{1,0:T(8,128)(2,1)} %get-tuple-element.49.shares_ref) | copy-start | bytes 1179652
  58.9 10.9 %copy-start.6 = (bf16[128,1152]{1,0:T(8,128)(2,1)S(1)}, bf16[128,1152]{1,0:T(8,128)(2,1)}, u32[]{:S(2)}) copy-start(bf16[128,1152]{1,0:T(8,128)(2,1)} %get-tuple-element.48.qkv_ref) | copy-start | bytes 884740
  58.9 10.9 %copy-start.7 = (bf16[128,384]{1,0:T(8,128)(2,1)S(1)}, bf16[128,384]{1,0:T(8,128)(2,1)}, u32[]{:S(2)}) copy-start(bf16[128,384]{1,0:T(8,128)(2,1)} %get-tuple-element.50.mix_ref) | copy-start | bytes 294916
  62.4 19.0 %collective-permute-start.1 = (bf16[3840,128]{1,0:T(8,128)(2,1)}, bf16[3840,128]{1,0:T(8,128)(2,1)S(1)}, u32[]{:S(2)}, u32[]{:S(2)}) collective-permute-start(bf16[3840,128]{1,0:T(8,128)(2,1)} %get-tuple-element.46), channel_id=1, source_target_pairs={{0,2},{1,3},{2,0},{3,1},{4,6},{5,7},{6,4},{7,5},{8,9},{9,8},{10,11... | collective-permute-start | bytes 2949128 | tf_op jit(solution)/shard_map/ppermute | solution.py:795
  69.9 11.6 %copy-start.4 = (bf16[3840,128]{1,0:T(8,128)(2,1)S(1)}, bf16[3840,128]{1,0:T(8,128)(2,1)}, u32[]{:S(2)}) copy-start(bf16[3840,128]{1,0:T(8,128)(2,1)} %get-tuple-element.45.early_ref) | copy-start | bytes 2949124
  73.2 2.1 %collective-permute-start.2 = (bf16[2304,128]{1,0:T(8,128)(2,1)S(1)}, bf16[2304,128]{1,0:T(8,128)(2,1)S(1)}, u32[]{:S(2)}, u32[]{:S(2)}) collective-permute-start(bf16[2304,128]{1,0:T(8,128)(2,1)S(1)} %get-tuple-element.52), channel_id=1, source_target_pairs={{0,8},{8,0},{1,9},{9,1},{2,10},{10,2},{3,11},{11,3},{4,12},{12,4},... | collective-permute-start | bytes 1769480 | tf_op jit(solution)/shard_map/ppermute | solution.py:799
  75.5 5.9 %collective-permute-start.3 = (bf16[1152,128]{1,0:T(8,128)(2,1)S(1)}, bf16[1152,128]{1,0:T(8,128)(2,1)S(1)}, u32[]{:S(2)}, u32[]{:S(2)}) collective-permute-start(bf16[1152,128]{1,0:T(8,128)(2,1)S(1)} %get-tuple-element.54), channel_id=1, source_target_pairs={{0,2},{1,3},{2,0},{3,1},{4,6},{5,7},{6,4},{7,5},{8,9},{9,8},{10,11... | collective-permute-start | bytes 884744 | tf_op jit(solution)/shard_map/ppermute | solution.py:801
  149.3 14.7 %collective-permute-start.4 = (bf16[8,2,2,2,160,128]{5,4,3,2,1,0:T(8,128)(2,1)S(1)}, bf16[8,2,2,2,160,128]{5,4,3,2,1,0:T(8,128)(2,1)}, u32[]{:S(2)}, u32[]{:S(2)}) collective-permute-start(bf16[8,2,2,2,160,128]{5,4,3,2,1,0:T(8,128)(2,1)S(1)} %bitcast.13), channel_id=1, source_target_pairs={{0,8},{8,0},{1,9},{9,1},{2,10},{10,2},{3,11},{11,3},{4,12},{12,4},... | collective-permute-start | bytes 7864328 | tf_op jit(solution)/shard_map/ppermute | solution.py:808
  152.5 11.5 %all-to-all-start.5 = ((bf16[16,8,768]{2,1,0:T(8,128)(2,1)}), bf16[16,8,768]{2,1,0:T(8,128)(2,1)S(1)}, u32[]{:S(2)}, u32[]{:S(2)}) async-start(bf16[16,8,768]{2,1,0:T(8,128)(2,1)} %bitcast.10), calls=%async_computation.5 | async-start | bytes 393216 | tf_op jit(solution)/shard_map/all_to_all | solution.py:772

commit v5 on v4

--- a/solution.py
+++ b/solution.py
@@ -41,20 +41,26 @@
 CHUNK = QUARTER // SHARERS
 
 
-def pair_groups():
+def ring_groups():
     bits = (2, 1)
-    place = lambda line, core, res: (line * 2 + core) * 8 + res
-    spots = [(line, core, res) for line in range(8) for core in range(2) for res in range(8)]
-    pairs = [(place(*spot), place(spot[0], spot[1], spot[2] ^ bits[spot[1]])) for spot in spots]
-    groups = [
-        [place(line, core, res) for line in range(8) for res in range(8) if bool(res & bits[core]) == odd]
-        for core in range(2)
-        for odd in (False, True)
-    ]
-    return pairs, groups
-
-
-PAIRS, GROUPS = pair_groups()
+    rings, groups = ([], []), [[], [], [], []]
+    for line in range(8):
+        for core in range(2):
+            for res in range(8):
+                place = (line * 2 + core) * 8 + res
+                groups[2 * core + bool(res & bits[core])].append(place)
+                for ring, step in zip(rings, (1, 3)):
+                    x, y = res // 2, line % 2 * 2 + res % 2
+                    if core == 0:
+                        x = (x + step) % 4
+                    else:
+                        y = (y + step) % 4
+                    there = ((line // 2 * 2 + y // 2) * 2 + core) * 8 + x * 2 + y % 2
+                    ring.append((place, there))
+    return rings, groups
+
+
+RINGS, GROUPS = ring_groups()
 
 
 def place_units():
@@ -520,6 +526,7 @@
             pltpu.VMEM((N, 3 * C), BF16), pltpu.VMEM((4 * N, N), BF16), pltpu.VMEM((4 * N, N), BF16),
         ],
         compiler_params=limit(20),
+        cost_estimate=pl.CostEstimate(flops=1000, bytes_accessed=1000, transcendentals=0),
         name="time_backward",
     )(core, back, rows, qkv, shares, mix, w_qkv, w_out)
 
@@ -548,16 +555,21 @@
     )(core, weight, rows, *sources)
 
 
-def add_early(side_ref, keep_ref, got_ref, mine_ref, give_ref, one_ref, two_ref, sems):
-    part = EARLY // 2
+def add_early(side_ref, keep_ref, got_ref, give_a_ref, give_b_ref, mine_ref, one_ref, two_ref, sems):
+    part = EARLY // 4
+    give, mine = 2 * (1 - side_ref[0]), 2 * side_ref[0]
+    targets = (
+        (give, give_a_ref), (give + 1, give_b_ref),
+        (mine, mine_ref.at[0:part]), (mine + 1, mine_ref.at[part : 2 * part]),
+    )
     steps = []
-    for step, target in enumerate((give_ref, mine_ref)):
-        start = pl.multiple_of((side_ref[0] if step else 1 - side_ref[0]) * part, part)
+    for step, (index, target) in enumerate(targets):
+        source = pl.ds(pl.multiple_of(index * part, part), part)
         span = slice(step * part, (step + 1) * part)
         steps.append(
             (
-                pltpu.make_async_copy(keep_ref.at[pl.ds(start, part)], one_ref.at[span], sems.at[3 * step]),
-                pltpu.make_async_copy(got_ref.at[pl.ds(start, part)], two_ref.at[span], sems.at[3 * step + 1]),
+                pltpu.make_async_copy(keep_ref.at[source], one_ref.at[span], sems.at[3 * step]),
+                pltpu.make_async_copy(got_ref.at[source], two_ref.at[span], sems.at[3 * step + 1]),
                 pltpu.make_async_copy(one_ref.at[span], target, sems.at[3 * step + 2]),
             )
         )
@@ -576,15 +588,15 @@
 
 
 def call_add_early(side, keep, got):
-    part = like((EARLY // 2, 128), BF16)
+    part = like((EARLY // 4, 128), BF16)
     return pl.pallas_call(
         add_early,
         in_specs=[SMEM, HBM, HBM],
-        out_specs=(HBM, HBM),
-        out_shape=(part, part),
+        out_specs=(HBM, HBM, HBM),
+        out_shape=(part, part, like((EARLY // 2, 128), BF16)),
         scratch_shapes=[
             pltpu.VMEM((EARLY, 128), BF16), pltpu.VMEM((EARLY, 128), BF16),
-            pltpu.SemaphoreType.DMA((6,)),
+            pltpu.SemaphoreType.DMA((12,)),
         ],
         compiler_params=limit(60),
         cost_estimate=pl.CostEstimate(flops=EARLY * 128, bytes_accessed=EARLY * 128 * 6, transcendentals=0),
@@ -592,32 +604,38 @@
     )(side, keep, got)
 
 
-def add_late(side_ref, keep_ref, got_ref, mine_ref, give_ref):
-    part = LATE // 2
-    for ref, index in ((mine_ref, side_ref[0]), (give_ref, 1 - side_ref[0])):
+def add_late(side_ref, keep_ref, got_ref, give_a_ref, give_b_ref, mine_ref):
+    part = LATE // 4
+    give, mine = 2 * (1 - side_ref[0]), 2 * side_ref[0]
+    targets = (
+        (give, give_a_ref, 0), (give + 1, give_b_ref, 0), (mine, mine_ref, 0), (mine + 1, mine_ref, part)
+    )
+    for index, ref, at in targets:
         span = pl.ds(pl.multiple_of(index * part, part), part)
         summed = keep_ref[span, :].astype(F32) + got_ref[span, :].astype(F32)
-        ref[...] = summed.astype(BF16)
+        ref[at : at + part, :] = summed.astype(BF16)
 
 
 def call_add_late(side, keep, got):
-    part = like((LATE // 2, 128), BF16)
+    part = like((LATE // 4, 128), BF16)
     return pl.pallas_call(
         add_late,
         in_specs=[SMEM, VMEM, VMEM],
-        out_shape=(part, part),
+        out_shape=(part, part, like((LATE // 2, 128), BF16)),
         compiler_params=limit(8),
         name="add_late",
     )(side, keep, got)
 
 
-def add_pairs(early_ref, got_early_ref, late_ref, got_late_ref, total_ref):
-    early, late = EARLY // 2, LATE // 2
-    summed = early_ref[...].astype(F32) + got_early_ref[...].astype(F32)
-    total_ref[0:early, :] = summed.astype(BF16)
-    summed = late_ref[...].astype(F32) + got_late_ref[...].astype(F32)
-    total_ref[early : early + late, :] = summed.astype(BF16)
-    total_ref[early + late :, :] = jnp.zeros((QUARTER - early - late, 128), BF16)
+def add_pairs(early_ref, early_a_ref, early_b_ref, late_ref, late_a_ref, late_b_ref, total_ref):
+    at = 0
+    for mine, parts in ((early_ref, (early_a_ref, early_b_ref)), (late_ref, (late_a_ref, late_b_ref))):
+        size = parts[0].shape[0]
+        for k, part in enumerate(parts):
+            summed = mine[k * size : (k + 1) * size, :].astype(F32) + part[...].astype(F32)
+            total_ref[at : at + size, :] = summed.astype(BF16)
+            at += size
+    total_ref[at:, :] = jnp.zeros((QUARTER - at, 128), BF16)
 
 
 def call_add_pairs(*parts):
@@ -638,7 +656,7 @@
 
 def call_add_parts(parts):
     return pl.pallas_call(
-        add_parts, out_shape=like((2 * SHARERS, *parts.shape[1:]), BF16), compiler_params=limit(12),
+        add_parts, out_shape=like(parts.shape, BF16), compiler_params=limit(12),
         name="add_parts",
     )(parts)
 
@@ -658,108 +676,168 @@
         begin += size
 
 
-def unpack_half(own, core_ref, parts_ref, out_refs, held_ref, stage_ref, gain_ref, in_sems, out_sems):
-    for half in range(2):
-
-        @pl.when((core_ref[0] == half) == own)
-        def run(half=half):
-            for q in range(2):
-                for line in range(8):
-                    for high in range(2):
-                        source = (
-                            parts_ref.at[line, high, q] if half == 0 else parts_ref.at[line, high, :, q]
-                        )
-                        target = held_ref.at[q, pl.ds((line * 2 + high) * 2, 2)]
-                        pltpu.make_async_copy(source, target, in_sems.at[q]).start()
-            leaving = []
-            for q in range(2):
-                pltpu.make_async_copy(held_ref.at[q], held_ref.at[q], in_sems.at[q]).wait()
-                for k, name in enumerate(PIECES):
-                    tiles = PIECES[name][1] // 128
-                    for unit, (owner, at) in enumerate(UNITS[name]):
-                        quarter, row = final_spot(name.startswith("time"), at)
-                        if owner != half or quarter != q:
-                            continue
-                        slot = len(leaving)
-                        for chunk, low, size, to in segments(row):
-                            stage_ref[slot, to : to + size, :] = held_ref[
-                                q, chunk, low : low + size, :
-                            ].astype(F32)
-                        down, across = (unit // tiles) * C, (unit % tiles) * 128
-                        rows = GAIN_ROW if name == "ipa_points" else C
-                        if name == "ipa_points" and across == 0:
-                            gain_ref[...] = stage_ref[slot, GAIN_ROW : GAIN_ROW + 1, :]
-                        leaving.append(
-                            pltpu.make_async_copy(
-                                stage_ref.at[slot, 0:rows],
-                                out_refs[k].at[down : down + rows, across : across + 128],
-                                out_sems.at[slot],
-                            )
-                        )
-                        leaving[-1].start()
-            for copy in leaving:
+FETCHES = 4
+
+
+class Quarter:
+    def __init__(self, spot, parts, out_refs, gain_ref, held_ref, stage_ref, in_sems, out_sems):
+        self.spot, self.out_refs, self.gain_ref = spot, out_refs, gain_ref
+        self.held_ref, self.stage_ref, self.out_sems = held_ref, stage_ref, out_sems
+        size = SHARERS // FETCHES
+        each = FETCHES // len(parts)
+        self.fetches = [
+            pltpu.make_async_copy(
+                parts[k // each].at[k % each * size : (k % each + 1) * size],
+                held_ref.at[k * size : (k + 1) * size],
+                in_sems.at[k],
+            )
+            for k in range(FETCHES)
+        ]
+        for copy in self.fetches:
+            copy.start()
+
+    def leaving(self, half, quarter):
+        found = []
+        for k, name in enumerate(PIECES):
+            tiles = PIECES[name][1] // 128
+            for unit, (owner, at) in enumerate(UNITS[name]):
+                where, row = final_spot(name.startswith("time"), at)
+                if (owner, where) != (half, quarter):
+                    continue
+                down, across = (unit // tiles) * C, (unit % tiles) * 128
+                rows = GAIN_ROW if name == "ipa_points" else C
+                slot = len(found)
+                copy = pltpu.make_async_copy(
+                    self.stage_ref.at[slot, 0:rows],
+                    self.out_refs[k].at[down : down + rows, across : across + 128],
+                    self.out_sems.at[slot],
+                )
+                found.append((row, copy, name == "ipa_points" and across == 0))
+        return found
+
+    def each(self, act):
+        for half in range(2):
+            for quarter in range(2):
+                pl.when(self.spot == 2 * half + quarter)(lambda h=half, q=quarter: act(h, q))
+
+    def send(self):
+        def act(half, quarter):
+            waited = 0
+            for slot, (row, copy, gains) in enumerate(self.leaving(half, quarter)):
+                for chunk, low, size, to in segments(row):
+                    while waited * (SHARERS // FETCHES) <= chunk:
+                        self.fetches[waited].wait()
+                        waited += 1
+                    self.stage_ref[slot, to : to + size, :] = self.held_ref[
+                        chunk, low : low + size, :
+                    ].astype(F32)
+                copy.start()
+                if gains:
+                    self.gain_ref[...] += self.stage_ref[slot, GAIN_ROW : GAIN_ROW + 1, :]
+            for copy in self.fetches[waited:]:
                 copy.wait()
 
-
-def unpack_own(core_ref, parts_ref, *refs):
-    gain_ref = refs[7]
+        self.each(act)
+
+    def finish(self):
+        def act(half, quarter):
+            for _, copy, _ in self.leaving(half, quarter):
+                copy.wait()
+
+        self.each(act)
+
+
+def unpack_first(spots_ref, own_ref, swapped_ref, *refs):
+    out_refs, gain_ref = refs[:7], refs[7]
     gain_ref[...] = jnp.zeros((1, 128), F32)
-    unpack_half(True, core_ref, parts_ref, refs[:7], refs[8], refs[9], gain_ref, refs[10], refs[11])
-
-
-def unpack_other(core_ref, parts_ref, gain_own_ref, ended_ref, *refs):
+    quarters = [
+        Quarter(spots_ref[0], (own_ref,), out_refs, gain_ref, *refs[8:12]),
+        Quarter(spots_ref[1], (swapped_ref,), out_refs, gain_ref, *refs[12:16]),
+    ]
+    for quarter in quarters:
+        quarter.send()
+    for quarter in quarters:
+        quarter.finish()
+
+
+def unpack_second(spots_ref, part_a_ref, part_b_ref, gain_in_ref, *refs):
+    out_refs, gain_ref = refs[7:14], refs[14]
+    gain_ref[...] = gain_in_ref[...]
+    quarter = Quarter(spots_ref[2], (part_a_ref, part_b_ref), out_refs, gain_ref, *refs[15:19])
+    quarter.send()
+    quarter.finish()
+
+
+def unpack_last(spots_ref, part_a_ref, part_b_ref, gain_in_ref, ended_ref, *refs):
     out_refs, gain_ref, output_ref, token_ref = refs[7:14], refs[14], refs[15], refs[16]
-    held_ref, stage_ref, part_ref, in_sems, out_sems = refs[17:]
+    total_ref = refs[17]
+    total_ref[...] = gain_in_ref[...]
+    quarter = Quarter(spots_ref[3], (part_a_ref, part_b_ref), out_refs, total_ref, *refs[18:22])
     residues, frames, _ = ended_ref.shape
     ended = mm(order_matrix(), ended_ref[...].reshape(N, 2 * C)).astype(BF16)
     token_ref[...] = ended[:, 0:C].reshape(frames, residues, C)
     output_ref[...] = ended[:, C:].reshape(frames, residues, C)
-    part_ref[...] = jnp.zeros((1, 128), F32)
-    unpack_half(False, core_ref, parts_ref, out_refs, held_ref, stage_ref, part_ref, in_sems, out_sems)
-    gain = gain_own_ref[...] + part_ref[...]
+    quarter.send()
     lane = lax.broadcasted_iota(jnp.int32, (1, 128), 1)
     for h in range(H):
-        gain_ref[h] = jnp.sum(jnp.where(lane == h, gain, 0.0))
+        gain_ref[h] = jnp.sum(jnp.where(lane == h, total_ref[...], 0.0))
+    quarter.finish()
 
 
 OUTS = [
-    (GAIN_ROW if name == "ipa_points" else rows, columns) for name, (rows, columns) in PIECES.items()
+    like((GAIN_ROW if name == "ipa_points" else rows, columns), F32)
+    for name, (rows, columns) in PIECES.items()
 ]
-UNPACK_SCRATCH = [
-    pltpu.VMEM((2, SHARERS, CHUNK, 128), BF16),
-    pltpu.VMEM((EARLY_UNITS[0] + LATE_UNITS[0], C, 128), F32),
+MOST = (EARLY_UNITS[0] + LATE_UNITS[0]) // 2
+QUARTER_SCRATCH = [
+    pltpu.VMEM((SHARERS, CHUNK, 128), BF16),
+    pltpu.VMEM((MOST, C, 128), F32),
+    pltpu.SemaphoreType.DMA((FETCHES,)),
+    pltpu.SemaphoreType.DMA((MOST,)),
 ]
-UNPACK_SEMS = [
-    pltpu.SemaphoreType.DMA((2,)), pltpu.SemaphoreType.DMA((EARLY_UNITS[0] + LATE_UNITS[0],)),
-]
-
-
-def call_unpack_own(core, parts):
-    return pl.pallas_call(
-        unpack_own,
-        in_specs=[SMEM, HBM],
+COST = pl.CostEstimate(flops=0, bytes_accessed=8 * MEGA, transcendentals=0)
+
+
+def call_unpack_first(spots, own, swapped):
+    return pl.pallas_call(
+        unpack_first,
+        in_specs=[SMEM, HBM, HBM],
         out_specs=(*[HBM] * 7, VMEM),
-        out_shape=(*[like(shape, F32) for shape in OUTS], like((1, 128), F32)),
-        scratch_shapes=UNPACK_SCRATCH + UNPACK_SEMS,
+        out_shape=(*OUTS, like((1, 128), F32)),
+        scratch_shapes=QUARTER_SCRATCH * 2,
         compiler_params=limit(20),
-        cost_estimate=pl.CostEstimate(flops=0, bytes_accessed=8 * MEGA, transcendentals=0),
-        name="unpack_own",
-    )(core, parts)
-
-
-def call_unpack_other(core, parts, gain, ended, grads):
+        cost_estimate=COST,
+        name="unpack_first",
+    )(spots, own, swapped)
+
+
+def call_unpack_second(spots, parts, gain, grads):
+    return pl.pallas_call(
+        unpack_second,
+        in_specs=[SMEM, HBM, HBM, VMEM] + [HBM] * 7,
+        out_specs=(*[HBM] * 7, VMEM),
+        out_shape=(*OUTS, like((1, 128), F32)),
+        scratch_shapes=QUARTER_SCRATCH,
+        input_output_aliases={4 + k: k for k in range(7)},
+        compiler_params=limit(20),
+        cost_estimate=COST,
+        name="unpack_second",
+    )(spots, *parts, gain, *grads)
+
+
+def call_unpack_last(spots, parts, gain, ended, grads):
     residues, frames, _ = ended.shape
     rows = like((frames, residues, C), BF16)
     return pl.pallas_call(
-        unpack_other,
-        in_specs=[SMEM, HBM, VMEM, VMEM] + [HBM] * 7,
+        unpack_last,
+        in_specs=[SMEM, HBM, HBM, VMEM, VMEM] + [HBM] * 7,
         out_specs=(*[HBM] * 7, SMEM, VMEM, VMEM),
-        out_shape=(*[like(shape, F32) for shape in OUTS], like((H,), F32), rows, rows),
-        scratch_shapes=UNPACK_SCRATCH + [pltpu.VMEM((1, 128), F32)] + UNPACK_SEMS,
-        input_output_aliases={4 + k: k for k in range(7)},
+        out_shape=(*OUTS, like((H,), F32), rows, rows),
+        scratch_shapes=[pltpu.VMEM((1, 128), F32)] + QUARTER_SCRATCH,
+        input_output_aliases={5 + k: k for k in range(7)},
         compiler_params=limit(20),
-        name="unpack_other",
-    )(core, parts, gain, ended, *grads)
+        name="unpack_last",
+    )(spots, *parts, gain, ended, *grads)
 
 
 def repeat_points(weight):
@@ -770,6 +848,16 @@
 
 def swap_rows(rows, axes):
     return lax.all_to_all(rows, axes, split_axis=0, concat_axis=0, tiled=True)
+
+
+def both_ways(parts):
+    return [lax.ppermute(part, EVERYONE, ring) for part, ring in zip(parts, RINGS)]
+
+
+def share(parts):
+    return lax.all_to_all(
+        parts, EVERYONE, split_axis=0, concat_axis=0, tiled=True, axis_index_groups=GROUPS
+    )
 
 
 def body(
@@ -780,7 +868,12 @@
     place = lax.axis_index(("line", "core")).astype(jnp.int32).reshape(1)
     core = lax.axis_index("core").astype(jnp.int32).reshape(1)
     place_res = lax.axis_index("res").astype(jnp.int32)
-    side = jnp.where(core == 0, (place_res >> 1) & 1, place_res & 1)
+    sides = jnp.stack([(place_res >> 1) & 1, place_res & 1])
+    side = jnp.where(core == 0, sides[0], sides[1])
+    far = jnp.where(core == 0, sides[1], sides[0])
+    spots = jnp.concatenate(
+        [2 * core + side, 2 - 2 * core + far, 2 * core + 1 - side, 2 - 2 * core + 1 - far]
+    )
     swap = [(0, 1), (1, 0)]
     points = w_ipa_points.T
     rows = swap_rows(call_pack_rows(tokens, cotangent, rigid_frames), ("line", "core"))
@@ -791,24 +884,26 @@
         w_ipa_out, w_up, w_down,
     )
     got_early = lax.ppermute(give_early, "core", swap)
-    mine_early, give_early = call_add_early(side, keep_early, got_early)
-    got_early = lax.ppermute(give_early, EVERYONE, PAIRS)
+    *give_early, mine_early = call_add_early(side, keep_early, got_early)
+    got_early = both_ways(give_early)
+    back, _ = lax.optimization_barrier((swap_rows(back, EVERYONE), give_early))
     ended, keep_late, give_late = call_time_backward(
-        core, swap_rows(back, EVERYONE), rows, qkv, shares, mix, w_time_qkv, w_time_out
+        core, back, rows, qkv, shares, mix, w_time_qkv, w_time_out
     )
     got_late = lax.ppermute(give_late, "core", swap)
-    mine_late, give_late = call_add_late(side, keep_late, got_late)
-    got_late = lax.ppermute(give_late, EVERYONE, PAIRS)
-    total = call_add_pairs(mine_early, got_early, mine_late, got_late)
-    parts = lax.all_to_all(
-        total.reshape(SHARERS, CHUNK, 128), EVERYONE, split_axis=0, concat_axis=0, tiled=True,
-        axis_index_groups=GROUPS,
-    )
-    own = swap_rows(call_add_parts(parts), ("line", "res")).reshape(8, 2, 2, 2, CHUNK, 128)
-    other = lax.ppermute(own, "core", swap)
+    *give_late, mine_late = call_add_late(side, keep_late, got_late)
+    got_late = both_ways(give_late)
+    total = call_add_pairs(mine_early, *got_early, mine_late, *got_late)
+    parts = share(total.reshape(SHARERS, CHUNK, 128))
+    own = share(call_add_parts(parts))
+    paired = both_ways((own[: SHARERS // 2], own[SHARERS // 2 :]))
+    swapped = lax.ppermute(own, "core", swap)
     ended = swap_rows(ended.reshape(residues, frames, 2 * C), ("line", "core"))
-    *grads, gain = call_unpack_own(core, own)
-    *grads, gain, output, token_grad = call_unpack_other(core, other, gain, ended, grads)
+    *grads, gain = call_unpack_first(spots, own, swapped)
+    paired, ended, gain = lax.optimization_barrier((paired, ended, gain))
+    last = [lax.ppermute(part, "core", swap) for part in paired]
+    *grads, gain = call_unpack_second(spots, paired, gain, grads)
+    *grads, gain, output, token_grad = call_unpack_last(spots, last, gain, ended, grads)
     grads = dict(zip(PIECES, grads))
     return (
         output, token_grad, grads["time_qkv"], grads["time_out"], grads["ipa_qkv"],

time: 169 us -> 162 us (0.959)
  blocking collectives: 67.3 us -> 48.4 us
  starting transfers between devices: 28.1 us -> 37.5 us
  local copies, waits for them, and re-layouts: 1.42 us -> 3.88 us
    all_to_all x2, blocking collectives: 67.3 us -> 48.4 us  [share(): lax.all_to_all(parts, EVERYONE, split_axis=0, concat_axis=0, tiled=True,...]
    ppermute x3 -> x9, starting transfers between devices: 5.17 us -> 13.1 us  [the longest x6 6.88 us: both_ways(): lax.ppermute(part, EVERYONE, ring)]
    pallas_call x4 -> x5, Pallas kernels: 12.5 us -> 13.9 us  [the longest x1 3.96 us: call_unpack_first(): pl.pallas_call(unpack_first, in_specs=[SMEM, HBM, HBM], out_specs=(*[HBM]...]
    ppermute x3 -> x9, waiting for transfers between devices: 5.53 us -> 5.21 us  [the longest x6 5.2 us: both_ways(): lax.ppermute(part, EVERYONE, ring)]
  transfers between devices with their start and end apart: 9 -> 15, of which waited for: 7 -> 6; matrix products, arithmetic and copies ran while one was open for 1% -> 1% of each run, Pallas kernels for 7% -> 6%
where the time goes in v5:
time: 162 us
  blocking collectives  48.4 us (30%)
  starting transfers between devices  37.5 us (23%)
  Pallas kernels  35.4 us (22%)
  waiting for transfers between devices  34.2 us (21%)
  local copies, waits for them, and re-layouts  3.88 us (2%)
    all_to_all x2, blocking collectives, share(): lax.all_to_all(parts, EVERYONE, split_axis=0, concat_axis=0, tiled=True,...  48.4 us
    all_to_all x4, waiting for transfers between devices, swap_rows(): return lax.all_to_all(rows, axes, split_axis=0, concat_axis=0, tiled=True)  29 us
    all_to_all x4, starting transfers between devices, swap_rows(): return lax.all_to_all(rows, axes, split_axis=0, concat_axis=0, tiled=True)  23.3 us
    pallas_call x1, Pallas kernels, call_point_attention(): pl.pallas_call(point_attention, in_specs=[SMEM, SMEM, VMEM] + [HBM] * len...  12.2 us
    ppermute x6, starting transfers between devices, both_ways(): lax.ppermute(part, EVERYONE, ring)  6.88 us
    ppermute x1, starting transfers between devices, body(): swapped = lax.ppermute(own, 'core', swap)  5.3 us
    ppermute x6, waiting for transfers between devices, both_ways(): lax.ppermute(part, EVERYONE, ring)  5.2 us
    pallas_call x1, Pallas kernels, call_time_forward(): pl.pallas_call(time_forward, in_specs=[SMEM, SMEM, VMEM, VMEM, VMEM], out...  4.03 us
  transfers between devices with their start and end apart: 15, of which 6 were waited for; matrix products, arithmetic and copies ran while one was open for 1% of the time, Pallas kernels for 6%

profile of v5, /device:TPU:1, one launch (start us, length us, event | category | flops | bytes accessed | tf_op | source)
XLA Modules:
  0.0 161.6 jit_solution(15320761798503122987)
XLA Ops:
  0.6 0.0 copy-start.11
  0.7 2.0 %pack_rows.1 = bf16[16,8,896]{2,1,0:T(8,128)(2,1)} custom-call(bf16[8,16,384]{2,1,0:T(8,128)(2,1)} %tokens_ref.1, bf16[8,16,384]{2,1,0:T(8,128)(2,1)} %cotangent_ref.1, bf16[12,8,16]{2,1,0:T(8,128)(2,1)} %rigid_ref.1), custom_call_target="tpu_custom_call" | custom-call | tf_op jit(solution)/shard_map/pack_rows/pallas_call | solution.py:499
  2.6 9.5 %all-to-all-start = ((bf16[16,8,896]{2,1,0:T(8,128)(2,1)}), bf16[16,8,896]{2,1,0:T(8,128)(2,1)S(1)}, u32[]{:S(2)}, u32[]{:S(2)}) async-start(bf16[16,8,896]{2,1,0:T(8,128)(2,1)} %pack_rows.1), calls=%async_computation | async-start | bytes 458752 | tf_op jit(solution)/shard_map/all_to_all | solution.py:850
  12.1 8.4 %all-to-all-done = bf16[16,8,896]{2,1,0:T(8,128)(2,1)S(1)} async-done(((bf16[16,8,896]{2,1,0:T(8,128)(2,1)}), bf16[16,8,896]{2,1,0:T(8,128)(2,1)S(1)}, u32[]{:S(2)}, u32[]{:S(2)}) %all-to-all-start) | async-done | bytes 229408 | tf_op jit(solution)/shard_map/all_to_all | solution.py:850
  20.5 0.7 copy-done.1
  21.2 4.0 %time_forward.1 = (bf16[128,8,128]{2,1,0:T(8,128)(2,1)}, bf16[128,1152]{1,0:T(8,128)(2,1)}, bf16[128,1536]{1,0:T(8,128)(2,1)}, bf16[128,384]{1,0:T(8,128)(2,1)}) custom-call(s32[1]{0:T(128)} %bitcast.3.place_ref, s32[16,32]{1,0:T(8,128)} %neighbors_ref.1, bf16[128,896]{1,0:T(8,128)(2,1)} %bitcast.13, bf16[384,1152]{1,0:T(8,128)(2,1)} %wqkv_ref.3, ...), custom_call_target="tpu_custom_call" | custom-call | tf_op jit(solution)/shard_map/time_forward/pallas_call | solution.py:508
  25.2 5.2 %all-to-all-start.1 = ((bf16[128,8,128]{2,1,0:T(8,128)(2,1)}), bf16[128,8,128]{2,1,0:T(8,128)(2,1)S(1)}, u32[]{:S(2)}, u32[]{:S(2)}) async-start(bf16[128,8,128]{2,1,0:T(8,128)(2,1)} %get-tuple-element.57), calls=%async_computation.1 | async-start | bytes 524288 | tf_op jit(solution)/shard_map/all_to_all | solution.py:850
  30.4 0.0 copy-done.11
  30.4 1.1 fusion.4
  31.5 9.9 %all-to-all-done.1.rows_ref = bf16[128,8,128]{2,1,0:T(8,128)(2,1)S(1)} async-done(((bf16[128,8,128]{2,1,0:T(8,128)(2,1)}), bf16[128,8,128]{2,1,0:T(8,128)(2,1)S(1)}, u32[]{:S(2)}, u32[]{:S(2)}) %all-to-all-start.1) | async-done | bytes 262176 | tf_op jit(solution)/shard_map/all_to_all | solution.py:850
  41.4 0.7 copy-done.10
  42.2 12.2 %point_attention.1 = (bf16[128,8,128]{2,1,0:T(8,128)(2,1)}, bf16[7680,128]{1,0:T(8,128)(2,1)}, bf16[7680,128]{1,0:T(8,128)(2,1)}) custom-call(s32[1]{0:T(128)} %bitcast.core_ref, f32[12]{0:T(128)} %weight_ref.1, bf16[128,8,128]{2,1,0:T(8,128)(2,1)} %copy-done.10, bf16[384,1152]{1,0:T(8,128)(2,1)} %refs_0_.1, bf16[128,1024]{1,0:T(8,128)(2,1)} %constant.37.clone.refs_1_, ...), custom_call_target="tpu_custom_call" | custom-call | tf_op jit(solution)/shard_map/point_attention/pallas_call | solution.py:537
  54.4 0.6 collective-permute-start
  55.0 3.8 %all-to-all-start.2 = ((bf16[128,8,128]{2,1,0:T(8,128)(2,1)}), bf16[128,8,128]{2,1,0:T(8,128)(2,1)S(1)}, u32[]{:S(2)}, u32[]{:S(2)}) async-start(bf16[128,8,128]{2,1,0:T(8,128)(2,1)} %get-tuple-element.63), calls=%async_computation.2 | async-start | bytes 524288 | tf_op jit(solution)/shard_map/all_to_all | solution.py:850
  58.8 0.0 collective-permute-done.got_ref
  58.8 0.0 copy-start.9
  58.8 1.3 copy-done.9
  60.0 0.0 copy-start.6
  60.1 0.0 copy-start.8
  60.1 3.2 %add_early.1 = (bf16[1920,128]{1,0:T(8,128)(2,1)}, bf16[1920,128]{1,0:T(8,128)(2,1)}, bf16[3840,128]{1,0:T(8,128)(2,1)}) custom-call(s32[1]{0:T(128)S(6)} %select_n.7.side_ref, bf16[7680,128]{1,0:T(8,128)(2,1)} %get-tuple-element.58.keep_ref, bf16[7680,128]{1,0:T(8,128)(2,1)} %copy-done.9), custom_call_target="tpu_custom_call" | custom-call | flops 983040 | bytes 5898240 | tf_op jit(solution)/shard_map/add_early/pallas_call | solution.py:592
  63.3 0.0 copy-start.13
  63.3 0.0 copy-start.12
  63.3 6.5 %all-to-all-done.2.back_ref = bf16[128,8,128]{2,1,0:T(8,128)(2,1)S(1)} async-done(((bf16[128,8,128]{2,1,0:T(8,128)(2,1)}), bf16[128,8,128]{2,1,0:T(8,128)(2,1)S(1)}, u32[]{:S(2)}, u32[]{:S(2)}) %all-to-all-start.2) | async-done | bytes 262176 | tf_op jit(solution)/shard_map/all_to_all | solution.py:850
  69.8 0.0 copy-done
  69.8 0.0 copy-done.2
  69.8 0.0 copy-done.3
  69.8 0.0 copy-done.5
  69.8 0.0 copy-done.6
  69.8 0.0 copy-done.8
  69.8 0.0 copy-start.4
  69.8 2.8 %time_backward.1 = (bf16[128,768]{1,0:T(8,128)(2,1)S(1)}, bf16[2304,128]{1,0:T(8,128)(2,1)S(1)}, bf16[2304,128]{1,0:T(8,128)(2,1)S(1)}) custom-call(s32[1]{0:T(128)} %bitcast.core_ref, bf16[128,8,128]{2,1,0:T(8,128)(2,1)S(1)} %all-to-all-done.2.back_ref, bf16[128,896]{1,0:T(8,128)(2,1)S(1)} %bitcast.14, bf16[128,1152]{1,0:T(8,128)(2,1)S(1)} %copy-done.6, ...), custom_call_target="tpu_custom_call" | custom-call | flops 1000 | bytes 1000 | tf_op jit(solution)/shard_map/time_backward/pallas_call | solution.py:521
  72.7 0.0 copy-start.7
  72.7 0.6 collective-permute-start.3
  73.3 0.4 collective-permute-start.1
  73.6 2.3 %collective-permute-start.2 = (bf16[1920,128]{1,0:T(8,128)(2,1)S(1)}, bf16[1920,128]{1,0:T(8,128)(2,1)S(1)}, u32[]{:S(2)}, u32[]{:S(2)}) collective-permute-start(bf16[1920,128]{1,0:T(8,128)(2,1)S(1)} %copy-done.12), channel_id=1, source_target_pairs={{0,6},{1,7},{2,0},{3,1},{4,2},{5,3},{6,4},{7,5},{8,25},{9,8},{10,2... | collective-permute-start | bytes 1474568 | tf_op jit(solution)/shard_map/ppermute | solution.py:854
  76.0 0.0 collective-permute-done.3.got_ref
  76.0 0.1 add_late.1
  76.1 0.1 collective-permute-start.4
  76.2 2.7 %collective-permute-start.5 = (bf16[576,128]{1,0:T(8,128)(2,1)S(1)}, bf16[576,128]{1,0:T(8,128)(2,1)S(1)}, u32[]{:S(2)}, u32[]{:S(2)}) collective-permute-start(bf16[576,128]{1,0:T(8,128)(2,1)S(1)} %get-tuple-element.72), channel_id=1, source_target_pairs={{0,6},{1,7},{2,0},{3,1},{4,2},{5,3},{6,4},{7,5},{8,25},{9,8},{10,2... | collective-permute-start | bytes 442376 | tf_op jit(solution)/shard_map/ppermute | solution.py:854
  78.8 3.6 %collective-permute-done.1.early_a_ref = bf16[1920,128]{1,0:T(8,128)(2,1)S(1)} collective-permute-done((bf16[1920,128]{1,0:T(8,128)(2,1)S(1)}, bf16[1920,128]{1,0:T(8,128)(2,1)S(1)}, u32[]{:S(2)}, u32[]{:S(2)}) %collective-permute-start.1) | collective-permute-done | bytes 491552 | tf_op jit(solution)/shard_map/ppermute | solution.py:854
  82.5 0.0 collective-permute-done.2.early_b_ref
  82.5 1.6 collective-permute-done.4.late_a_ref
  84.0 0.0 collective-permute-done.5.late_b_ref
  84.0 0.3 add_pairs.1
  84.4 24.4 %all_to_all.30.parts_ref = bf16[32,160,128]{2,1,0:T(8,128)(2,1)S(1)} all-to-all(bf16[32,160,128]{2,1,0:T(8,128)(2,1)S(1)} %bitcast.12), channel_id=1, replica_groups={{0,1,4,5,16,17,20,21,32,33,36,37,48,49,52,53,64,65,68,69,80,81,84,85,96..., dimensions={0} | all-to-all | bytes 2621440 | tf_op jit(solution)/shard_map/all_to_all | solution.py:858
  108.7 0.2 add_parts.1
  108.9 24.0 %all_to_all.31.own_ref = bf16[32,160,128]{2,1,0:T(8,128)(2,1)S(1)} all-to-all(bf16[32,160,128]{2,1,0:T(8,128)(2,1)S(1)} %add_parts.1), channel_id=1, replica_groups={{0,1,4,5,16,17,20,21,32,33,36,37,48,49,52,53,64,65,68,69,80,81,84,85,96..., dimensions={0} | all-to-all | bytes 2621440 | tf_op jit(solution)/shard_map/all_to_all | solution.py:858
  132.9 5.3 %collective-permute-start.8 = (bf16[32,160,128]{2,1,0:T(8,128)(2,1)S(1)}, bf16[32,160,128]{2,1,0:T(8,128)(2,1)S(1)}, u32[]{:S(2)}, u32[]{:S(2)}) collective-permute-start(bf16[32,160,128]{2,1,0:T(8,128)(2,1)S(1)} %all_to_all.31.own_ref), channel_id=1, source_target_pairs={{0,8},{8,0},{1,9},{9,1},{2,10},{10,2},{3,11},{11,3},{4,12},{12,4},... | collective-permute-start | bytes 3932168 | tf_op jit(solution)/shard_map/ppermute | solution.py:900
  138.2 1.2 fusion.5
  139.4 1.0 collective-permute-start.7
  140.4 0.5 collective-permute-start.6
  140.9 4.9 %all-to-all-start.5 = ((bf16[16,8,768]{2,1,0:T(8,128)(2,1)}), bf16[16,8,768]{2,1,0:T(8,128)(2,1)S(1)}, u32[]{:S(2)}, u32[]{:S(2)}) async-start(bf16[16,8,768]{2,1,0:T(8,128)(2,1)} %bitcast.15), calls=%async_computation.5 | async-start | bytes 393216 | tf_op jit(solution)/shard_map/all_to_all | solution.py:850
  145.8 0.1 pad_add_fusion.spots_ref
  145.9 0.0 collective-permute-done.8.swapped_ref
  145.9 4.0 %unpack_first.1 = (f32[384,1536]{1,0:T(8,128)}, f32[384,384]{1,0:T(8,128)}, f32[288,384]{1,0:T(8,128)}, f32[384,1152]{1,0:T(8,128)}, f32[1536,384]{1,0:T(8,128)}...) custom-call(s32[4]{0:T(128)S(1)} %pad_add_fusion.spots_ref, ...), custom_call_target="tpu_custom_call" | custom-call | bytes 8388608 | tf_op jit(solution)/shard_map/unpack_first/pallas_call | solution.py:802
  149.9 4.1 %all-to-all-done.5.ended_ref = bf16[16,8,768]{2,1,0:T(8,128)(2,1)S(1)} async-done(((bf16[16,8,768]{2,1,0:T(8,128)(2,1)}), bf16[16,8,768]{2,1,0:T(8,128)(2,1)S(1)}, u32[]{:S(2)}, u32[]{:S(2)}) %all-to-all-start.5) | async-done | bytes 196640 | tf_op jit(solution)/shard_map/all_to_all | solution.py:850
  154.0 0.0 collective-permute-done.7.part_b_ref
  154.0 0.0 collective-permute-done.6.part_a_ref
  154.0 0.8 collective-permute-start.9
  154.8 0.1 collective-permute-start.10
  154.9 3.1 %unpack_second.1 = (f32[384,1536]{1,0:T(8,128)}, f32[384,384]{1,0:T(8,128)}, f32[288,384]{1,0:T(8,128)}, f32[384,1152]{1,0:T(8,128)}, f32[1536,384]{1,0:T(8,128)...) custom-call(s32[4]{0:T(128)S(1)} %pad_add_fusion.spots_ref, ...), custom_call_target="tpu_custom_call", output_to_operand_aliasing={{0}: (4, {}), {1}: (5, {}), {2}: (6, {}), {3}: (7, {}), {4}... | custom-call | bytes 8388608 | tf_op jit(solution)/shard_map/unpack_second/pallas_call | solution.py:815
  158.0 0.0 collective-permute-done.9.part_a_ref
  158.0 0.0 collective-permute-done.10.part_b_ref
  158.0 3.5 %unpack_last.1 = (f32[384,1536]{1,0:T(8,128)}, f32[384,384]{1,0:T(8,128)}, f32[288,384]{1,0:T(8,128)}, f32[384,1152]{1,0:T(8,128)}, f32[1536,384]{1,0:T(8,128)},...) custom-call(s32[4]{0:T(128)S(1)} %pad_add_fusion.spots_ref, ...), custom_call_target="tpu_custom_call", output_to_operand_aliasing={{0}: (5, {}), {1}: (6, {}), {2}: (7, {}), {3}: (8, {}), {4}... | custom-call | tf_op jit(solution)/shard_map/unpack_last/pallas_call | solution.py:831
  (10 shorter events, 0.0 us)
Async XLA Ops:
  0.6 29.8 %copy-start.11 = (bf16[384,288]{0,1:T(8,128)(2,1)S(1)}, bf16[384,288]{0,1:T(8,128)(2,1)}, u32[]{:S(2)}) copy-start(bf16[384,288]{0,1:T(8,128)(2,1)} %param.22) | copy-start | bytes 663556
  2.6 17.9 %all-to-all-start = ((bf16[16,8,896]{2,1,0:T(8,128)(2,1)}), bf16[16,8,896]{2,1,0:T(8,128)(2,1)S(1)}, u32[]{:S(2)}, u32[]{:S(2)}) async-start(bf16[16,8,896]{2,1,0:T(8,128)(2,1)} %pack_rows.1), calls=%async_computation | async-start | bytes 458752 | tf_op jit(solution)/shard_map/all_to_all | solution.py:850
  20.5 0.7 copy-start.1
  25.2 16.2 %all-to-all-start.1 = ((bf16[128,8,128]{2,1,0:T(8,128)(2,1)}), bf16[128,8,128]{2,1,0:T(8,128)(2,1)S(1)}, u32[]{:S(2)}, u32[]{:S(2)}) async-start(bf16[128,8,128]{2,1,0:T(8,128)(2,1)} %get-tuple-element.57), calls=%async_computation.1 | async-start | bytes 524288 | tf_op jit(solution)/shard_map/all_to_all | solution.py:850
  41.4 0.7 copy-start.10
  54.4 4.4 %collective-permute-start = (bf16[7680,128]{1,0:T(8,128)(2,1)}, bf16[7680,128]{1,0:T(8,128)(2,1)S(1)}, u32[]{:S(2)}, u32[]{:S(2)}) collective-permute-start(bf16[7680,128]{1,0:T(8,128)(2,1)} %get-tuple-element.59), channel_id=1, source_target_pairs={{0,8},{8,0},{1,9},{9,1},{2,10},{10,2},{3,11},{11,3},{4,12},{12,4},... | collective-permute-start | bytes 5898248 | tf_op jit(solution)/shard_map/ppermute | solution.py:886
  55.0 14.8 %all-to-all-start.2 = ((bf16[128,8,128]{2,1,0:T(8,128)(2,1)}), bf16[128,8,128]{2,1,0:T(8,128)(2,1)S(1)}, u32[]{:S(2)}, u32[]{:S(2)}) async-start(bf16[128,8,128]{2,1,0:T(8,128)(2,1)} %get-tuple-element.63), calls=%async_computation.2 | async-start | bytes 524288 | tf_op jit(solution)/shard_map/all_to_all | solution.py:850
  58.8 1.3 copy-start.9
  60.0 9.7 %copy-start = (bf16[384,1152]{1,0:T(8,128)(2,1)S(1)}, bf16[384,1152]{1,0:T(8,128)(2,1)}, u32[]{:S(2)}) copy-start(bf16[384,1152]{1,0:T(8,128)(2,1)} %wqkv_ref.3) | copy-start | bytes 2654212
  60.0 9.7 %copy-start.2 = (bf16[16,8,896]{2,1,0:T(8,128)(2,1)S(1)}, bf16[16,8,896]{2,1,0:T(8,128)(2,1)}, u32[]{:S(2)}) copy-start(bf16[16,8,896]{2,1,0:T(8,128)(2,1)} %copy-done.1) | copy-start | bytes 688132
  60.0 9.7 %copy-start.3 = (bf16[384,384]{1,0:T(8,128)(2,1)S(1)}, bf16[384,384]{1,0:T(8,128)(2,1)}, u32[]{:S(2)}) copy-start(bf16[384,384]{1,0:T(8,128)(2,1)} %wout_ref.3) | copy-start | bytes 884740
  60.0 9.8 %copy-start.5 = (bf16[128,1536]{1,0:T(8,128)(2,1)S(1)}, bf16[128,1536]{1,0:T(8,128)(2,1)}, u32[]{:S(2)}) copy-start(bf16[128,1536]{1,0:T(8,128)(2,1)} %get-tuple-element.66.shares_ref) | copy-start | bytes 1179652
  60.0 9.8 %copy-start.6 = (bf16[128,1152]{1,0:T(8,128)(2,1)S(1)}, bf16[128,1152]{1,0:T(8,128)(2,1)}, u32[]{:S(2)}) copy-start(bf16[128,1152]{1,0:T(8,128)(2,1)} %get-tuple-element.65.qkv_ref) | copy-start | bytes 884740
  60.1 9.8 %copy-start.8 = (bf16[128,384]{1,0:T(8,128)(2,1)S(1)}, bf16[128,384]{1,0:T(8,128)(2,1)}, u32[]{:S(2)}) copy-start(bf16[128,384]{1,0:T(8,128)(2,1)} %get-tuple-element.67.mix_ref) | copy-start | bytes 294916
  63.3 10.0 %copy-start.13 = (bf16[1920,128]{1,0:T(8,128)(2,1)S(1)}, bf16[1920,128]{1,0:T(8,128)(2,1)}, u32[]{:S(2)}) copy-start(bf16[1920,128]{1,0:T(8,128)(2,1)} %get-tuple-element.61) | copy-start | bytes 1474564
  63.3 10.3 %copy-start.12 = (bf16[1920,128]{1,0:T(8,128)(2,1)S(1)}, bf16[1920,128]{1,0:T(8,128)(2,1)}, u32[]{:S(2)}) copy-start(bf16[1920,128]{1,0:T(8,128)(2,1)} %get-tuple-element.62) | copy-start | bytes 1474564
  69.8 14.2 %copy-start.4 = (bf16[3840,128]{1,0:T(8,128)(2,1)S(1)}, bf16[3840,128]{1,0:T(8,128)(2,1)}, u32[]{:S(2)}) copy-start(bf16[3840,128]{1,0:T(8,128)(2,1)} %get-tuple-element.60.early_ref) | copy-start | bytes 2949124
  72.7 11.7 %copy-start.7 = (bf16[128,768]{1,0:T(8,128)(2,1)}, bf16[128,768]{1,0:T(8,128)(2,1)S(1)}, u32[]{:S(2)}) copy-start(bf16[128,768]{1,0:T(8,128)(2,1)S(1)} %get-tuple-element.73) | copy-start | bytes 589828
  72.7 3.3 %collective-permute-start.3 = (bf16[2304,128]{1,0:T(8,128)(2,1)S(1)}, bf16[2304,128]{1,0:T(8,128)(2,1)S(1)}, u32[]{:S(2)}, u32[]{:S(2)}) collective-permute-start(bf16[2304,128]{1,0:T(8,128)(2,1)S(1)} %get-tuple-element.69), channel_id=1, source_target_pairs={{0,8},{8,0},{1,9},{9,1},{2,10},{10,2},{3,11},{11,3},{4,12},{12,4},... | collective-permute-start | bytes 1769480 | tf_op jit(solution)/shard_map/ppermute | solution.py:893
  73.3 9.2 %collective-permute-start.1 = (bf16[1920,128]{1,0:T(8,128)(2,1)S(1)}, bf16[1920,128]{1,0:T(8,128)(2,1)S(1)}, u32[]{:S(2)}, u32[]{:S(2)}) collective-permute-start(bf16[1920,128]{1,0:T(8,128)(2,1)S(1)} %copy-done.13), channel_id=1, source_target_pairs={{0,2},{1,3},{2,4},{3,5},{4,6},{5,7},{6,0},{7,1},{8,9},{9,24},{10,1... | collective-permute-start | bytes 1474568 | tf_op jit(solution)/shard_map/ppermute | solution.py:854
  73.6 8.8 %collective-permute-start.2 = (bf16[1920,128]{1,0:T(8,128)(2,1)S(1)}, bf16[1920,128]{1,0:T(8,128)(2,1)S(1)}, u32[]{:S(2)}, u32[]{:S(2)}) collective-permute-start(bf16[1920,128]{1,0:T(8,128)(2,1)S(1)} %copy-done.12), channel_id=1, source_target_pairs={{0,6},{1,7},{2,0},{3,1},{4,2},{5,3},{6,4},{7,5},{8,25},{9,8},{10,2... | collective-permute-start | bytes 1474568 | tf_op jit(solution)/shard_map/ppermute | solution.py:854
  76.1 7.9 %collective-permute-start.4 = (bf16[576,128]{1,0:T(8,128)(2,1)S(1)}, bf16[576,128]{1,0:T(8,128)(2,1)S(1)}, u32[]{:S(2)}, u32[]{:S(2)}) collective-permute-start(bf16[576,128]{1,0:T(8,128)(2,1)S(1)} %get-tuple-element.71), channel_id=1, source_target_pairs={{0,2},{1,3},{2,4},{3,5},{4,6},{5,7},{6,0},{7,1},{8,9},{9,24},{10,1... | collective-permute-start | bytes 442376 | tf_op jit(solution)/shard_map/ppermute | solution.py:854
  76.2 7.9 %collective-permute-start.5 = (bf16[576,128]{1,0:T(8,128)(2,1)S(1)}, bf16[576,128]{1,0:T(8,128)(2,1)S(1)}, u32[]{:S(2)}, u32[]{:S(2)}) collective-permute-start(bf16[576,128]{1,0:T(8,128)(2,1)S(1)} %get-tuple-element.72), channel_id=1, source_target_pairs={{0,6},{1,7},{2,0},{3,1},{4,2},{5,3},{6,4},{7,5},{8,25},{9,8},{10,2... | collective-permute-start | bytes 442376 | tf_op jit(solution)/shard_map/ppermute | solution.py:854
  132.9 13.0 %collective-permute-start.8 = (bf16[32,160,128]{2,1,0:T(8,128)(2,1)S(1)}, bf16[32,160,128]{2,1,0:T(8,128)(2,1)S(1)}, u32[]{:S(2)}, u32[]{:S(2)}) collective-permute-start(bf16[32,160,128]{2,1,0:T(8,128)(2,1)S(1)} %all_to_all.31.own_ref), channel_id=1, source_target_pairs={{0,8},{8,0},{1,9},{9,1},{2,10},{10,2},{3,11},{11,3},{4,12},{12,4},... | collective-permute-start | bytes 3932168 | tf_op jit(solution)/shard_map/ppermute | solution.py:900
  139.4 14.6 %collective-permute-start.7 = (bf16[16,160,128]{2,1,0:T(8,128)(2,1)}, bf16[16,160,128]{2,1,0:T(8,128)(2,1)S(1)}, u32[]{:S(2)}, u32[]{:S(2)}) collective-permute-start(bf16[16,160,128]{2,1,0:T(8,128)(2,1)} %get-tuple-element.104), channel_id=1, source_target_pairs={{0,6},{1,7},{2,0},{3,1},{4,2},{5,3},{6,4},{7,5},{8,25},{9,8},{10,2... | collective-permute-start | bytes 1966088 | tf_op jit(solution)/shard_map/ppermute | solution.py:854
  140.4 13.6 %collective-permute-start.6 = (bf16[16,160,128]{2,1,0:T(8,128)(2,1)}, bf16[16,160,128]{2,1,0:T(8,128)(2,1)}, u32[]{:S(2)}, u32[]{:S(2)}) collective-permute-start(bf16[16,160,128]{2,1,0:T(8,128)(2,1)} %get-tuple-element.105), channel_id=1, source_target_pairs={{0,2},{1,3},{2,4},{3,5},{4,6},{5,7},{6,0},{7,1},{8,9},{9,24},{10,1... | collective-permute-start | bytes 1966088 | tf_op jit(solution)/shard_map/ppermute | solution.py:854
  140.9 13.1 %all-to-all-start.5 = ((bf16[16,8,768]{2,1,0:T(8,128)(2,1)}), bf16[16,8,768]{2,1,0:T(8,128)(2,1)S(1)}, u32[]{:S(2)}, u32[]{:S(2)}) async-start(bf16[16,8,768]{2,1,0:T(8,128)(2,1)} %bitcast.15), calls=%async_computation.5 | async-start | bytes 393216 | tf_op jit(solution)/shard_map/all_to_all | solution.py:850
  154.0 4.0 %collective-permute-start.9 = (bf16[16,160,128]{2,1,0:T(8,128)(2,1)}, bf16[16,160,128]{2,1,0:T(8,128)(2,1)S(1)}, u32[]{:S(2)}, u32[]{:S(2)}) collective-permute-start(bf16[16,160,128]{2,1,0:T(8,128)(2,1)} %collective-permute-done.6.part_a_ref), channel_id=1, source_target_pairs={{0,8},{8,0},{1,9},{9,1},{2,10},{10,2},{3,11},{11,3},{4,12},{12,4},... | collective-permute-start | bytes 1966088 | tf_op jit(solution)/shard_map/ppermute | solution.py:904
  154.8 3.2 %collective-permute-start.10 = (bf16[16,160,128]{2,1,0:T(8,128)(2,1)S(1)}, bf16[16,160,128]{2,1,0:T(8,128)(2,1)S(1)}, u32[]{:S(2)}, u32[]{:S(2)}) collective-permute-start(bf16[16,160,128]{2,1,0:T(8,128)(2,1)S(1)} %collective-permute-done.7.part_b_ref), channel_id=1, source_target_pairs={{0,8},{8,0},{1,9},{9,1},{2,10},{10,2},{3,11},{11,3},{4,12},{12,4},... | collective-permute-start | bytes 1966088 | tf_op jit(solution)/shard_map/ppermute | solution.py:904

commit v6 on v5

--- a/solution.py
+++ b/solution.py
@@ -132,6 +132,10 @@
 MEGA = 1024 * 1024
 
 
+def pinned(*arrays):
+    return [pltpu.with_memory_space_constraint(array, pltpu.HBM) for array in arrays]
+
+
 def limit(megabytes):
     return pltpu.CompilerParams(vmem_limit_bytes=megabytes * MEGA)
 
@@ -211,10 +215,19 @@
 
 
 def time_forward(
-    place_ref, neighbors_ref, rows_ref, wqkv_ref, wout_ref, sent_ref, qkv_ref, shares_ref, mix_ref
+    place_ref, neighbors_ref, rows_ref, wqkv_hbm, wout_hbm, sent_ref, qkv_ref, shares_ref, mix_ref,
+    tokens_ref, wqkv_ref, wout_ref, sems,
 ):
+    fetched = [
+        pltpu.make_async_copy(wqkv_hbm, wqkv_ref, sems.at[0]),
+        pltpu.make_async_copy(wout_hbm, wout_ref, sems.at[1]),
+    ]
+    for copy in fetched:
+        copy.start()
+    tokens_ref[...] = rows_ref[:, 0:C]
     x = rows_ref[:, 0:C].astype(F32)
     normed, _ = norm(x)
+    fetched[0].wait()
     qkv_ref[...] = mm(normed.astype(BF16), wqkv_ref[...]).astype(BF16)
     masks = tile_masks()
     for g in range(3):
@@ -229,6 +242,7 @@
             shares_ref[:, h * 128 : (h + 1) * 128] = shares.astype(BF16)
         mixed = mm(shares_ref[:, g * 512 : (g + 1) * 512], masked_stack(v, masks))
         mix_ref[:, g * 128 : (g + 1) * 128] = mixed.astype(BF16)
+    fetched[1].wait()
     x1 = (x + mm(mix_ref[...], wout_ref[...])).astype(BF16)
     lane = lax.broadcasted_iota(jnp.int32, (N, 128), 1)
     count = jnp.zeros((N, 128), F32)
@@ -245,7 +259,7 @@
     put = halves(core_ref[0], keep_ref, give_ref)
     back = back_ref[...].reshape(N, 1024)
     dx1 = back[:, 0:C]
-    normed, inverse = norm(rows_ref[:, 0:C].astype(F32))
+    normed, inverse = norm(rows_ref[...].astype(F32))
     dmix = mt(dx1, wout_ref[...]).astype(BF16)
     put("time_out", tm(mix_ref[...], dx1))
     masks = tile_masks()
@@ -499,22 +513,25 @@
     return pl.pallas_call(
         pack_rows,
         out_shape=like((residues, frames, 2 * C + 128), BF16),
-        compiler_params=limit(60),
+        compiler_params=limit(8),
         name="pack_rows",
-    )(tokens, cotangent, rigid)
+    )(*pinned(tokens, cotangent, rigid))
 
 
 def call_time_forward(place, neighbors, rows, w_qkv, w_out):
     return pl.pallas_call(
         time_forward,
-        in_specs=[SMEM, SMEM, VMEM, VMEM, VMEM],
+        in_specs=[SMEM, SMEM, VMEM, HBM, HBM],
+        scratch_shapes=[
+            pltpu.VMEM((C, 3 * C), BF16), pltpu.VMEM((C, C), BF16), pltpu.SemaphoreType.DMA((2,)),
+        ],
         out_shape=(
-            like((N, 8, 128), BF16), like((N, 3 * C), BF16), like((N, H * N), BF16),
-            like((N, C), BF16),
+            like((N, 8, 128), BF16), pltpu.HBM((N, 3 * C), BF16), pltpu.HBM((N, H * N), BF16),
+            pltpu.HBM((N, C), BF16), pltpu.HBM((N, C), BF16),
         ),
-        compiler_params=limit(60),
+        compiler_params=limit(12),
         name="time_forward",
-    )(place, neighbors, rows, w_qkv, w_out)
+    )(place, *pinned(neighbors), rows, *pinned(w_qkv, w_out))
 
 
 def call_time_backward(core, back, rows, qkv, shares, mix, w_qkv, w_out):
@@ -528,7 +545,7 @@
         compiler_params=limit(20),
         cost_estimate=pl.CostEstimate(flops=1000, bytes_accessed=1000, transcendentals=0),
         name="time_backward",
-    )(core, back, rows, qkv, shares, mix, w_qkv, w_out)
+    )(core, back, *pinned(rows, qkv, shares, mix, w_qkv, w_out))
 
 
 def call_point_attention(core, weight, rows, w_qkv, w_pts, w_rep, w_out, w_up, w_down):
@@ -538,7 +555,7 @@
         point_attention,
         in_specs=[SMEM, SMEM, VMEM] + [HBM] * len(sources),
         out_specs=(VMEM, HBM, HBM),
-        out_shape=(like((N, 8, 128), BF16), like((EARLY, 128), BF16), like((EARLY, 128), BF16)),
+        out_shape=(like((N, 8, 128), BF16), pltpu.HBM((EARLY, 128), BF16), pltpu.HBM((EARLY, 128), BF16)),
         scratch_shapes=[
             pltpu.VMEM((N, 3 * C), BF16), pltpu.VMEM((N, C), BF16),
             pltpu.VMEM((N, H * N), F32), pltpu.VMEM((N, H * N), F32),
@@ -550,16 +567,16 @@
             *[pltpu.VMEM(source.shape, BF16) for source in sources],
             pltpu.SemaphoreType.DMA((len(sources),)), pltpu.SemaphoreType.DMA((9,)),
         ],
-        compiler_params=limit(60),
+        compiler_params=limit(40),
         name="point_attention",
-    )(core, weight, rows, *sources)
-
-
-def add_early(side_ref, keep_ref, got_ref, give_a_ref, give_b_ref, mine_ref, one_ref, two_ref, sems):
+    )(core, weight, rows, *pinned(*sources))
+
+
+def add_early(side_ref, keep_ref, got_ref, give_ref, mine_ref, one_ref, two_ref, sems):
     part = EARLY // 4
     give, mine = 2 * (1 - side_ref[0]), 2 * side_ref[0]
     targets = (
-        (give, give_a_ref), (give + 1, give_b_ref),
+        (give, give_ref.at[0:part]), (give + 1, give_ref.at[part : 2 * part]),
         (mine, mine_ref.at[0:part]), (mine + 1, mine_ref.at[part : 2 * part]),
     )
     steps = []
@@ -588,20 +605,20 @@
 
 
 def call_add_early(side, keep, got):
-    part = like((EARLY // 4, 128), BF16)
+    part = like((EARLY // 2, 128), BF16)
     return pl.pallas_call(
         add_early,
         in_specs=[SMEM, HBM, HBM],
-        out_specs=(HBM, HBM, HBM),
-        out_shape=(part, part, like((EARLY // 2, 128), BF16)),
+        out_specs=(HBM, HBM),
+        out_shape=(pltpu.HBM(part.shape, BF16),) * 2,
         scratch_shapes=[
             pltpu.VMEM((EARLY, 128), BF16), pltpu.VMEM((EARLY, 128), BF16),
             pltpu.SemaphoreType.DMA((12,)),
         ],
-        compiler_params=limit(60),
+        compiler_params=limit(8),
         cost_estimate=pl.CostEstimate(flops=EARLY * 128, bytes_accessed=EARLY * 128 * 6, transcendentals=0),
         name="add_early",
-    )(side, keep, got)
+    )(side, *pinned(keep), got)
 
 
 def add_late(side_ref, keep_ref, got_ref, give_a_ref, give_b_ref, mine_ref):
@@ -627,9 +644,9 @@
     )(side, keep, got)
 
 
-def add_pairs(early_ref, early_a_ref, early_b_ref, late_ref, late_a_ref, late_b_ref, total_ref):
+def add_pairs(early_ref, got_early_ref, late_ref, late_a_ref, late_b_ref, total_ref):
     at = 0
-    for mine, parts in ((early_ref, (early_a_ref, early_b_ref)), (late_ref, (late_a_ref, late_b_ref))):
+    for mine, parts in ((early_ref, (got_early_ref,)), (late_ref, (late_a_ref, late_b_ref))):
         size = parts[0].shape[0]
         for k, part in enumerate(parts):
             summed = mine[k * size : (k + 1) * size, :].astype(F32) + part[...].astype(F32)
@@ -878,22 +895,22 @@
     points = w_ipa_points.T
     rows = swap_rows(call_pack_rows(tokens, cotangent, rigid_frames), ("line", "core"))
     rows = rows.reshape(N, 2 * C + 128)
-    sent, qkv, shares, mix = call_time_forward(place, neighbors, rows, w_time_qkv, w_time_out)
+    sent, qkv, shares, mix, rows = call_time_forward(place, neighbors, rows, w_time_qkv, w_time_out)
     back, keep_early, give_early = call_point_attention(
         core, point_weight, swap_rows(sent, EVERYONE), w_ipa_qkv, points, repeat_points(points),
         w_ipa_out, w_up, w_down,
     )
     got_early = lax.ppermute(give_early, "core", swap)
-    *give_early, mine_early = call_add_early(side, keep_early, got_early)
-    got_early = both_ways(give_early)
-    back, _ = lax.optimization_barrier((swap_rows(back, EVERYONE), give_early))
+    give_early, mine_early = call_add_early(side, keep_early, got_early)
+    got_early = lax.ppermute(give_early, EVERYONE, RINGS[0])
+    back = swap_rows(back, EVERYONE)
     ended, keep_late, give_late = call_time_backward(
         core, back, rows, qkv, shares, mix, w_time_qkv, w_time_out
     )
     got_late = lax.ppermute(give_late, "core", swap)
     *give_late, mine_late = call_add_late(side, keep_late, got_late)
     got_late = both_ways(give_late)
-    total = call_add_pairs(mine_early, *got_early, mine_late, *got_late)
+    total = call_add_pairs(mine_early, got_early, mine_late, *got_late)
     parts = share(total.reshape(SHARERS, CHUNK, 128))
     own = share(call_add_parts(parts))
     paired = both_ways((own[: SHARERS // 2], own[SHARERS // 2 :]))

time: 162 us -> 159 us (0.981)
  local copies, waits for them, and re-layouts: 3.88 us -> 1.2 us
    unnamed x28 -> x8, local copies, waits for them, and re-layouts: 2.71 us -> 0.02 us
    ppermute x6 -> x4, starting transfers between devices: 6.88 us -> 4.21 us  [both_ways(): lax.ppermute(part, EVERYONE, ring)]
    ppermute x6 -> x4, waiting for transfers between devices: 5.2 us -> 2.83 us  [both_ways(): lax.ppermute(part, EVERYONE, ring)]
    ppermute x0 -> x1, starting transfers between devices: none -> 1.64 us  [body(): got_early = lax.ppermute(give_early, EVERYONE, RINGS[0])]
    ppermute x1, waiting for transfers between devices: 0.01 us -> 1.63 us  [body(): got_late = lax.ppermute(give_late, 'core', swap)]
  transfers between devices with their start and end apart: 15 -> 14, of which waited for: 6 -> 6; matrix products, arithmetic and copies ran while one was open for 1% -> 1% of each run, Pallas kernels for 6% -> 9%
where the time goes in v6:
time: 159 us
  blocking collectives  49 us (31%)
  Pallas kernels  36.9 us (23%)
  starting transfers between devices  36 us (23%)
  waiting for transfers between devices  33.3 us (21%)
    all_to_all x2, blocking collectives, share(): lax.all_to_all(parts, EVERYONE, split_axis=0, concat_axis=0, tiled=True,...  49 us
    all_to_all x4, waiting for transfers between devices, swap_rows(): return lax.all_to_all(rows, axes, split_axis=0, concat_axis=0, tiled=True)  28.8 us
    all_to_all x4, starting transfers between devices, swap_rows(): return lax.all_to_all(rows, axes, split_axis=0, concat_axis=0, tiled=True)  23.3 us
    pallas_call x1, Pallas kernels, call_point_attention(): pl.pallas_call(point_attention, in_specs=[SMEM, SMEM, VMEM] + [HBM] * len...  11.8 us
    ppermute x1, starting transfers between devices, body(): swapped = lax.ppermute(own, 'core', swap)  4.74 us
    pallas_call x1, Pallas kernels, call_time_forward(): pl.pallas_call(time_forward, in_specs=[SMEM, SMEM, VMEM, HBM, HBM], scrat...  4.69 us
    ppermute x4, starting transfers between devices, both_ways(): lax.ppermute(part, EVERYONE, ring)  4.21 us
    pallas_call x1, Pallas kernels, call_time_backward(): pl.pallas_call(time_backward, in_specs=[SMEM] + [VMEM] * 7, out_shape=(li...  4.2 us
  transfers between devices with their start and end apart: 14, of which 6 were waited for; matrix products, arithmetic and copies ran while one was open for 1% of the time, Pallas kernels for 9%

profile of v6, /device:TPU:1, one launch (start us, length us, event | category | flops | bytes accessed | tf_op | source)
XLA Modules:
  0.0 158.5 jit_solution(15249431627053225472)
XLA Ops:
  0.6 0.0 copy-start.3
  0.7 2.0 %pack_rows.1 = bf16[16,8,896]{2,1,0:T(8,128)(2,1)} custom-call(bf16[8,16,384]{2,1,0:T(8,128)(2,1)} %tokens_ref.1, bf16[8,16,384]{2,1,0:T(8,128)(2,1)} %cotangent_ref.1, bf16[12,8,16]{2,1,0:T(8,128)(2,1)} %rigid_ref.1), custom_call_target="tpu_custom_call" | custom-call | tf_op jit(solution)/shard_map/pack_rows/pallas_call | solution.py:513
  2.6 9.5 %all-to-all-start = ((bf16[16,8,896]{2,1,0:T(8,128)(2,1)}), bf16[16,8,896]{2,1,0:T(8,128)(2,1)S(1)}, u32[]{:S(2)}, u32[]{:S(2)}) async-start(bf16[16,8,896]{2,1,0:T(8,128)(2,1)} %pack_rows.1), calls=%async_computation | async-start | bytes 458752 | tf_op jit(solution)/shard_map/all_to_all | solution.py:867
  12.1 0.0 copy-start.2
  12.1 8.4 %all-to-all-done = bf16[16,8,896]{2,1,0:T(8,128)(2,1)S(1)} async-done(((bf16[16,8,896]{2,1,0:T(8,128)(2,1)}), bf16[16,8,896]{2,1,0:T(8,128)(2,1)S(1)}, u32[]{:S(2)}, u32[]{:S(2)}) %all-to-all-start) | async-done | bytes 229408 | tf_op jit(solution)/shard_map/all_to_all | solution.py:867
  20.5 4.7 %time_forward.1 = (bf16[128,8,128]{2,1,0:T(8,128)(2,1)}, bf16[128,1152]{1,0:T(8,128)(2,1)}, bf16[128,1536]{1,0:T(8,128)(2,1)}, bf16[128,384]{1,0:T(8,128)(2,1)}, bf16[128,384]{1,0:T(8,128)(2,1)}) custom-call(s32[1]{0:T(128)} %bitcast.3.place_ref, s32[16,32]{1,0:T(8,128)} %neighbors_ref.1, bf16[128,896]{1,0:T(8,128)(2,1)S(1)} %bitcast.13, ...), custom_call_target="tpu_custom_call" | custom-call | tf_op jit(solution)/shard_map/time_forward/pallas_call | solution.py:522
  25.2 5.2 %all-to-all-start.1 = ((bf16[128,8,128]{2,1,0:T(8,128)(2,1)}), bf16[128,8,128]{2,1,0:T(8,128)(2,1)S(1)}, u32[]{:S(2)}, u32[]{:S(2)}) async-start(bf16[128,8,128]{2,1,0:T(8,128)(2,1)} %get-tuple-element.56), calls=%async_computation.1 | async-start | bytes 524288 | tf_op jit(solution)/shard_map/all_to_all | solution.py:867
  30.4 0.0 copy-done.3
  30.4 1.1 fusion.4
  31.5 9.9 %all-to-all-done.1.rows_ref = bf16[128,8,128]{2,1,0:T(8,128)(2,1)S(1)} async-done(((bf16[128,8,128]{2,1,0:T(8,128)(2,1)}), bf16[128,8,128]{2,1,0:T(8,128)(2,1)S(1)}, u32[]{:S(2)}, u32[]{:S(2)}) %all-to-all-start.1) | async-done | bytes 262176 | tf_op jit(solution)/shard_map/all_to_all | solution.py:867
  41.4 0.0 copy-done.2
  41.4 11.8 %point_attention.1 = (bf16[128,8,128]{2,1,0:T(8,128)(2,1)}, bf16[7680,128]{1,0:T(8,128)(2,1)}, bf16[7680,128]{1,0:T(8,128)(2,1)}) custom-call(s32[1]{0:T(128)} %bitcast.core_ref, f32[12]{0:T(128)S(1)} %copy-done.2, bf16[128,8,128]{2,1,0:T(8,128)(2,1)S(1)} %all-to-all-done.1.rows_ref, bf16[384,1152]{1,0:T(8,128)(2,1)} %refs_0_.1, ...), custom_call_target="tpu_custom_call" | custom-call | tf_op jit(solution)/shard_map/point_attention/pallas_call | solution.py:554
  53.3 0.6 collective-permute-start
  53.9 3.8 %all-to-all-start.2 = ((bf16[128,8,128]{2,1,0:T(8,128)(2,1)}), bf16[128,8,128]{2,1,0:T(8,128)(2,1)S(1)}, u32[]{:S(2)}, u32[]{:S(2)}) async-start(bf16[128,8,128]{2,1,0:T(8,128)(2,1)} %get-tuple-element.61), calls=%async_computation.2 | async-start | bytes 524288 | tf_op jit(solution)/shard_map/all_to_all | solution.py:867
  57.7 0.0 collective-permute-done.got_ref
  57.7 3.1 %add_early.1 = (bf16[3840,128]{1,0:T(8,128)(2,1)}, bf16[3840,128]{1,0:T(8,128)(2,1)}) custom-call(s32[1]{0:T(128)S(6)} %select_n.7.side_ref, bf16[7680,128]{1,0:T(8,128)(2,1)} %get-tuple-element.57.keep_ref, bf16[7680,128]{1,0:T(8,128)(2,1)S(1)} %collective-permute-done.got_ref), custom_call_target="tpu_custom_call" | custom-call | flops 983040 | bytes 5898240 | tf_op jit(solution)/shard_map/add_early/pallas_call | solution.py:609
  60.8 0.0 copy-start
  60.8 1.6 %collective-permute-start.1 = (bf16[3840,128]{1,0:T(8,128)(2,1)}, bf16[3840,128]{1,0:T(8,128)(2,1)S(1)}, u32[]{:S(2)}, u32[]{:S(2)}) collective-permute-start(bf16[3840,128]{1,0:T(8,128)(2,1)} %get-tuple-element.60), channel_id=1, source_target_pairs={{0,2},{1,3},{2,4},{3,5},{4,6},{5,7},{6,0},{7,1},{8,9},{9,24},{10,1... | collective-permute-start | bytes 2949128 | tf_op jit(solution)/shard_map/ppermute | solution.py:905
  62.4 6.3 %all-to-all-done.2.back_ref = bf16[128,8,128]{2,1,0:T(8,128)(2,1)S(1)} async-done(((bf16[128,8,128]{2,1,0:T(8,128)(2,1)}), bf16[128,8,128]{2,1,0:T(8,128)(2,1)S(1)}, u32[]{:S(2)}, u32[]{:S(2)}) %all-to-all-start.2) | async-done | bytes 262176 | tf_op jit(solution)/shard_map/all_to_all | solution.py:867
  68.7 4.2 %time_backward.1 = (bf16[128,768]{1,0:T(8,128)(2,1)S(1)}, bf16[2304,128]{1,0:T(8,128)(2,1)S(1)}, bf16[2304,128]{1,0:T(8,128)(2,1)S(1)}) custom-call(s32[1]{0:T(128)} %bitcast.core_ref, bf16[128,8,128]{2,1,0:T(8,128)(2,1)S(1)} %all-to-all-done.2.back_ref, bf16[128,384]{1,0:T(8,128)(2,1)} %get-tuple-element.62.rows_ref, ...), custom_call_target="tpu_custom_call" | custom-call | flops 1000 | bytes 1000 | tf_op jit(solution)/shard_map/time_backward/pallas_call | solution.py:538
  72.9 0.0 copy-start.1
  72.9 0.6 collective-permute-start.2
  73.5 1.6 %collective-permute-done.2.got_ref = bf16[2304,128]{1,0:T(8,128)(2,1)S(1)} collective-permute-done((bf16[2304,128]{1,0:T(8,128)(2,1)S(1)}, bf16[2304,128]{1,0:T(8,128)(2,1)S(1)}, u32[]{:S(2)}, u32[]{:S(2)}) %collective-permute-start.2) | collective-permute-done | bytes 589856 | tf_op jit(solution)/shard_map/ppermute | solution.py:910
  75.1 0.1 add_late.1
  75.3 0.4 collective-permute-start.3
  75.7 2.3 %collective-permute-start.4 = (bf16[576,128]{1,0:T(8,128)(2,1)S(1)}, bf16[576,128]{1,0:T(8,128)(2,1)S(1)}, u32[]{:S(2)}, u32[]{:S(2)}) collective-permute-start(bf16[576,128]{1,0:T(8,128)(2,1)S(1)} %get-tuple-element.70), channel_id=1, source_target_pairs={{0,6},{1,7},{2,0},{3,1},{4,2},{5,3},{6,4},{7,5},{8,25},{9,8},{10,2... | collective-permute-start | bytes 442376 | tf_op jit(solution)/shard_map/ppermute | solution.py:871
  78.0 2.8 %collective-permute-done.3.late_a_ref = bf16[576,128]{1,0:T(8,128)(2,1)S(1)} collective-permute-done((bf16[576,128]{1,0:T(8,128)(2,1)S(1)}, bf16[576,128]{1,0:T(8,128)(2,1)S(1)}, u32[]{:S(2)}, u32[]{:S(2)}) %collective-permute-start.3) | collective-permute-done | bytes 147488 | tf_op jit(solution)/shard_map/ppermute | solution.py:871
  80.8 0.0 collective-permute-done.4.late_b_ref
  80.9 0.0 collective-permute-done.1.got_early_ref
  80.9 0.0 copy-done
  80.9 0.3 add_pairs.1
  81.2 0.0 copy-done.1
  81.2 24.7 %all_to_all.30.parts_ref = bf16[32,160,128]{2,1,0:T(8,128)(2,1)S(1)} all-to-all(bf16[32,160,128]{2,1,0:T(8,128)(2,1)S(1)} %bitcast.12), channel_id=1, replica_groups={{0,1,4,5,16,17,20,21,32,33,36,37,48,49,52,53,64,65,68,69,80,81,84,85,96..., dimensions={0} | all-to-all | bytes 2621440 | tf_op jit(solution)/shard_map/all_to_all | solution.py:875
  105.9 0.2 add_parts.1
  106.1 24.3 %all_to_all.31.own_ref = bf16[32,160,128]{2,1,0:T(8,128)(2,1)S(1)} all-to-all(bf16[32,160,128]{2,1,0:T(8,128)(2,1)S(1)} %add_parts.1), channel_id=1, replica_groups={{0,1,4,5,16,17,20,21,32,33,36,37,48,49,52,53,64,65,68,69,80,81,84,85,96..., dimensions={0} | all-to-all | bytes 2621440 | tf_op jit(solution)/shard_map/all_to_all | solution.py:875
  130.4 4.7 %collective-permute-start.7 = (bf16[32,160,128]{2,1,0:T(8,128)(2,1)S(1)}, bf16[32,160,128]{2,1,0:T(8,128)(2,1)S(1)}, u32[]{:S(2)}, u32[]{:S(2)}) collective-permute-start(bf16[32,160,128]{2,1,0:T(8,128)(2,1)S(1)} %all_to_all.31.own_ref), channel_id=1, source_target_pairs={{0,8},{8,0},{1,9},{9,1},{2,10},{10,2},{3,11},{11,3},{4,12},{12,4},... | collective-permute-start | bytes 3932168 | tf_op jit(solution)/shard_map/ppermute | solution.py:917
  135.1 1.2 fusion.5
  136.3 1.0 collective-permute-start.6
  137.3 0.5 collective-permute-start.5
  137.8 4.9 %all-to-all-start.5 = ((bf16[16,8,768]{2,1,0:T(8,128)(2,1)}), bf16[16,8,768]{2,1,0:T(8,128)(2,1)S(1)}, u32[]{:S(2)}, u32[]{:S(2)}) async-start(bf16[16,8,768]{2,1,0:T(8,128)(2,1)} %bitcast.14), calls=%async_computation.5 | async-start | bytes 393216 | tf_op jit(solution)/shard_map/all_to_all | solution.py:867
  142.7 0.1 pad_add_fusion.spots_ref
  142.8 0.0 collective-permute-done.7.swapped_ref
  142.8 4.0 %unpack_first.1 = (f32[384,1536]{1,0:T(8,128)}, f32[384,384]{1,0:T(8,128)}, f32[288,384]{1,0:T(8,128)}, f32[384,1152]{1,0:T(8,128)}, f32[1536,384]{1,0:T(8,128)}...) custom-call(s32[4]{0:T(128)S(1)} %pad_add_fusion.spots_ref, ...), custom_call_target="tpu_custom_call" | custom-call | bytes 8388608 | tf_op jit(solution)/shard_map/unpack_first/pallas_call | solution.py:819
  146.8 4.1 %all-to-all-done.5.ended_ref = bf16[16,8,768]{2,1,0:T(8,128)(2,1)S(1)} async-done(((bf16[16,8,768]{2,1,0:T(8,128)(2,1)}), bf16[16,8,768]{2,1,0:T(8,128)(2,1)S(1)}, u32[]{:S(2)}, u32[]{:S(2)}) %all-to-all-start.5) | async-done | bytes 196640 | tf_op jit(solution)/shard_map/all_to_all | solution.py:867
  150.9 0.0 collective-permute-done.6.part_b_ref
  150.9 0.0 collective-permute-done.5.part_a_ref
  150.9 0.8 collective-permute-start.8
  151.7 0.1 collective-permute-start.9
  151.8 3.1 %unpack_second.1 = (f32[384,1536]{1,0:T(8,128)}, f32[384,384]{1,0:T(8,128)}, f32[288,384]{1,0:T(8,128)}, f32[384,1152]{1,0:T(8,128)}, f32[1536,384]{1,0:T(8,128)...) custom-call(s32[4]{0:T(128)S(1)} %pad_add_fusion.spots_ref, ...), custom_call_target="tpu_custom_call", output_to_operand_aliasing={{0}: (4, {}), {1}: (5, {}), {2}: (6, {}), {3}: (7, {}), {4}... | custom-call | bytes 8388608 | tf_op jit(solution)/shard_map/unpack_second/pallas_call | solution.py:832
  154.9 0.0 collective-permute-done.8.part_a_ref
  154.9 0.0 collective-permute-done.9.part_b_ref
  154.9 3.5 %unpack_last.1 = (f32[384,1536]{1,0:T(8,128)}, f32[384,384]{1,0:T(8,128)}, f32[288,384]{1,0:T(8,128)}, f32[384,1152]{1,0:T(8,128)}, f32[1536,384]{1,0:T(8,128)},...) custom-call(s32[4]{0:T(128)S(1)} %pad_add_fusion.spots_ref, ...), custom_call_target="tpu_custom_call", output_to_operand_aliasing={{0}: (5, {}), {1}: (6, {}), {2}: (7, {}), {3}: (8, {}), {4}... | custom-call | tf_op jit(solution)/shard_map/unpack_last/pallas_call | solution.py:848
Async XLA Ops:
  0.6 29.8 %copy-start.3 = (bf16[384,288]{0,1:T(8,128)(2,1)S(1)}, bf16[384,288]{0,1:T(8,128)(2,1)}, u32[]{:S(2)}) copy-start(bf16[384,288]{0,1:T(8,128)(2,1)} %param.22) | copy-start | bytes 663556
  2.6 17.9 %all-to-all-start = ((bf16[16,8,896]{2,1,0:T(8,128)(2,1)}), bf16[16,8,896]{2,1,0:T(8,128)(2,1)S(1)}, u32[]{:S(2)}, u32[]{:S(2)}) async-start(bf16[16,8,896]{2,1,0:T(8,128)(2,1)} %pack_rows.1), calls=%async_computation | async-start | bytes 458752 | tf_op jit(solution)/shard_map/all_to_all | solution.py:867
  12.1 29.4 %copy-start.2 = (f32[12]{0:T(128)S(1)}, f32[12]{0:T(128)}, u32[]{:S(2)}) copy-start(f32[12]{0:T(128)} %weight_ref.1) | copy-start | bytes 148
  25.2 16.2 %all-to-all-start.1 = ((bf16[128,8,128]{2,1,0:T(8,128)(2,1)}), bf16[128,8,128]{2,1,0:T(8,128)(2,1)S(1)}, u32[]{:S(2)}, u32[]{:S(2)}) async-start(bf16[128,8,128]{2,1,0:T(8,128)(2,1)} %get-tuple-element.56), calls=%async_computation.1 | async-start | bytes 524288 | tf_op jit(solution)/shard_map/all_to_all | solution.py:867
  53.3 4.4 %collective-permute-start = (bf16[7680,128]{1,0:T(8,128)(2,1)}, bf16[7680,128]{1,0:T(8,128)(2,1)S(1)}, u32[]{:S(2)}, u32[]{:S(2)}) collective-permute-start(bf16[7680,128]{1,0:T(8,128)(2,1)} %get-tuple-element.58), channel_id=1, source_target_pairs={{0,8},{8,0},{1,9},{9,1},{2,10},{10,2},{3,11},{11,3},{4,12},{12,4},... | collective-permute-start | bytes 5898248 | tf_op jit(solution)/shard_map/ppermute | solution.py:903
  53.9 14.8 %all-to-all-start.2 = ((bf16[128,8,128]{2,1,0:T(8,128)(2,1)}), bf16[128,8,128]{2,1,0:T(8,128)(2,1)S(1)}, u32[]{:S(2)}, u32[]{:S(2)}) async-start(bf16[128,8,128]{2,1,0:T(8,128)(2,1)} %get-tuple-element.61), calls=%async_computation.2 | async-start | bytes 524288 | tf_op jit(solution)/shard_map/all_to_all | solution.py:867
  60.8 20.1 %copy-start = (bf16[3840,128]{1,0:T(8,128)(2,1)S(1)}, bf16[3840,128]{1,0:T(8,128)(2,1)}, u32[]{:S(2)}) copy-start(bf16[3840,128]{1,0:T(8,128)(2,1)} %get-tuple-element.59.early_ref) | copy-start | bytes 2949124
  60.8 20.1 %collective-permute-start.1 = (bf16[3840,128]{1,0:T(8,128)(2,1)}, bf16[3840,128]{1,0:T(8,128)(2,1)S(1)}, u32[]{:S(2)}, u32[]{:S(2)}) collective-permute-start(bf16[3840,128]{1,0:T(8,128)(2,1)} %get-tuple-element.60), channel_id=1, source_target_pairs={{0,2},{1,3},{2,4},{3,5},{4,6},{5,7},{6,0},{7,1},{8,9},{9,24},{10,1... | collective-permute-start | bytes 2949128 | tf_op jit(solution)/shard_map/ppermute | solution.py:905
  72.9 8.3 %copy-start.1 = (bf16[128,768]{1,0:T(8,128)(2,1)}, bf16[128,768]{1,0:T(8,128)(2,1)S(1)}, u32[]{:S(2)}) copy-start(bf16[128,768]{1,0:T(8,128)(2,1)S(1)} %get-tuple-element.71) | copy-start | bytes 589828
  72.9 2.2 %collective-permute-start.2 = (bf16[2304,128]{1,0:T(8,128)(2,1)S(1)}, bf16[2304,128]{1,0:T(8,128)(2,1)S(1)}, u32[]{:S(2)}, u32[]{:S(2)}) collective-permute-start(bf16[2304,128]{1,0:T(8,128)(2,1)S(1)} %get-tuple-element.67), channel_id=1, source_target_pairs={{0,8},{8,0},{1,9},{9,1},{2,10},{10,2},{3,11},{11,3},{4,12},{12,4},... | collective-permute-start | bytes 1769480 | tf_op jit(solution)/shard_map/ppermute | solution.py:910
  75.3 5.6 %collective-permute-start.3 = (bf16[576,128]{1,0:T(8,128)(2,1)S(1)}, bf16[576,128]{1,0:T(8,128)(2,1)S(1)}, u32[]{:S(2)}, u32[]{:S(2)}) collective-permute-start(bf16[576,128]{1,0:T(8,128)(2,1)S(1)} %get-tuple-element.69), channel_id=1, source_target_pairs={{0,2},{1,3},{2,4},{3,5},{4,6},{5,7},{6,0},{7,1},{8,9},{9,24},{10,1... | collective-permute-start | bytes 442376 | tf_op jit(solution)/shard_map/ppermute | solution.py:871
  75.7 5.2 %collective-permute-start.4 = (bf16[576,128]{1,0:T(8,128)(2,1)S(1)}, bf16[576,128]{1,0:T(8,128)(2,1)S(1)}, u32[]{:S(2)}, u32[]{:S(2)}) collective-permute-start(bf16[576,128]{1,0:T(8,128)(2,1)S(1)} %get-tuple-element.70), channel_id=1, source_target_pairs={{0,6},{1,7},{2,0},{3,1},{4,2},{5,3},{6,4},{7,5},{8,25},{9,8},{10,2... | collective-permute-start | bytes 442376 | tf_op jit(solution)/shard_map/ppermute | solution.py:871
  130.4 12.4 %collective-permute-start.7 = (bf16[32,160,128]{2,1,0:T(8,128)(2,1)S(1)}, bf16[32,160,128]{2,1,0:T(8,128)(2,1)S(1)}, u32[]{:S(2)}, u32[]{:S(2)}) collective-permute-start(bf16[32,160,128]{2,1,0:T(8,128)(2,1)S(1)} %all_to_all.31.own_ref), channel_id=1, source_target_pairs={{0,8},{8,0},{1,9},{9,1},{2,10},{10,2},{3,11},{11,3},{4,12},{12,4},... | collective-permute-start | bytes 3932168 | tf_op jit(solution)/shard_map/ppermute | solution.py:917
  136.3 14.6 %collective-permute-start.6 = (bf16[16,160,128]{2,1,0:T(8,128)(2,1)}, bf16[16,160,128]{2,1,0:T(8,128)(2,1)S(1)}, u32[]{:S(2)}, u32[]{:S(2)}) collective-permute-start(bf16[16,160,128]{2,1,0:T(8,128)(2,1)} %get-tuple-element.102), channel_id=1, source_target_pairs={{0,6},{1,7},{2,0},{3,1},{4,2},{5,3},{6,4},{7,5},{8,25},{9,8},{10,2... | collective-permute-start | bytes 1966088 | tf_op jit(solution)/shard_map/ppermute | solution.py:871
  137.3 13.6 %collective-permute-start.5 = (bf16[16,160,128]{2,1,0:T(8,128)(2,1)}, bf16[16,160,128]{2,1,0:T(8,128)(2,1)}, u32[]{:S(2)}, u32[]{:S(2)}) collective-permute-start(bf16[16,160,128]{2,1,0:T(8,128)(2,1)} %get-tuple-element.103), channel_id=1, source_target_pairs={{0,2},{1,3},{2,4},{3,5},{4,6},{5,7},{6,0},{7,1},{8,9},{9,24},{10,1... | collective-permute-start | bytes 1966088 | tf_op jit(solution)/shard_map/ppermute | solution.py:871
  137.8 13.1 %all-to-all-start.5 = ((bf16[16,8,768]{2,1,0:T(8,128)(2,1)}), bf16[16,8,768]{2,1,0:T(8,128)(2,1)S(1)}, u32[]{:S(2)}, u32[]{:S(2)}) async-start(bf16[16,8,768]{2,1,0:T(8,128)(2,1)} %bitcast.14), calls=%async_computation.5 | async-start | bytes 393216 | tf_op jit(solution)/shard_map/all_to_all | solution.py:867
  150.9 4.0 %collective-permute-start.8 = (bf16[16,160,128]{2,1,0:T(8,128)(2,1)}, bf16[16,160,128]{2,1,0:T(8,128)(2,1)S(1)}, u32[]{:S(2)}, u32[]{:S(2)}) collective-permute-start(bf16[16,160,128]{2,1,0:T(8,128)(2,1)} %collective-permute-done.5.part_a_ref), channel_id=1, source_target_pairs={{0,8},{8,0},{1,9},{9,1},{2,10},{10,2},{3,11},{11,3},{4,12},{12,4},... | collective-permute-start | bytes 1966088 | tf_op jit(solution)/shard_map/ppermute | solution.py:921
  151.7 3.2 %collective-permute-start.9 = (bf16[16,160,128]{2,1,0:T(8,128)(2,1)S(1)}, bf16[16,160,128]{2,1,0:T(8,128)(2,1)S(1)}, u32[]{:S(2)}, u32[]{:S(2)}) collective-permute-start(bf16[16,160,128]{2,1,0:T(8,128)(2,1)S(1)} %collective-permute-done.6.part_b_ref), channel_id=1, source_target_pairs={{0,8},{8,0},{1,9},{9,1},{2,10},{10,2},{3,11},{11,3},{4,12},{12,4},... | collective-permute-start | bytes 1966088 | tf_op jit(solution)/shard_map/ppermute | solution.py:921

commit v7 on v6

--- a/solution.py
+++ b/solution.py
@@ -215,9 +215,18 @@
 
 
 def time_forward(
-    place_ref, neighbors_ref, rows_ref, wqkv_hbm, wout_hbm, sent_ref, qkv_ref, shares_ref, mix_ref,
-    tokens_ref, wqkv_ref, wout_ref, sems,
+    place_ref, neighbors_ref, rows_ref, wqkv_hbm, wout_hbm, sent_ref, qkv_hbm, shares_hbm, mix_hbm,
+    tokens_hbm, wqkv_ref, wout_ref, sems, qkv_ref, shares_ref, mix_ref, tokens_ref, out_sems,
 ):
+    saved = [
+        pltpu.make_async_copy(source, target, out_sems.at[k])
+        for k, (source, target) in enumerate(
+            (
+                (tokens_ref, tokens_hbm), (qkv_ref, qkv_hbm), (shares_ref, shares_hbm),
+                (mix_ref, mix_hbm),
+            )
+        )
+    ]
     fetched = [
         pltpu.make_async_copy(wqkv_hbm, wqkv_ref, sems.at[0]),
         pltpu.make_async_copy(wout_hbm, wout_ref, sems.at[1]),
@@ -225,10 +234,12 @@
     for copy in fetched:
         copy.start()
     tokens_ref[...] = rows_ref[:, 0:C]
+    saved[0].start()
     x = rows_ref[:, 0:C].astype(F32)
     normed, _ = norm(x)
     fetched[0].wait()
     qkv_ref[...] = mm(normed.astype(BF16), wqkv_ref[...]).astype(BF16)
+    saved[1].start()
     masks = tile_masks()
     for g in range(3):
         q = qkv_ref[:, g * 128 : (g + 1) * 128]
@@ -242,6 +253,8 @@
             shares_ref[:, h * 128 : (h + 1) * 128] = shares.astype(BF16)
         mixed = mm(shares_ref[:, g * 512 : (g + 1) * 512], masked_stack(v, masks))
         mix_ref[:, g * 128 : (g + 1) * 128] = mixed.astype(BF16)
+    saved[2].start()
+    saved[3].start()
     fetched[1].wait()
     x1 = (x + mm(mix_ref[...], wout_ref[...])).astype(BF16)
     lane = lax.broadcasted_iota(jnp.int32, (N, 128), 1)
@@ -250,19 +263,33 @@
         count = count + jnp.where(lane == neighbors_ref[place_ref[0], n], 1.0, 0.0)
     sent = jnp.concatenate([x1, rows_ref[:, C:], count.astype(BF16)], axis=1)
     sent_ref[...] = sent.reshape(N, 8, 128)
+    for copy in saved:
+        copy.wait()
 
 
 def time_backward(
-    core_ref, back_ref, rows_ref, qkv_ref, shares_ref, mix_ref, wqkv_ref, wout_ref,
-    sent_ref, keep_ref, give_ref, dqkv_ref, dcol_ref, pcol_ref,
+    core_ref, back_ref, *refs
 ):
+    sources, (sent_ref, keep_ref, give_ref, dqkv_ref, dcol_ref, pcol_ref) = refs[:6], refs[6:12]
+    held, sems = refs[12:18], refs[18]
+    fetched = [
+        pltpu.make_async_copy(source, target, sems.at[k])
+        for k, (source, target) in enumerate(zip(sources, held))
+    ]
+    for copy in fetched:
+        copy.start()
+    wout_ref, mix_ref, rows_ref, qkv_ref, shares_ref, wqkv_ref = held
     put = halves(core_ref[0], keep_ref, give_ref)
     back = back_ref[...].reshape(N, 1024)
     dx1 = back[:, 0:C]
+    for copy in fetched[0:3]:
+        copy.wait()
     normed, inverse = norm(rows_ref[...].astype(F32))
     dmix = mt(dx1, wout_ref[...]).astype(BF16)
     put("time_out", tm(mix_ref[...], dx1))
     masks = tile_masks()
+    for copy in fetched[3:6]:
+        copy.wait()
     for g in range(3):
         q = qkv_ref[:, g * 128 : (g + 1) * 128]
         k = qkv_ref[:, C + g * 128 : C + (g + 1) * 128]
@@ -522,8 +549,11 @@
     return pl.pallas_call(
         time_forward,
         in_specs=[SMEM, SMEM, VMEM, HBM, HBM],
+        out_specs=(VMEM, HBM, HBM, HBM, HBM),
         scratch_shapes=[
             pltpu.VMEM((C, 3 * C), BF16), pltpu.VMEM((C, C), BF16), pltpu.SemaphoreType.DMA((2,)),
+            pltpu.VMEM((N, 3 * C), BF16), pltpu.VMEM((N, H * N), BF16), pltpu.VMEM((N, C), BF16),
+            pltpu.VMEM((N, C), BF16), pltpu.SemaphoreType.DMA((4,)),
         ],
         out_shape=(
             like((N, 8, 128), BF16), pltpu.HBM((N, 3 * C), BF16), pltpu.HBM((N, H * N), BF16),
@@ -535,17 +565,20 @@
 
 
 def call_time_backward(core, back, rows, qkv, shares, mix, w_qkv, w_out):
+    sources = [w_out, mix, rows, qkv, shares, w_qkv]
     return pl.pallas_call(
         time_backward,
-        in_specs=[SMEM] + [VMEM] * 7,
+        in_specs=[SMEM, VMEM] + [HBM] * 6,
         out_shape=(like((N, 2 * C), BF16), like((LATE, 128), BF16), like((LATE, 128), BF16)),
         scratch_shapes=[
             pltpu.VMEM((N, 3 * C), BF16), pltpu.VMEM((4 * N, N), BF16), pltpu.VMEM((4 * N, N), BF16),
+            *[pltpu.VMEM(source.shape, BF16) for source in sources],
+            pltpu.SemaphoreType.DMA((len(sources),)),
         ],
         compiler_params=limit(20),
         cost_estimate=pl.CostEstimate(flops=1000, bytes_accessed=1000, transcendentals=0),
         name="time_backward",
-    )(core, back, *pinned(rows, qkv, shares, mix, w_qkv, w_out))
+    )(core, back, *pinned(*sources))
 
 
 def call_point_attention(core, weight, rows, w_qkv, w_pts, w_rep, w_out, w_up, w_down):

time: 159 us -> 159 us (level)
  no operation moved by 1% of the time
where the time goes in v7:
time: 159 us
  blocking collectives  49.2 us (31%)
  Pallas kernels  37 us (23%)
  starting transfers between devices  35.7 us (22%)
  waiting for transfers between devices  33.3 us (21%)
    all_to_all x2, blocking collectives, share(): lax.all_to_all(parts, EVERYONE, split_axis=0, concat_axis=0, tiled=True,...  49.2 us
    all_to_all x4, waiting for transfers between devices, swap_rows(): return lax.all_to_all(rows, axes, split_axis=0, concat_axis=0, tiled=True)  28.8 us
    all_to_all x4, starting transfers between devices, swap_rows(): return lax.all_to_all(rows, axes, split_axis=0, concat_axis=0, tiled=True)  23.3 us
    pallas_call x1, Pallas kernels, call_point_attention(): pl.pallas_call(point_attention, in_specs=[SMEM, SMEM, VMEM] + [HBM] * len...  11.9 us
    pallas_call x1, Pallas kernels, call_time_forward(): pl.pallas_call(time_forward, in_specs=[SMEM, SMEM, VMEM, HBM, HBM], out_s...  4.99 us
    ppermute x1, starting transfers between devices, body(): swapped = lax.ppermute(own, 'core', swap)  4.54 us
    ppermute x4, starting transfers between devices, both_ways(): lax.ppermute(part, EVERYONE, ring)  4.21 us
    pallas_call x1, Pallas kernels, call_unpack_first(): pl.pallas_call(unpack_first, in_specs=[SMEM, HBM, HBM], out_specs=(*[HBM]...  3.96 us
  transfers between devices with their start and end apart: 14, of which 6 were waited for; matrix products, arithmetic and copies ran while one was open for 1% of the time, Pallas kernels for 9%

profile of v7, /device:TPU:1, one launch (start us, length us, event | category | flops | bytes accessed | tf_op | source)
XLA Modules:
  0.0 158.5 jit_solution(7306140876518575045)
XLA Ops:
  0.6 0.0 copy-start.3
  0.7 2.0 %pack_rows.1 = bf16[16,8,896]{2,1,0:T(8,128)(2,1)} custom-call(bf16[8,16,384]{2,1,0:T(8,128)(2,1)} %tokens_ref.1, bf16[8,16,384]{2,1,0:T(8,128)(2,1)} %cotangent_ref.1, bf16[12,8,16]{2,1,0:T(8,128)(2,1)} %rigid_ref.1), custom_call_target="tpu_custom_call" | custom-call | tf_op jit(solution)/shard_map/pack_rows/pallas_call | solution.py:540
  2.6 9.5 %all-to-all-start = ((bf16[16,8,896]{2,1,0:T(8,128)(2,1)}), bf16[16,8,896]{2,1,0:T(8,128)(2,1)S(1)}, u32[]{:S(2)}, u32[]{:S(2)}) async-start(bf16[16,8,896]{2,1,0:T(8,128)(2,1)} %pack_rows.1), calls=%async_computation | async-start | bytes 458752 | tf_op jit(solution)/shard_map/all_to_all | solution.py:900
  12.1 0.0 copy-start.2
  12.1 8.4 %all-to-all-done = bf16[16,8,896]{2,1,0:T(8,128)(2,1)S(1)} async-done(((bf16[16,8,896]{2,1,0:T(8,128)(2,1)}), bf16[16,8,896]{2,1,0:T(8,128)(2,1)S(1)}, u32[]{:S(2)}, u32[]{:S(2)}) %all-to-all-start) | async-done | bytes 229408 | tf_op jit(solution)/shard_map/all_to_all | solution.py:900
  20.5 5.0 %time_forward.1 = (bf16[128,8,128]{2,1,0:T(8,128)(2,1)}, bf16[128,1152]{1,0:T(8,128)(2,1)}, bf16[128,1536]{1,0:T(8,128)(2,1)}, bf16[128,384]{1,0:T(8,128)(2,1)}, bf16[128,384]{1,0:T(8,128)(2,1)}) custom-call(s32[1]{0:T(128)} %bitcast.3.place_ref, s32[16,32]{1,0:T(8,128)} %neighbors_ref.1, bf16[128,896]{1,0:T(8,128)(2,1)S(1)} %bitcast.13, ...), custom_call_target="tpu_custom_call" | custom-call | tf_op jit(solution)/shard_map/time_forward/pallas_call | solution.py:549
  25.5 5.2 %all-to-all-start.1 = ((bf16[128,8,128]{2,1,0:T(8,128)(2,1)}), bf16[128,8,128]{2,1,0:T(8,128)(2,1)S(1)}, u32[]{:S(2)}, u32[]{:S(2)}) async-start(bf16[128,8,128]{2,1,0:T(8,128)(2,1)} %get-tuple-element.56), calls=%async_computation.1 | async-start | bytes 524288 | tf_op jit(solution)/shard_map/all_to_all | solution.py:900
  30.7 0.0 copy-done.3
  30.7 1.1 fusion.4
  31.8 9.9 %all-to-all-done.1.rows_ref = bf16[128,8,128]{2,1,0:T(8,128)(2,1)S(1)} async-done(((bf16[128,8,128]{2,1,0:T(8,128)(2,1)}), bf16[128,8,128]{2,1,0:T(8,128)(2,1)S(1)}, u32[]{:S(2)}, u32[]{:S(2)}) %all-to-all-start.1) | async-done | bytes 262176 | tf_op jit(solution)/shard_map/all_to_all | solution.py:900
  41.7 0.0 copy-done.2
  41.7 11.9 %point_attention.1 = (bf16[128,8,128]{2,1,0:T(8,128)(2,1)}, bf16[7680,128]{1,0:T(8,128)(2,1)}, bf16[7680,128]{1,0:T(8,128)(2,1)}) custom-call(s32[1]{0:T(128)} %bitcast.core_ref, f32[12]{0:T(128)S(1)} %copy-done.2, bf16[128,8,128]{2,1,0:T(8,128)(2,1)S(1)} %all-to-all-done.1.rows_ref, bf16[384,1152]{1,0:T(8,128)(2,1)} %refs_0_.2, ...), custom_call_target="tpu_custom_call" | custom-call | tf_op jit(solution)/shard_map/point_attention/pallas_call | solution.py:587
  53.6 0.6 collective-permute-start
  54.2 3.8 %all-to-all-start.2 = ((bf16[128,8,128]{2,1,0:T(8,128)(2,1)}), bf16[128,8,128]{2,1,0:T(8,128)(2,1)S(1)}, u32[]{:S(2)}, u32[]{:S(2)}) async-start(bf16[128,8,128]{2,1,0:T(8,128)(2,1)} %get-tuple-element.61), calls=%async_computation.2 | async-start | bytes 524288 | tf_op jit(solution)/shard_map/all_to_all | solution.py:900
  58.0 0.0 collective-permute-done.got_ref
  58.0 3.1 %add_early.1 = (bf16[3840,128]{1,0:T(8,128)(2,1)}, bf16[3840,128]{1,0:T(8,128)(2,1)}) custom-call(s32[1]{0:T(128)S(6)} %select_n.7.side_ref, bf16[7680,128]{1,0:T(8,128)(2,1)} %get-tuple-element.57.keep_ref, bf16[7680,128]{1,0:T(8,128)(2,1)S(1)} %collective-permute-done.got_ref), custom_call_target="tpu_custom_call" | custom-call | flops 983040 | bytes 5898240 | tf_op jit(solution)/shard_map/add_early/pallas_call | solution.py:642
  61.1 0.0 copy-start
  61.1 1.6 %collective-permute-start.1 = (bf16[3840,128]{1,0:T(8,128)(2,1)}, bf16[3840,128]{1,0:T(8,128)(2,1)S(1)}, u32[]{:S(2)}, u32[]{:S(2)}) collective-permute-start(bf16[3840,128]{1,0:T(8,128)(2,1)} %get-tuple-element.60), channel_id=1, source_target_pairs={{0,2},{1,3},{2,4},{3,5},{4,6},{5,7},{6,0},{7,1},{8,9},{9,24},{10,1... | collective-permute-start | bytes 2949128 | tf_op jit(solution)/shard_map/ppermute | solution.py:938
  62.7 6.3 %all-to-all-done.2.back_ref = bf16[128,8,128]{2,1,0:T(8,128)(2,1)S(1)} async-done(((bf16[128,8,128]{2,1,0:T(8,128)(2,1)}), bf16[128,8,128]{2,1,0:T(8,128)(2,1)S(1)}, u32[]{:S(2)}, u32[]{:S(2)}) %all-to-all-start.2) | async-done | bytes 262176 | tf_op jit(solution)/shard_map/all_to_all | solution.py:900
  69.0 3.9 %time_backward.1 = (bf16[128,768]{1,0:T(8,128)(2,1)S(1)}, bf16[2304,128]{1,0:T(8,128)(2,1)S(1)}, bf16[2304,128]{1,0:T(8,128)(2,1)S(1)}) custom-call(s32[1]{0:T(128)} %bitcast.core_ref, bf16[128,8,128]{2,1,0:T(8,128)(2,1)S(1)} %all-to-all-done.2.back_ref, bf16[384,384]{1,0:T(8,128)(2,1)} %refs_0_.3, bf16[128,384]{1,0:T(8,128)(2,1)} %get-tuple-element.62.refs_1_, ...), custom_call_target="tpu_custom_call" | custom-call | flops 1000 | bytes 1000 | tf_op jit(solution)/shard_map/time_backward/pallas_call | solution.py:569
  72.9 0.0 copy-start.1
  72.9 0.6 collective-permute-start.2
  73.5 1.6 %collective-permute-done.2.got_ref = bf16[2304,128]{1,0:T(8,128)(2,1)S(1)} collective-permute-done((bf16[2304,128]{1,0:T(8,128)(2,1)S(1)}, bf16[2304,128]{1,0:T(8,128)(2,1)S(1)}, u32[]{:S(2)}, u32[]{:S(2)}) %collective-permute-start.2) | collective-permute-done | bytes 589856 | tf_op jit(solution)/shard_map/ppermute | solution.py:943
  75.1 0.1 add_late.1
  75.3 0.4 collective-permute-start.3
  75.7 2.3 %collective-permute-start.4 = (bf16[576,128]{1,0:T(8,128)(2,1)S(1)}, bf16[576,128]{1,0:T(8,128)(2,1)S(1)}, u32[]{:S(2)}, u32[]{:S(2)}) collective-permute-start(bf16[576,128]{1,0:T(8,128)(2,1)S(1)} %get-tuple-element.70), channel_id=1, source_target_pairs={{0,6},{1,7},{2,0},{3,1},{4,2},{5,3},{6,4},{7,5},{8,25},{9,8},{10,2... | collective-permute-start | bytes 442376 | tf_op jit(solution)/shard_map/ppermute | solution.py:904
  78.0 2.8 %collective-permute-done.3.late_a_ref = bf16[576,128]{1,0:T(8,128)(2,1)S(1)} collective-permute-done((bf16[576,128]{1,0:T(8,128)(2,1)S(1)}, bf16[576,128]{1,0:T(8,128)(2,1)S(1)}, u32[]{:S(2)}, u32[]{:S(2)}) %collective-permute-start.3) | collective-permute-done | bytes 147488 | tf_op jit(solution)/shard_map/ppermute | solution.py:904
  80.9 0.0 collective-permute-done.4.late_b_ref
  80.9 0.0 collective-permute-done.1.got_early_ref
  80.9 0.0 copy-done
  80.9 0.3 add_pairs.1
  81.2 0.0 copy-done.1
  81.2 25.0 %all_to_all.30.parts_ref = bf16[32,160,128]{2,1,0:T(8,128)(2,1)S(1)} all-to-all(bf16[32,160,128]{2,1,0:T(8,128)(2,1)S(1)} %bitcast.12), channel_id=1, replica_groups={{0,1,4,5,16,17,20,21,32,33,36,37,48,49,52,53,64,65,68,69,80,81,84,85,96..., dimensions={0} | all-to-all | bytes 2621440 | tf_op jit(solution)/shard_map/all_to_all | solution.py:908
  106.2 0.2 add_parts.1
  106.4 24.3 %all_to_all.31.own_ref = bf16[32,160,128]{2,1,0:T(8,128)(2,1)S(1)} all-to-all(bf16[32,160,128]{2,1,0:T(8,128)(2,1)S(1)} %add_parts.1), channel_id=1, replica_groups={{0,1,4,5,16,17,20,21,32,33,36,37,48,49,52,53,64,65,68,69,80,81,84,85,96..., dimensions={0} | all-to-all | bytes 2621440 | tf_op jit(solution)/shard_map/all_to_all | solution.py:908
  130.6 4.5 %collective-permute-start.7 = (bf16[32,160,128]{2,1,0:T(8,128)(2,1)S(1)}, bf16[32,160,128]{2,1,0:T(8,128)(2,1)S(1)}, u32[]{:S(2)}, u32[]{:S(2)}) collective-permute-start(bf16[32,160,128]{2,1,0:T(8,128)(2,1)S(1)} %all_to_all.31.own_ref), channel_id=1, source_target_pairs={{0,8},{8,0},{1,9},{9,1},{2,10},{10,2},{3,11},{11,3},{4,12},{12,4},... | collective-permute-start | bytes 3932168 | tf_op jit(solution)/shard_map/ppermute | solution.py:950
  135.2 1.2 fusion.5
  136.3 1.0 collective-permute-start.6
  137.3 0.5 collective-permute-start.5
  137.8 4.9 %all-to-all-start.5 = ((bf16[16,8,768]{2,1,0:T(8,128)(2,1)}), bf16[16,8,768]{2,1,0:T(8,128)(2,1)S(1)}, u32[]{:S(2)}, u32[]{:S(2)}) async-start(bf16[16,8,768]{2,1,0:T(8,128)(2,1)} %bitcast.14), calls=%async_computation.5 | async-start | bytes 393216 | tf_op jit(solution)/shard_map/all_to_all | solution.py:900
  142.7 0.1 pad_add_fusion.spots_ref
  142.8 0.0 collective-permute-done.7.swapped_ref
  142.8 4.0 %unpack_first.1 = (f32[384,1536]{1,0:T(8,128)}, f32[384,384]{1,0:T(8,128)}, f32[288,384]{1,0:T(8,128)}, f32[384,1152]{1,0:T(8,128)}, f32[1536,384]{1,0:T(8,128)}...) custom-call(s32[4]{0:T(128)S(1)} %pad_add_fusion.spots_ref, ...), custom_call_target="tpu_custom_call" | custom-call | bytes 8388608 | tf_op jit(solution)/shard_map/unpack_first/pallas_call | solution.py:852
  146.8 4.1 %all-to-all-done.5.ended_ref = bf16[16,8,768]{2,1,0:T(8,128)(2,1)S(1)} async-done(((bf16[16,8,768]{2,1,0:T(8,128)(2,1)}), bf16[16,8,768]{2,1,0:T(8,128)(2,1)S(1)}, u32[]{:S(2)}, u32[]{:S(2)}) %all-to-all-start.5) | async-done | bytes 196640 | tf_op jit(solution)/shard_map/all_to_all | solution.py:900
  150.9 0.0 collective-permute-done.6.part_b_ref
  150.9 0.0 collective-permute-done.5.part_a_ref
  150.9 0.8 collective-permute-start.8
  151.7 0.1 collective-permute-start.9
  151.8 3.1 %unpack_second.1 = (f32[384,1536]{1,0:T(8,128)}, f32[384,384]{1,0:T(8,128)}, f32[288,384]{1,0:T(8,128)}, f32[384,1152]{1,0:T(8,128)}, f32[1536,384]{1,0:T(8,128)...) custom-call(s32[4]{0:T(128)S(1)} %pad_add_fusion.spots_ref, ...), custom_call_target="tpu_custom_call", output_to_operand_aliasing={{0}: (4, {}), {1}: (5, {}), {2}: (6, {}), {3}: (7, {}), {4}... | custom-call | bytes 8388608 | tf_op jit(solution)/shard_map/unpack_second/pallas_call | solution.py:865
  154.9 0.0 collective-permute-done.8.part_a_ref
  154.9 0.0 collective-permute-done.9.part_b_ref
  154.9 3.5 %unpack_last.1 = (f32[384,1536]{1,0:T(8,128)}, f32[384,384]{1,0:T(8,128)}, f32[288,384]{1,0:T(8,128)}, f32[384,1152]{1,0:T(8,128)}, f32[1536,384]{1,0:T(8,128)},...) custom-call(s32[4]{0:T(128)S(1)} %pad_add_fusion.spots_ref, ...), custom_call_target="tpu_custom_call", output_to_operand_aliasing={{0}: (5, {}), {1}: (6, {}), {2}: (7, {}), {3}: (8, {}), {4}... | custom-call | tf_op jit(solution)/shard_map/unpack_last/pallas_call | solution.py:881
Async XLA Ops:
  0.6 30.1 %copy-start.3 = (bf16[384,288]{0,1:T(8,128)(2,1)S(1)}, bf16[384,288]{0,1:T(8,128)(2,1)}, u32[]{:S(2)}) copy-start(bf16[384,288]{0,1:T(8,128)(2,1)} %param.22) | copy-start | bytes 663556
  2.6 17.9 %all-to-all-start = ((bf16[16,8,896]{2,1,0:T(8,128)(2,1)}), bf16[16,8,896]{2,1,0:T(8,128)(2,1)S(1)}, u32[]{:S(2)}, u32[]{:S(2)}) async-start(bf16[16,8,896]{2,1,0:T(8,128)(2,1)} %pack_rows.1), calls=%async_computation | async-start | bytes 458752 | tf_op jit(solution)/shard_map/all_to_all | solution.py:900
  12.1 29.7 %copy-start.2 = (f32[12]{0:T(128)S(1)}, f32[12]{0:T(128)}, u32[]{:S(2)}) copy-start(f32[12]{0:T(128)} %weight_ref.1) | copy-start | bytes 148
  25.5 16.2 %all-to-all-start.1 = ((bf16[128,8,128]{2,1,0:T(8,128)(2,1)}), bf16[128,8,128]{2,1,0:T(8,128)(2,1)S(1)}, u32[]{:S(2)}, u32[]{:S(2)}) async-start(bf16[128,8,128]{2,1,0:T(8,128)(2,1)} %get-tuple-element.56), calls=%async_computation.1 | async-start | bytes 524288 | tf_op jit(solution)/shard_map/all_to_all | solution.py:900
  53.6 4.4 %collective-permute-start = (bf16[7680,128]{1,0:T(8,128)(2,1)}, bf16[7680,128]{1,0:T(8,128)(2,1)S(1)}, u32[]{:S(2)}, u32[]{:S(2)}) collective-permute-start(bf16[7680,128]{1,0:T(8,128)(2,1)} %get-tuple-element.58), channel_id=1, source_target_pairs={{0,8},{8,0},{1,9},{9,1},{2,10},{10,2},{3,11},{11,3},{4,12},{12,4},... | collective-permute-start | bytes 5898248 | tf_op jit(solution)/shard_map/ppermute | solution.py:936
  54.2 14.8 %all-to-all-start.2 = ((bf16[128,8,128]{2,1,0:T(8,128)(2,1)}), bf16[128,8,128]{2,1,0:T(8,128)(2,1)S(1)}, u32[]{:S(2)}, u32[]{:S(2)}) async-start(bf16[128,8,128]{2,1,0:T(8,128)(2,1)} %get-tuple-element.61), calls=%async_computation.2 | async-start | bytes 524288 | tf_op jit(solution)/shard_map/all_to_all | solution.py:900
  61.1 19.8 %copy-start = (bf16[3840,128]{1,0:T(8,128)(2,1)S(1)}, bf16[3840,128]{1,0:T(8,128)(2,1)}, u32[]{:S(2)}) copy-start(bf16[3840,128]{1,0:T(8,128)(2,1)} %get-tuple-element.59.early_ref) | copy-start | bytes 2949124
  61.1 19.8 %collective-permute-start.1 = (bf16[3840,128]{1,0:T(8,128)(2,1)}, bf16[3840,128]{1,0:T(8,128)(2,1)S(1)}, u32[]{:S(2)}, u32[]{:S(2)}) collective-permute-start(bf16[3840,128]{1,0:T(8,128)(2,1)} %get-tuple-element.60), channel_id=1, source_target_pairs={{0,2},{1,3},{2,4},{3,5},{4,6},{5,7},{6,0},{7,1},{8,9},{9,24},{10,1... | collective-permute-start | bytes 2949128 | tf_op jit(solution)/shard_map/ppermute | solution.py:938
  72.9 8.2 %copy-start.1 = (bf16[128,768]{1,0:T(8,128)(2,1)}, bf16[128,768]{1,0:T(8,128)(2,1)S(1)}, u32[]{:S(2)}) copy-start(bf16[128,768]{1,0:T(8,128)(2,1)S(1)} %get-tuple-element.71) | copy-start | bytes 589828
  72.9 2.2 %collective-permute-start.2 = (bf16[2304,128]{1,0:T(8,128)(2,1)S(1)}, bf16[2304,128]{1,0:T(8,128)(2,1)S(1)}, u32[]{:S(2)}, u32[]{:S(2)}) collective-permute-start(bf16[2304,128]{1,0:T(8,128)(2,1)S(1)} %get-tuple-element.67), channel_id=1, source_target_pairs={{0,8},{8,0},{1,9},{9,1},{2,10},{10,2},{3,11},{11,3},{4,12},{12,4},... | collective-permute-start | bytes 1769480 | tf_op jit(solution)/shard_map/ppermute | solution.py:943
  75.3 5.6 %collective-permute-start.3 = (bf16[576,128]{1,0:T(8,128)(2,1)S(1)}, bf16[576,128]{1,0:T(8,128)(2,1)S(1)}, u32[]{:S(2)}, u32[]{:S(2)}) collective-permute-start(bf16[576,128]{1,0:T(8,128)(2,1)S(1)} %get-tuple-element.69), channel_id=1, source_target_pairs={{0,2},{1,3},{2,4},{3,5},{4,6},{5,7},{6,0},{7,1},{8,9},{9,24},{10,1... | collective-permute-start | bytes 442376 | tf_op jit(solution)/shard_map/ppermute | solution.py:904
  75.7 5.1 %collective-permute-start.4 = (bf16[576,128]{1,0:T(8,128)(2,1)S(1)}, bf16[576,128]{1,0:T(8,128)(2,1)S(1)}, u32[]{:S(2)}, u32[]{:S(2)}) collective-permute-start(bf16[576,128]{1,0:T(8,128)(2,1)S(1)} %get-tuple-element.70), channel_id=1, source_target_pairs={{0,6},{1,7},{2,0},{3,1},{4,2},{5,3},{6,4},{7,5},{8,25},{9,8},{10,2... | collective-permute-start | bytes 442376 | tf_op jit(solution)/shard_map/ppermute | solution.py:904
  130.6 12.2 %collective-permute-start.7 = (bf16[32,160,128]{2,1,0:T(8,128)(2,1)S(1)}, bf16[32,160,128]{2,1,0:T(8,128)(2,1)S(1)}, u32[]{:S(2)}, u32[]{:S(2)}) collective-permute-start(bf16[32,160,128]{2,1,0:T(8,128)(2,1)S(1)} %all_to_all.31.own_ref), channel_id=1, source_target_pairs={{0,8},{8,0},{1,9},{9,1},{2,10},{10,2},{3,11},{11,3},{4,12},{12,4},... | collective-permute-start | bytes 3932168 | tf_op jit(solution)/shard_map/ppermute | solution.py:950
  136.3 14.6 %collective-permute-start.6 = (bf16[16,160,128]{2,1,0:T(8,128)(2,1)}, bf16[16,160,128]{2,1,0:T(8,128)(2,1)S(1)}, u32[]{:S(2)}, u32[]{:S(2)}) collective-permute-start(bf16[16,160,128]{2,1,0:T(8,128)(2,1)} %get-tuple-element.102), channel_id=1, source_target_pairs={{0,6},{1,7},{2,0},{3,1},{4,2},{5,3},{6,4},{7,5},{8,25},{9,8},{10,2... | collective-permute-start | bytes 1966088 | tf_op jit(solution)/shard_map/ppermute | solution.py:904
  137.3 13.6 %collective-permute-start.5 = (bf16[16,160,128]{2,1,0:T(8,128)(2,1)}, bf16[16,160,128]{2,1,0:T(8,128)(2,1)}, u32[]{:S(2)}, u32[]{:S(2)}) collective-permute-start(bf16[16,160,128]{2,1,0:T(8,128)(2,1)} %get-tuple-element.103), channel_id=1, source_target_pairs={{0,2},{1,3},{2,4},{3,5},{4,6},{5,7},{6,0},{7,1},{8,9},{9,24},{10,1... | collective-permute-start | bytes 1966088 | tf_op jit(solution)/shard_map/ppermute | solution.py:904
  137.8 13.1 %all-to-all-start.5 = ((bf16[16,8,768]{2,1,0:T(8,128)(2,1)}), bf16[16,8,768]{2,1,0:T(8,128)(2,1)S(1)}, u32[]{:S(2)}, u32[]{:S(2)}) async-start(bf16[16,8,768]{2,1,0:T(8,128)(2,1)} %bitcast.14), calls=%async_computation.5 | async-start | bytes 393216 | tf_op jit(solution)/shard_map/all_to_all | solution.py:900
  150.9 4.0 %collective-permute-start.8 = (bf16[16,160,128]{2,1,0:T(8,128)(2,1)}, bf16[16,160,128]{2,1,0:T(8,128)(2,1)S(1)}, u32[]{:S(2)}, u32[]{:S(2)}) collective-permute-start(bf16[16,160,128]{2,1,0:T(8,128)(2,1)} %collective-permute-done.5.part_a_ref), channel_id=1, source_target_pairs={{0,8},{8,0},{1,9},{9,1},{2,10},{10,2},{3,11},{11,3},{4,12},{12,4},... | collective-permute-start | bytes 1966088 | tf_op jit(solution)/shard_map/ppermute | solution.py:954
  151.7 3.2 %collective-permute-start.9 = (bf16[16,160,128]{2,1,0:T(8,128)(2,1)S(1)}, bf16[16,160,128]{2,1,0:T(8,128)(2,1)S(1)}, u32[]{:S(2)}, u32[]{:S(2)}) collective-permute-start(bf16[16,160,128]{2,1,0:T(8,128)(2,1)S(1)} %collective-permute-done.6.part_b_ref), channel_id=1, source_target_pairs={{0,8},{8,0},{1,9},{9,1},{2,10},{10,2},{3,11},{11,3},{4,12},{12,4},... | collective-permute-start | bytes 1966088 | tf_op jit(solution)/shard_map/ppermute | solution.py:954
